TPU v7x, 256 devices: a whole 4x4x8 slice. The times are simulated.
256 devices in a mesh: lat: 32 (over x_lo, z, core), lon: 8 (over y, x_hi).
Axes of the slice: x: 4 (x_hi: 2, x_lo: 2; x = x_hi * 2 + x_lo), y: 4, z: 8, core: 2. Of those that a mesh axis runs over, the one named last changes fastest.
Arguments:
- tokens: bfloat16 [4, 192, 96, 512], P(None, 'lat', 'lon'), may hold values from -6 to 6
- cotangent: bfloat16 [4, 192, 96, 512], P(None, 'lat', 'lon'), may hold values from -6 to 6
- region: int32 [4, 192, 96], P(None, 'lat', 'lon'), may hold values from 0 to 7, as said below
- gain: float32 [512], replicated, may hold values from 0.5 to 1.5
- qkv_weight: bfloat16 [512, 1536], replicated, may hold values from -12 to 12
- proj_weight: bfloat16 [512, 512], replicated, may hold values from -0.25 to 0.25
Outputs:
- mixed: bfloat16 [4, 192, 96, 512], P(None, 'lat', 'lon')
- grad_tokens: bfloat16 [4, 192, 96, 512], P(None, 'lat', 'lon')
- grad_qkv: float32 [512, 1536], replicated
- grad_proj: float32 [512, 512], replicated
- grad_gain: float32 [512], replicated
Inputs may be any that keep to these rules, and one draw needn't show every extreme that they name: region is constant on aligned blocks of one level, 3 rows and 6 columns; the last level and the last 3 rows of the shifted grid carry ids of their own.
All inputs are finite; a program needn't handle non-finite values.
Results may differ from a plain program's by a relative error of at most 0.013.
Values may be sent and summed in bfloat16 or wider, within the bound.
No kernel may reach another device: no remote copies, remote signals or barrier semaphores. Data moves between devices by JAX's collectives and lax.ppermute only.
A program may use at most 64 MiB of HBM per device.

v0:
```python
import jax
import jax.numpy as jnp
from jax import lax
from jax.experimental import pallas as pl
from jax.experimental.pallas import tpu as pltpu
from jax.sharding import Mesh, PartitionSpec as P

D = 512
HALF_D = D // 2
HEADS = 8
HEAD = 64
PAIRS = HEADS // 2
WINDOWS = 2
COUNT = 144
TOKENS = WINDOWS * COUNT
HALF_R = 3
HALF_C = 6
EPS = 1e-05
TOGETHER = 4
SIZES = {"xl": 2, "zh": 4, "zl": 2, "c": 2, "y": 4, "xh": 2}
AXES = tuple(SIZES)
LAT = AXES[:4]
LON = AXES[4:]
NEAR = ("xh", "xl", "y", "zl")
N_NEAR = 32
FAR = "zh"
N_FAR = 4
CHUNK = 2 * D // N_NEAR
PIECE = (2, HALF_R, HALF_C, 4, D)
F32 = jnp.float32
BF16 = jnp.bfloat16


def dot(left, right):
    return jnp.dot(left, right, preferred_element_type=F32)


def dot_first(left, right):
    return lax.dot_general(left, right, (((0,), (0,)), ((), ())), preferred_element_type=F32)


def dot_last(left, right):
    return lax.dot_general(left, right, (((1,), (1,)), ((), ())), preferred_element_type=F32)


def pack_kernel(tok_ref, cot_ref, own_ref, right_ref, below_ref, corner_ref, sems):
    copies = []
    for n, ref in enumerate((tok_ref, cot_ref)):
        for rows, cols, piece in quadrants(own_ref, right_ref, below_ref, corner_ref):
            sem = sems.at[len(copies)]
            copies.append(pltpu.make_async_copy(ref.at[rows, cols], piece.at[n], sem))
    for copy in copies:
        copy.start()
    for copy in copies:
        copy.wait()


def quadrants(own, right, below, corner):
    late_r, early_r = pl.ds(HALF_R, HALF_R), pl.ds(0, HALF_R)
    late_c, early_c = pl.ds(HALF_C, HALF_C), pl.ds(0, HALF_C)
    return (
        (late_r, late_c, own),
        (late_r, early_c, right),
        (early_r, late_c, below),
        (early_r, early_c, corner),
    )


def source_of(place):
    window = place // COUNT
    rest = place - window * COUNT
    level = (1 + 2 * window + rest % 2) % 4
    return (rest // 2) * 4 + level


def attend_kernel(
    corner_ref, right_ref, below_ref, own_ref, bias_ref, gain_ref, qkv_ref, proj_ref,
    send_ref, left_ref, rows_ref, att_ref, normed_ref, inv_ref,
):
    first = lax.broadcasted_iota(jnp.int32, (TOKENS, 1), 0)
    second = lax.broadcasted_iota(jnp.int32, (TOKENS, TOKENS), 1)
    to_order = (second == source_of(first)).astype(BF16)
    pieces = (own_ref, right_ref, below_ref, corner_ref)

    def gathered(n):
        return jnp.concatenate([ref[n] for ref in pieces], axis=0).reshape(TOKENS, D)

    values = dot(to_order, gathered(0))
    cot = dot(to_order, gathered(1)).astype(BF16)
    gain = gain_ref[...]
    mean = jnp.mean(values, -1, keepdims=True)
    centred = values - mean
    inv_std = lax.rsqrt(jnp.mean(centred * centred, -1, keepdims=True) + EPS)
    normed = centred * inv_std
    hidden = (normed * gain).astype(BF16)
    projected = dot(hidden, qkv_ref[...]).astype(BF16)
    grad_att = dot_last(cot, proj_ref[...]).astype(BF16)
    normed_ref[...] = normed
    inv_ref[...] = inv_std
    left_ref[0] = hidden.T
    rows_ref[3] = cot

    lane = lax.broadcasted_iota(jnp.int32, (COUNT, 2 * HEAD), 1)
    low = lane < HEAD
    zero = jnp.zeros((COUNT, 2 * HEAD), BF16)

    def both(pair):
        return jnp.concatenate([jnp.where(low, pair, zero), jnp.where(low, zero, pair)], axis=0)

    def merged(stacked):
        return jnp.where(low, stacked[:COUNT], stacked[COUNT:])

    factor = HEAD ** (-0.5)
    biases = [jnp.concatenate([bias_ref[w]] * 2, axis=1) for w in range(WINDOWS)]
    spots = [(w, p) for w in range(WINDOWS) for p in range(PAIRS)]
    for at in range(0, len(spots), TOGETHER):
        here, cols, bias = [], [], []
        for window, pair in spots[at : at + TOGETHER]:
            here.append(slice(window * COUNT, (window + 1) * COUNT))
            cols.append(slice(pair * 2 * HEAD, (pair + 1) * 2 * HEAD))
            bias.append(biases[window])
        each = range(len(here))
        query = [both(projected[here[i], cols[i]] * jnp.asarray(factor, BF16)) for i in each]
        keys = [projected[here[i], D + cols[i].start : D + cols[i].stop] for i in each]
        vals = [projected[here[i], 2 * D + cols[i].start : 2 * D + cols[i].stop] for i in each]
        grad_out = [both(grad_att[here[i], cols[i]]) for i in each]
        scores = [dot_last(keys[i], query[i]) + bias[i] for i in each]
        grad_weights = [dot_last(vals[i], grad_out[i]) for i in each]
        numer = [jnp.exp(s - jnp.max(s, 0, keepdims=True)) for s in scores]
        weights = [n * (1.0 / jnp.sum(n, 0, keepdims=True)) for n in numer]
        weights_low = [w.astype(BF16) for w in weights]
        inner = [jnp.sum(g * w, 0, keepdims=True) for g, w in zip(grad_weights, weights)]
        grad_scores = [
            (w * (g - i)).astype(BF16) for w, g, i in zip(weights, grad_weights, inner)
        ]
        for i in each:
            att_ref[here[i], cols[i]] = merged(dot_first(weights_low[i], vals[i])).astype(BF16)
            rows_ref[2, here[i], cols[i]] = dot(weights_low[i], grad_out[i]).astype(BF16)
        for i in each:
            grad_query = merged(dot_first(grad_scores[i], keys[i])) * factor
            rows_ref[0, here[i], cols[i]] = grad_query.astype(BF16)
            rows_ref[1, here[i], cols[i]] = dot(grad_scores[i], query[i]).astype(BF16)

    left_ref[1] = att_ref[...].T
    half_grads(1 - lax.axis_index("c"), left_ref, rows_ref, send_ref)


def half_grads(half, left_ref, rows_ref, out_ref):
    here = pl.ds(pl.multiple_of(half * HALF_D, HALF_D), HALF_D)
    for block in range(4):
        out_ref[block] = dot(left_ref[block // 3, here], rows_ref[block]).astype(BF16)


def rest_kernel(
    left_ref, rows_ref, att_ref, normed_ref, inv_ref, gain_ref, qkv_ref, proj_ref,
    keep_ref, own_out, right_out, lower_out,
):
    half_grads(lax.axis_index("c"), left_ref, rows_ref, keep_ref)
    first = lax.broadcasted_iota(jnp.int32, (TOKENS, TOKENS), 0)
    second = lax.broadcasted_iota(jnp.int32, (1, TOKENS), 1)
    from_order = (first == source_of(second)).astype(BF16)
    normed = normed_ref[...]
    inv_std = inv_ref[...]
    attended = att_ref[...]
    gain = gain_ref[...]
    branch = dot(attended, proj_ref[...]).astype(BF16)
    grad_hidden = dot_last(rows_ref[0], qkv_ref[:, :D])
    grad_hidden += dot_last(rows_ref[1], qkv_ref[:, D : 2 * D])
    grad_hidden += dot_last(rows_ref[2], qkv_ref[:, 2 * D :])
    grad_norm = grad_hidden * gain
    grad_shift = inv_std * (
        grad_norm
        - jnp.mean(grad_norm, -1, keepdims=True)
        - normed * jnp.mean(grad_norm * normed, -1, keepdims=True)
    )
    for n, result in enumerate((branch, grad_shift.astype(BF16))):
        back = dot(from_order, result).reshape(4, HALF_R, HALF_C, 4, D).astype(BF16)
        own_out[n] = back[0]
        right_out[n] = back[1]
        lower_out[0, n] = back[2]
        lower_out[1, n] = back[3]


def weights_kernel(qkv_ref, proj_ref, gain_ref, qkv_out, proj_out, gain_out, sems):
    copies = [
        pltpu.make_async_copy(ref, out, sems.at[n])
        for n, (ref, out) in enumerate(
            ((qkv_ref, qkv_out), (proj_ref, proj_out), (gain_ref, gain_out))
        )
    ]
    for copy in copies:
        copy.start()
    for copy in copies:
        copy.wait()


def add_kernel(keep_ref, got_ref, out_ref):
    out_ref[...] = (keep_ref[...].astype(F32) + got_ref[...].astype(F32)).astype(BF16)


def sum_kernel(got_ref, lower_ref, right_ref, out_ref, side_ref):
    side_ref[0] = right_ref[...]
    side_ref[1] = lower_ref[1]
    total = got_ref[0].astype(F32)
    for n in range(1, got_ref.shape[0]):
        total += got_ref[n].astype(F32)
    out_ref[...] = total.astype(BF16)


def spread_kernel(own_ref, one_ref, two_ref, three_ref, side_ref, out_ref):
    del side_ref
    even = own_ref[...].astype(F32) + two_ref[...].astype(F32)
    odd = one_ref[...].astype(F32) + three_ref[...].astype(F32)
    total = (even + odd).astype(BF16)
    for n in range(out_ref.shape[0]):
        out_ref[n] = total


def finish_kernel(tok_ref, cot_ref, own_ref, lower_ref, side_ref, mixed_ref, grad_ref):
    right_ref, below_ref, corner_ref = side_ref.at[0], lower_ref.at[0], side_ref.at[1]
    for n, (ref, out) in enumerate(((tok_ref, mixed_ref), (cot_ref, grad_ref))):
        for rows, cols, piece in quadrants(own_ref, right_ref, below_ref, corner_ref):
            out[rows, cols] = (ref[rows, cols].astype(F32) + piece[n].astype(F32)).astype(BF16)


def grads_half(half, ref, qkv_ref, gain_ref, qkv_out, proj_out, gain_out, wide, sems):
    copies = []
    here = pl.ds(pl.multiple_of(half * HALF_D, HALF_D), HALF_D)
    total = jnp.zeros((HALF_D, 128), F32)
    for block in range(4):
        part = ref[block].astype(F32)
        wide[block] = part
        cols = pl.ds(block * D, D)
        out = proj_out.at[here] if block == 3 else qkv_out.at[here, cols]
        copy = pltpu.make_async_copy(wide.at[block], out, sems.at[block])
        copy.start()
        copies.append(copy)
        if block < 3:
            product = part * qkv_ref[here, cols].astype(F32)
            for q in range(4):
                total += product[:, q * 128 : (q + 1) * 128]
    sums = jnp.sum(total.T, axis=0, keepdims=True)
    gain_out[:, here] = sums / gain_ref[:, here]
    for copy in copies:
        copy.wait()


def mine_kernel(ref, qkv_ref, gain_ref, qkv_out, proj_out, gain_out, wide, sems):
    gain_out[...] = jnp.zeros_like(gain_out)
    core = lax.axis_index("c")
    grads_half(core, ref, qkv_ref, gain_ref, qkv_out, proj_out, gain_out, wide, sems)


def other_kernel(
    ref, qkv_ref, gain_ref, qkv_in, proj_in, gain_in, qkv_out, proj_out, gain_out, wide, sems
):
    del qkv_in, proj_in
    gain_out[...] = gain_in[...]
    core = lax.axis_index("c")
    grads_half(1 - core, ref, qkv_ref, gain_ref, qkv_out, proj_out, gain_out, wide, sems)


def call(kernel, outs, scratch=(), ins=None, out_specs=None, mib=8, aliases=None):
    more = {"input_output_aliases": aliases or {}}
    if ins is not None:
        more["in_specs"] = ins
    if out_specs is not None:
        more["out_specs"] = out_specs
    return pl.pallas_call(
        kernel,
        out_shape=outs,
        scratch_shapes=list(scratch),
        compiler_params=pltpu.CompilerParams(vmem_limit_bytes=mib * 1024 * 1024),
        **more,
    )


def in_hbm(array):
    return pltpu.with_memory_space_constraint(array, pltpu.HBM)


def shaped(shape, dtype):
    return jax.ShapeDtypeStruct(shape, dtype)


def moved(block, lat_step, lon_step):
    route = [
        (lat * 8 + lon, (lat + lat_step) % 32 * 8 + (lon + lon_step) % 8)
        for lat in range(32)
        for lon in range(8)
    ]
    return lax.ppermute(block, AXES, route)


def swapped(block):
    return lax.ppermute(block, "c", [(0, 1), (1, 0)])


def on_device(tokens, cotangent, region, gain, qkv_weight, proj_weight):
    tok = tokens.transpose(1, 2, 0, 3)
    cot = cotangent.transpose(1, 2, 0, 3)
    anywhere = pl.BlockSpec(memory_space=pl.ANY)
    vmem = pl.BlockSpec(memory_space=pltpu.VMEM)
    hbm = pl.BlockSpec(memory_space=pltpu.HBM)
    own, right, below, corner = call(
        pack_kernel,
        [shaped(PIECE, BF16)] * 4,
        [pltpu.SemaphoreType.DMA((8,))],
        [hbm] * 2,
        [vmem] * 4,
        mib=2,
    )(in_hbm(tok), in_hbm(cot))
    corner = moved(corner, -1, -1)
    right = moved(right, 0, -1)
    below = moved(below, -1, 0)
    ids = region.reshape(2, 2, 2, HALF_R, 2, HALF_C).transpose(0, 2, 4, 3, 5, 1).reshape(2, COUNT)
    bias = jnp.where(ids[:, :, None] == ids[:, None, :], 0.0, -1e30).astype(F32)
    gain = gain.reshape(1, D)
    qkv_weight, proj_weight, gain = call(
        weights_kernel,
        [shaped((D, 3 * D), BF16), shaped((D, D), BF16), shaped((1, D), F32)],
        [pltpu.SemaphoreType.DMA((3,))],
        [hbm] * 3,
        [vmem] * 3,
        mib=1,
    )(in_hbm(qkv_weight), in_hbm(proj_weight), in_hbm(gain))
    send, *state = call(
        attend_kernel,
        [
            shaped((4, HALF_D, D), BF16),
            shaped((2, D, TOKENS), BF16),
            shaped((4, TOKENS, D), BF16),
            shaped((TOKENS, D), BF16),
            shaped((TOKENS, D), F32),
            shaped((TOKENS, 1), F32),
        ],
        mib=16,
    )(corner, right, below, own, bias, gain, qkv_weight, proj_weight)
    got = swapped(send)
    pair = shaped((2,) + PIECE, BF16)
    keep, own_back, right_back, lower_back = call(
        rest_kernel,
        [shaped((4, HALF_D, D), BF16), shaped(PIECE, BF16), shaped(PIECE, BF16), pair],
        mib=16,
    )(*state, gain, qkv_weight, proj_weight)
    half = call(add_kernel, shaped((4, HALF_D, D), BF16), mib=4)(keep, got)
    got = lax.all_to_all(half.reshape(N_NEAR, CHUNK, D), NEAR, 0, 0)
    lower_back = moved(lower_back, 1, 0)
    part, side_back = call(
        sum_kernel, [shaped((CHUNK, D), BF16), pair], ins=[vmem] * 3, out_specs=[vmem] * 2, mib=6
    )(got, lower_back, right_back)
    others = [
        lax.ppermute(part, FAR, [(n, (n - step) % N_FAR) for n in range(N_FAR)])
        for step in range(1, N_FAR)
    ]
    side_back = moved(side_back, 0, 1)
    parts = call(
        spread_kernel,
        shaped((N_NEAR, CHUNK, D), BF16),
        ins=[vmem] * 4 + [anywhere],
        out_specs=vmem,
        mib=4,
    )(part, *others, side_back)
    mine = lax.all_to_all(parts, NEAR, 0, 0)
    mine = mine.reshape(4, HALF_D, D)
    other = swapped(mine)
    grads = call(
        mine_kernel,
        [shaped((D, 3 * D), F32), shaped((D, D), F32), shaped((1, D), F32)],
        [pltpu.VMEM((4, HALF_D, D), F32), pltpu.SemaphoreType.DMA((4,))],
        [vmem] * 3,
        [anywhere, anywhere, vmem],
        mib=6,
    )(mine, qkv_weight, gain)
    grad_qkv, grad_proj, grad_gain = call(
        other_kernel,
        [shaped((D, 3 * D), F32), shaped((D, D), F32), shaped((1, D), F32)],
        [pltpu.VMEM((4, HALF_D, D), F32), pltpu.SemaphoreType.DMA((4,))],
        [vmem] * 3 + [anywhere] * 2 + [vmem],
        [anywhere, anywhere, vmem],
        mib=6,
        aliases={3: 0, 4: 1},
    )(other, qkv_weight, gain, *grads)
    mixed, grad_tokens = call(finish_kernel, [shaped((6, 12, 4, D), BF16)] * 2, mib=6)(
        tok, cot, own_back, lower_back, side_back
    )
    return (
        mixed.transpose(2, 0, 1, 3),
        grad_tokens.transpose(2, 0, 1, 3),
        grad_qkv,
        grad_proj,
        grad_gain.reshape(D),
    )


def solution(mesh):
    fine = Mesh(mesh.devices.reshape(tuple(SIZES.values())), AXES)
    grid = P(None, LAT, LON, None)
    return jax.shard_map(
        on_device,
        mesh=fine,
        in_specs=(grid, grid, P(None, LAT, LON), P(), P(), P()),
        out_specs=(grid, grid, P(), P(), P()),
        check_vma=False,
    )
```

profile of v0, /device:TPU:1, one launch (start us, length us, event | category | flops | bytes accessed | tf_op | source)
XLA Modules:
  0.0 93.3 jit_solution(17175238987673032891)
XLA Ops:
  0.6 1.2 %shard_map.101 = (bf16[2,3,6,4,512]{4,3,2,1,0:T(4,128)(2,1)S(1)}, bf16[2,3,6,4,512]{4,3,2,1,0:T(4,128)(2,1)S(1)}, bf16[2,3,6,4,512]{4,3,2,1,0:T(4,128)(2,1)S(1)}, bf16[2,3,6,4,512]{4,3,2,1,0:T(4,128)(2,1)S(1)}) custom-call(bf16[6,12,4,512]{3,2,1,0:T(4,128)(2,1)} %bitcast.13, bf16[6,12,4,512]{3,2,1,0:T(4,128)(2,1)} %bitcast.15), custom_call_target="tpu_custom_call" | custom-call | tf_op jit(solution)/shard_map/pallas_call | solution.py:305
  1.8 6.7 %collective-permute-start = (bf16[2,3,6,4,512]{4,3,2,1,0:T(4,128)(2,1)S(1)}, bf16[2,3,6,4,512]{4,3,2,1,0:T(4,128)(2,1)S(1)}, u32[]{:S(2)}, u32[]{:S(2)}) collective-permute-start(bf16[2,3,6,4,512]{4,3,2,1,0:T(4,128)(2,1)S(1)} %get-tuple-element.32), channel_id=1, source_target_pairs={{0,255},{1,248},{2,249},{3,250},{4,251},{5,252},{6,253},{7,254},{8... | collective-permute-start | bytes 442376 | tf_op jit(solution)/shard_map/ppermute | solution.py:292
  8.5 0.2 collective-permute-start.1
  8.7 5.4 %collective-permute-start.2 = (bf16[2,3,6,4,512]{4,3,2,1,0:T(4,128)(2,1)S(1)}, bf16[2,3,6,4,512]{4,3,2,1,0:T(4,128)(2,1)S(1)}, u32[]{:S(2)}, u32[]{:S(2)}) collective-permute-start(bf16[2,3,6,4,512]{4,3,2,1,0:T(4,128)(2,1)S(1)} %get-tuple-element.34), channel_id=1, source_target_pairs={{0,248},{1,249},{2,250},{3,251},{4,252},{5,253},{6,254},{7,255},{8... | collective-permute-start | bytes 442376 | tf_op jit(solution)/shard_map/ppermute | solution.py:292
  14.2 0.8 reshape.27
  15.0 0.3 copy.14
  15.2 0.1 eq.15
  15.4 1.5 %shard_map.102 = (bf16[512,1536]{1,0:T(8,128)(2,1)S(1)}, bf16[512,512]{1,0:T(8,128)(2,1)S(1)}, f32[1,512]{1,0:T(1,128)S(1)}) custom-call(bf16[512,1536]{1,0:T(8,128)(2,1)} %qkv_ref.1, bf16[512,512]{1,0:T(8,128)(2,1)} %proj_ref.1, f32[1,512]{1,0:T(1,128)} %bitcast.18), custom_call_target="tpu_custom_call" | custom-call | tf_op jit(solution)/shard_map/pallas_call | solution.py:319
  16.9 0.1 compare_select_fusion.bias_ref
  17.0 0.0 collective-permute-done.corner_ref
  17.0 0.0 collective-permute-done.1.right_ref
  17.1 0.0 collective-permute-done.2.below_ref
  17.1 4.3 %shard_map.103 = (bf16[4,256,512]{2,1,0:T(8,128)(2,1)S(1)}, bf16[2,512,288]{2,1,0:T(8,128)(2,1)S(1)}, bf16[4,288,512]{2,1,0:T(8,128)(2,1)S(1)}, bf16[288,512]{1,...) custom-call(bf16[2,3,6,4,512]{4,3,2,1,0:T(4,128)(2,1)S(1)} %collective-permute-done.corner_ref, ...), custom_call_target="tpu_custom_call" | custom-call | tf_op jit(solution)/shard_map/pallas_call | solution.py:327
  21.4 3.0 %collective-permute-start.4 = (bf16[4,256,512]{2,1,0:T(8,128)(2,1)S(1)}, bf16[4,256,512]{2,1,0:T(8,128)(2,1)S(1)}, u32[]{:S(2)}, u32[]{:S(2)}) collective-permute-start(bf16[4,256,512]{2,1,0:T(8,128)(2,1)S(1)} %get-tuple-element.47), channel_id=1, source_target_pairs={{0,8},{8,0},{1,9},{9,1},{2,10},{10,2},{3,11},{11,3},{4,12},{12,4},... | collective-permute-start | bytes 3145736 | tf_op jit(solution)/shard_map/ppermute | solution.py:296
  24.4 1.8 %shard_map.104 = (bf16[4,256,512]{2,1,0:T(8,128)(2,1)S(1)}, bf16[2,3,6,4,512]{4,3,2,1,0:T(4,128)(2,1)S(1)}, bf16[2,3,6,4,512]{4,3,2,1,0:T(4,128)(2,1)S(1)}, bf16[2,2,3,6,4,512]{5,4,3,2,1,0:T(4,128)(2,1)S(1)}) custom-call(bf16[2,512,288]{2,1,0:T(8,128)(2,1)S(1)} %get-tuple-element.39.left_ref, bf16[4,288,512]{2,1,0:T(8,128)(2,1)S(1)} %get-tuple-element.40.rows_ref, ...), custom_call_target="tpu_custom_call" | custom-call | tf_op jit(solution)/shard_map/pallas_call | solution.py:341
  26.2 0.5 collective-permute-done.4.got_ref
  26.7 1.2 %shard_map.105 = bf16[4,256,512]{2,1,0:T(8,128)(2,1)} custom-call(bf16[4,256,512]{2,1,0:T(8,128)(2,1)S(1)} %get-tuple-element.46.keep_ref, bf16[4,256,512]{2,1,0:T(8,128)(2,1)S(1)} %collective-permute-done.4.got_ref), custom_call_target="tpu_custom_call" | custom-call | tf_op jit(solution)/shard_map/pallas_call | solution.py:346
  27.9 4.3 %all-to-all-start = ((bf16[32,32,512]{2,1,0:T(8,128)(2,1)}), bf16[32,32,512]{2,1,0:T(8,128)(2,1)S(1)}, u32[]{:S(2)}, u32[]{:S(2)}) async-start(bf16[32,32,512]{2,1,0:T(8,128)(2,1)} %bitcast.4), calls=%async_computation | async-start | bytes 2097152 | tf_op jit(solution)/shard_map/all_to_all | solution.py:347
  32.3 2.1 %collective-permute-start.3 = (bf16[2,2,3,6,4,512]{5,4,3,2,1,0:T(4,128)(2,1)S(1)}, bf16[2,2,3,6,4,512]{5,4,3,2,1,0:T(4,128)(2,1)S(1)}, u32[]{:S(2)}, u32[]{:S(2)}) collective-permute-start(bf16[2,2,3,6,4,512]{5,4,3,2,1,0:T(4,128)(2,1)S(1)} %get-tuple-element.45), channel_id=1, source_target_pairs={{0,8},{1,9},{2,10},{3,11},{4,12},{5,13},{6,14},{7,15},{8,16},{9,17... | collective-permute-start | bytes 884744 | tf_op jit(solution)/shard_map/ppermute | solution.py:292
  34.4 12.7 %collective-permute-done.3.lower_ref = bf16[2,2,3,6,4,512]{5,4,3,2,1,0:T(4,128)(2,1)S(1)} collective-permute-done((bf16[2,2,3,6,4,512]{5,4,3,2,1,0:T(4,128)(2,1)S(1)}, bf16[2,2,3,6,4,512]{5,4,3,2,1,0:T(4,128)(2,1)S(1)}, u32[]{:S(2)}, u32[]{:S(2)}) %collective-permute-start.3) | collective-permute-done | bytes 294944 | tf_op jit(solution)/shard_map/ppermute | solution.py:292
  47.1 3.8 %all-to-all-done.got_ref = bf16[32,32,512]{2,1,0:T(8,128)(2,1)S(1)} async-done(((bf16[32,32,512]{2,1,0:T(8,128)(2,1)}), bf16[32,32,512]{2,1,0:T(8,128)(2,1)S(1)}, u32[]{:S(2)}, u32[]{:S(2)}) %all-to-all-start) | async-done | bytes 1048608 | tf_op jit(solution)/shard_map/all_to_all | solution.py:347
  50.9 0.2 shard_map.106
  51.1 0.6 collective-permute-start.5
  51.7 0.0 copy-start
  51.7 0.0 copy-start.1
  51.7 1.5 %collective-permute-start.8 = (bf16[32,512]{1,0:T(8,128)(2,1)S(1)}, bf16[32,512]{1,0:T(8,128)(2,1)S(1)}, u32[]{:S(2)}, u32[]{:S(2)}) collective-permute-start(bf16[32,512]{1,0:T(8,128)(2,1)S(1)} %get-tuple-element.52.own_ref), channel_id=1, source_target_pairs={{0,32},{32,64},{64,96},{96,0},{1,33},{33,65},{65,97},{97,1},{2,34}... | collective-permute-start | bytes 98312 | tf_op jit(solution)/shard_map/ppermute | solution.py:353
  53.2 5.6 %collective-permute-start.7 = (bf16[32,512]{1,0:T(8,128)(2,1)S(1)}, bf16[32,512]{1,0:T(8,128)(2,1)S(1)}, u32[]{:S(2)}, u32[]{:S(2)}) collective-permute-start(bf16[32,512]{1,0:T(8,128)(2,1)S(1)} %get-tuple-element.52.own_ref), channel_id=1, source_target_pairs={{0,64},{32,96},{64,0},{96,32},{1,65},{33,97},{65,1},{97,33},{2,66}... | collective-permute-start | bytes 98312 | tf_op jit(solution)/shard_map/ppermute | solution.py:353
  58.7 1.0 %collective-permute-start.6 = (bf16[32,512]{1,0:T(8,128)(2,1)S(1)}, bf16[32,512]{1,0:T(8,128)(2,1)S(1)}, u32[]{:S(2)}, u32[]{:S(2)}) collective-permute-start(bf16[32,512]{1,0:T(8,128)(2,1)S(1)} %get-tuple-element.52.own_ref), channel_id=1, source_target_pairs={{0,96},{32,0},{64,32},{96,64},{1,97},{33,1},{65,33},{97,65},{2,98}... | collective-permute-start | bytes 98312 | tf_op jit(solution)/shard_map/ppermute | solution.py:353
  59.8 0.0 collective-permute-done.8.three_ref
  59.8 1.3 %collective-permute-done.7.two_ref = bf16[32,512]{1,0:T(8,128)(2,1)S(1)} collective-permute-done((bf16[32,512]{1,0:T(8,128)(2,1)S(1)}, bf16[32,512]{1,0:T(8,128)(2,1)S(1)}, u32[]{:S(2)}, u32[]{:S(2)}) %collective-permute-start.7) | collective-permute-done | bytes 32800 | tf_op jit(solution)/shard_map/ppermute | solution.py:353
  61.0 1.7 %collective-permute-done.6.one_ref = bf16[32,512]{1,0:T(8,128)(2,1)S(1)} collective-permute-done((bf16[32,512]{1,0:T(8,128)(2,1)S(1)}, bf16[32,512]{1,0:T(8,128)(2,1)S(1)}, u32[]{:S(2)}, u32[]{:S(2)}) %collective-permute-start.6) | collective-permute-done | bytes 32800 | tf_op jit(solution)/shard_map/ppermute | solution.py:353
  62.7 0.0 collective-permute-done.5.side_ref
  62.7 0.1 shard_map.108
  62.8 23.0 %all_to_all.10 = bf16[32,32,512]{2,1,0:T(8,128)(2,1)S(1)} all-to-all(bf16[32,32,512]{2,1,0:T(8,128)(2,1)S(1)} %shard_map.108), channel_id=1, replica_groups=mesh['xl'=2,'zh'=4,'zl'=2,'c'=2,'y'=4,'xh'=2] {'xh','xl','y','zl'}, dimensions={0} | all-to-all | bytes 2097152 | tf_op jit(solution)/shard_map/all_to_all | solution.py:364
  85.8 2.7 %collective-permute-start.9 = (bf16[4,256,512]{2,1,0:T(8,128)(2,1)S(1)}, bf16[4,256,512]{2,1,0:T(8,128)(2,1)S(1)}, u32[]{:S(2)}, u32[]{:S(2)}) collective-permute-start(bf16[4,256,512]{2,1,0:T(8,128)(2,1)S(1)} %bitcast.11), channel_id=1, source_target_pairs={{0,8},{8,0},{1,9},{9,1},{2,10},{10,2},{3,11},{11,3},{4,12},{12,4},... | collective-permute-start | bytes 3145736 | tf_op jit(solution)/shard_map/ppermute | solution.py:296
  88.5 0.0 copy-done
  88.5 0.0 copy-done.1
  88.5 1.0 %shard_map.107 = (bf16[6,12,4,512]{3,2,1,0:T(4,128)(2,1)}, bf16[6,12,4,512]{3,2,1,0:T(4,128)(2,1)}) custom-call(bf16[6,12,4,512]{3,2,1,0:T(4,128)(2,1)S(1)} %bitcast.14, bf16[6,12,4,512]{3,2,1,0:T(4,128)(2,1)S(1)} %bitcast.16, bf16[2,3,6,4,512]{4,3,2,1,0:T(4,128)(2,1)S(1)} %get-tuple-element.44.own_ref, ...), custom_call_target="tpu_custom_call" | custom-call | tf_op jit(solution)/shard_map/pallas_call | solution.py:384
  89.5 1.6 %shard_map.109 = (f32[512,1536]{1,0:T(8,128)}, f32[512,512]{1,0:T(8,128)}, f32[1,512]{1,0:T(1,128)S(1)}) custom-call(bf16[4,256,512]{2,1,0:T(8,128)(2,1)S(1)} %bitcast.12, bf16[512,1536]{1,0:T(8,128)(2,1)S(1)} %get-tuple-element.37.qkv_ref, f32[1,512]{1,0:T(1,128)S(1)} %get-tuple-element.36.gain_ref), custom_call_target="tpu_custom_call" | custom-call | tf_op jit(solution)/shard_map/pallas_call | solution.py:367
  91.0 0.0 collective-permute-done.9.ref
  91.0 2.1 %shard_map.110 = (f32[512,1536]{1,0:T(8,128)}, f32[512,512]{1,0:T(8,128)}, f32[1,512]{1,0:T(1,128)}) custom-call(bf16[4,256,512]{2,1,0:T(8,128)(2,1)S(1)} %collective-permute-done.9.ref, bf16[512,1536]{1,0:T(8,128)(2,1)S(1)} %get-tuple-element.37.qkv_ref, f32[1,512]{1,0:T(1,128)S(1)} %get-tuple-element.36.gain_ref, ...), custom_call_target="tpu_custom_call", output_to_operand_aliasing={{0}: (3, {}), {1}: (4, {})} | custom-call | tf_op jit(solution)/shard_map/pallas_call | solution.py:375
Async XLA Ops:
  1.8 15.2 %collective-permute-start = (bf16[2,3,6,4,512]{4,3,2,1,0:T(4,128)(2,1)S(1)}, bf16[2,3,6,4,512]{4,3,2,1,0:T(4,128)(2,1)S(1)}, u32[]{:S(2)}, u32[]{:S(2)}) collective-permute-start(bf16[2,3,6,4,512]{4,3,2,1,0:T(4,128)(2,1)S(1)} %get-tuple-element.32), channel_id=1, source_target_pairs={{0,255},{1,248},{2,249},{3,250},{4,251},{5,252},{6,253},{7,254},{8... | collective-permute-start | bytes 442376 | tf_op jit(solution)/shard_map/ppermute | solution.py:292
  8.5 8.5 %collective-permute-start.1 = (bf16[2,3,6,4,512]{4,3,2,1,0:T(4,128)(2,1)S(1)}, bf16[2,3,6,4,512]{4,3,2,1,0:T(4,128)(2,1)S(1)}, u32[]{:S(2)}, u32[]{:S(2)}) collective-permute-start(bf16[2,3,6,4,512]{4,3,2,1,0:T(4,128)(2,1)S(1)} %get-tuple-element.33), channel_id=1, source_target_pairs={{0,7},{1,0},{2,1},{3,2},{4,3},{5,4},{6,5},{7,6},{8,15},{9,8},{10,9... | collective-permute-start | bytes 442376 | tf_op jit(solution)/shard_map/ppermute | solution.py:292
  8.7 8.3 %collective-permute-start.2 = (bf16[2,3,6,4,512]{4,3,2,1,0:T(4,128)(2,1)S(1)}, bf16[2,3,6,4,512]{4,3,2,1,0:T(4,128)(2,1)S(1)}, u32[]{:S(2)}, u32[]{:S(2)}) collective-permute-start(bf16[2,3,6,4,512]{4,3,2,1,0:T(4,128)(2,1)S(1)} %get-tuple-element.34), channel_id=1, source_target_pairs={{0,248},{1,249},{2,250},{3,251},{4,252},{5,253},{6,254},{7,255},{8... | collective-permute-start | bytes 442376 | tf_op jit(solution)/shard_map/ppermute | solution.py:292
  21.4 5.3 %collective-permute-start.4 = (bf16[4,256,512]{2,1,0:T(8,128)(2,1)S(1)}, bf16[4,256,512]{2,1,0:T(8,128)(2,1)S(1)}, u32[]{:S(2)}, u32[]{:S(2)}) collective-permute-start(bf16[4,256,512]{2,1,0:T(8,128)(2,1)S(1)} %get-tuple-element.47), channel_id=1, source_target_pairs={{0,8},{8,0},{1,9},{9,1},{2,10},{10,2},{3,11},{11,3},{4,12},{12,4},... | collective-permute-start | bytes 3145736 | tf_op jit(solution)/shard_map/ppermute | solution.py:296
  27.9 23.0 %all-to-all-start = ((bf16[32,32,512]{2,1,0:T(8,128)(2,1)}), bf16[32,32,512]{2,1,0:T(8,128)(2,1)S(1)}, u32[]{:S(2)}, u32[]{:S(2)}) async-start(bf16[32,32,512]{2,1,0:T(8,128)(2,1)} %bitcast.4), calls=%async_computation | async-start | bytes 2097152 | tf_op jit(solution)/shard_map/all_to_all | solution.py:347
  32.3 14.9 %collective-permute-start.3 = (bf16[2,2,3,6,4,512]{5,4,3,2,1,0:T(4,128)(2,1)S(1)}, bf16[2,2,3,6,4,512]{5,4,3,2,1,0:T(4,128)(2,1)S(1)}, u32[]{:S(2)}, u32[]{:S(2)}) collective-permute-start(bf16[2,2,3,6,4,512]{5,4,3,2,1,0:T(4,128)(2,1)S(1)} %get-tuple-element.45), channel_id=1, source_target_pairs={{0,8},{1,9},{2,10},{3,11},{4,12},{5,13},{6,14},{7,15},{8,16},{9,17... | collective-permute-start | bytes 884744 | tf_op jit(solution)/shard_map/ppermute | solution.py:292
  51.1 11.6 %collective-permute-start.5 = (bf16[2,2,3,6,4,512]{5,4,3,2,1,0:T(4,128)(2,1)S(1)}, bf16[2,2,3,6,4,512]{5,4,3,2,1,0:T(4,128)(2,1)S(1)}, u32[]{:S(2)}, u32[]{:S(2)}) collective-permute-start(bf16[2,2,3,6,4,512]{5,4,3,2,1,0:T(4,128)(2,1)S(1)} %get-tuple-element.49), channel_id=1, source_target_pairs={{0,1},{1,2},{2,3},{3,4},{4,5},{5,6},{6,7},{7,0},{8,9},{9,10},{10,1... | collective-permute-start | bytes 884744 | tf_op jit(solution)/shard_map/ppermute | solution.py:292
  51.7 36.8 %copy-start = (bf16[4,6,12,512]{3,0,2,1:T(4,128)(2,1)S(1)}, bf16[4,6,12,512]{3,0,2,1:T(4,128)(2,1)}, u32[]{:S(2)}) copy-start(bf16[4,6,12,512]{3,0,2,1:T(4,128)(2,1)} %param.6) | copy-start | bytes 884740
  51.7 36.8 %copy-start.1 = (bf16[4,6,12,512]{3,0,2,1:T(4,128)(2,1)S(1)}, bf16[4,6,12,512]{3,0,2,1:T(4,128)(2,1)}, u32[]{:S(2)}) copy-start(bf16[4,6,12,512]{3,0,2,1:T(4,128)(2,1)} %param.7) | copy-start | bytes 884740
  51.7 8.1 %collective-permute-start.8 = (bf16[32,512]{1,0:T(8,128)(2,1)S(1)}, bf16[32,512]{1,0:T(8,128)(2,1)S(1)}, u32[]{:S(2)}, u32[]{:S(2)}) collective-permute-start(bf16[32,512]{1,0:T(8,128)(2,1)S(1)} %get-tuple-element.52.own_ref), channel_id=1, source_target_pairs={{0,32},{32,64},{64,96},{96,0},{1,33},{33,65},{65,97},{97,1},{2,34}... | collective-permute-start | bytes 98312 | tf_op jit(solution)/shard_map/ppermute | solution.py:353
  53.2 7.9 %collective-permute-start.7 = (bf16[32,512]{1,0:T(8,128)(2,1)S(1)}, bf16[32,512]{1,0:T(8,128)(2,1)S(1)}, u32[]{:S(2)}, u32[]{:S(2)}) collective-permute-start(bf16[32,512]{1,0:T(8,128)(2,1)S(1)} %get-tuple-element.52.own_ref), channel_id=1, source_target_pairs={{0,64},{32,96},{64,0},{96,32},{1,65},{33,97},{65,1},{97,33},{2,66}... | collective-permute-start | bytes 98312 | tf_op jit(solution)/shard_map/ppermute | solution.py:353
  58.7 4.0 %collective-permute-start.6 = (bf16[32,512]{1,0:T(8,128)(2,1)S(1)}, bf16[32,512]{1,0:T(8,128)(2,1)S(1)}, u32[]{:S(2)}, u32[]{:S(2)}) collective-permute-start(bf16[32,512]{1,0:T(8,128)(2,1)S(1)} %get-tuple-element.52.own_ref), channel_id=1, source_target_pairs={{0,96},{32,0},{64,32},{96,64},{1,97},{33,1},{65,33},{97,65},{2,98}... | collective-permute-start | bytes 98312 | tf_op jit(solution)/shard_map/ppermute | solution.py:353
  85.8 5.3 %collective-permute-start.9 = (bf16[4,256,512]{2,1,0:T(8,128)(2,1)S(1)}, bf16[4,256,512]{2,1,0:T(8,128)(2,1)S(1)}, u32[]{:S(2)}, u32[]{:S(2)}) collective-permute-start(bf16[4,256,512]{2,1,0:T(8,128)(2,1)S(1)} %bitcast.11), channel_id=1, source_target_pairs={{0,8},{8,0},{1,9},{9,1},{2,10},{10,2},{3,11},{11,3},{4,12},{12,4},... | collective-permute-start | bytes 3145736 | tf_op jit(solution)/shard_map/ppermute | solution.py:296
where the time goes:
time: 93.7 us; the launch traced here: 93.3 us
  starting transfers between devices  33.2 us (35%)
  blocking collectives  23 us (25%)
  waiting for transfers between devices  20 us (21%)
  Pallas kernels  15 us (16%)
  local copies, waits for them, and re-layouts  1.2 us (1%)
    all_to_all x1, blocking collectives, on_device(): mine = lax.all_to_all(parts, NEAR, 0, 0)  23 us
    ppermute x5, starting transfers between devices, moved(): return lax.ppermute(block, AXES, route)  15.1 us
    ppermute x5, waiting for transfers between devices, moved(): return lax.ppermute(block, AXES, route)  12.8 us
    ppermute x3, starting transfers between devices, on_device(): lax.ppermute(part, FAR, [(n, (n - step) % N_FAR) for n in range(N_FAR)])  8.09 us
    ppermute x2, starting transfers between devices, swapped(): return lax.ppermute(block, 'c', [(0, 1), (1, 0)])  5.78 us
    pallas_call x1, Pallas kernels, on_device(): call(attend_kernel, [shaped((4, HALF_D, D), BF16), shaped((2, D, TOKENS),...  4.34 us
    all_to_all x1, starting transfers between devices, on_device(): got = lax.all_to_all(half.reshape(N_NEAR, CHUNK, D), NEAR, 0, 0)  4.3 us
    all_to_all x1, waiting for transfers between devices, on_device(): got = lax.all_to_all(half.reshape(N_NEAR, CHUNK, D), NEAR, 0, 0)  3.77 us
  transfers between devices with their start and end apart: 11, of which 5 were waited for; matrix products, arithmetic and copies ran while one was open for 1% of the time, Pallas kernels for 6%

commit v1 on v0

--- a/solution.py
+++ b/solution.py
@@ -16,7 +16,7 @@
 HALF_R = 3
 HALF_C = 6
 EPS = 1e-05
-TOGETHER = 4
+TOGETHER = 8
 SIZES = {"xl": 2, "zh": 4, "zl": 2, "c": 2, "y": 4, "xh": 2}
 AXES = tuple(SIZES)
 LAT = AXES[:4]
@@ -194,8 +194,15 @@
         copy.wait()
 
 
-def add_kernel(keep_ref, got_ref, out_ref):
-    out_ref[...] = (keep_ref[...].astype(F32) + got_ref[...].astype(F32)).astype(BF16)
+def add_kernel(keep_ref, got_ref, out_ref, held, sems):
+    copies = []
+    for block in range(4):
+        held[block] = (keep_ref[block].astype(F32) + got_ref[block].astype(F32)).astype(BF16)
+        copy = pltpu.make_async_copy(held.at[block], out_ref.at[block], sems.at[block])
+        copy.start()
+        copies.append(copy)
+    for copy in copies:
+        copy.wait()
 
 
 def sum_kernel(got_ref, lower_ref, right_ref, out_ref, side_ref):
@@ -241,23 +248,29 @@
                 total += product[:, q * 128 : (q + 1) * 128]
     sums = jnp.sum(total.T, axis=0, keepdims=True)
     gain_out[:, here] = sums / gain_ref[:, here]
-    for copy in copies:
-        copy.wait()
+    return copies
 
 
 def mine_kernel(ref, qkv_ref, gain_ref, qkv_out, proj_out, gain_out, wide, sems):
     gain_out[...] = jnp.zeros_like(gain_out)
     core = lax.axis_index("c")
-    grads_half(core, ref, qkv_ref, gain_ref, qkv_out, proj_out, gain_out, wide, sems)
+    copies = grads_half(core, ref, qkv_ref, gain_ref, qkv_out, proj_out, gain_out, wide, sems)
+    for copy in copies:
+        copy.wait()
 
 
 def other_kernel(
-    ref, qkv_ref, gain_ref, qkv_in, proj_in, gain_in, qkv_out, proj_out, gain_out, wide, sems
+    ref, qkv_ref, gain_ref, qkv_in, proj_in, gain_in, qkv_out, proj_out, gain_out, wide, sems,
+    held, gain_sem,
 ):
     del qkv_in, proj_in
-    gain_out[...] = gain_in[...]
-    core = lax.axis_index("c")
-    grads_half(1 - core, ref, qkv_ref, gain_ref, qkv_out, proj_out, gain_out, wide, sems)
+    held[...] = gain_in[...]
+    half = 1 - lax.axis_index("c")
+    copies = grads_half(half, ref, qkv_ref, gain_ref, qkv_out, proj_out, held, wide, sems)
+    copies.append(pltpu.make_async_copy(held, gain_out, gain_sem))
+    copies[-1].start()
+    for copy in copies:
+        copy.wait()
 
 
 def call(kernel, outs, scratch=(), ins=None, out_specs=None, mib=8, aliases=None):
@@ -343,7 +356,14 @@
         [shaped((4, HALF_D, D), BF16), shaped(PIECE, BF16), shaped(PIECE, BF16), pair],
         mib=16,
     )(*state, gain, qkv_weight, proj_weight)
-    half = call(add_kernel, shaped((4, HALF_D, D), BF16), mib=4)(keep, got)
+    half = call(
+        add_kernel,
+        shaped((4, HALF_D, D), BF16),
+        [pltpu.VMEM((4, HALF_D, D), BF16), pltpu.SemaphoreType.DMA((4,))],
+        [vmem] * 2,
+        anywhere,
+        mib=4,
+    )(keep, got)
     got = lax.all_to_all(half.reshape(N_NEAR, CHUNK, D), NEAR, 0, 0)
     lower_back = moved(lower_back, 1, 0)
     part, side_back = call(
@@ -375,9 +395,14 @@
     grad_qkv, grad_proj, grad_gain = call(
         other_kernel,
         [shaped((D, 3 * D), F32), shaped((D, D), F32), shaped((1, D), F32)],
-        [pltpu.VMEM((4, HALF_D, D), F32), pltpu.SemaphoreType.DMA((4,))],
+        [
+            pltpu.VMEM((4, HALF_D, D), F32),
+            pltpu.SemaphoreType.DMA((4,)),
+            pltpu.VMEM((1, D), F32),
+            pltpu.SemaphoreType.DMA,
+        ],
         [vmem] * 3 + [anywhere] * 2 + [vmem],
-        [anywhere, anywhere, vmem],
+        [anywhere] * 3,
         mib=6,
         aliases={3: 0, 4: 1},
     )(other, qkv_weight, gain, *grads)

time: 93.7 us -> 92.9 us (level)
  no operation moved by 1% of the time
where the time goes in v1:
time: 92.9 us; the launch traced here: 92.6 us
  starting transfers between devices  33.2 us (36%)
  blocking collectives  23 us (25%)
  waiting for transfers between devices  20 us (22%)
  Pallas kernels  14.2 us (15%)
  local copies, waits for them, and re-layouts  1.2 us (1%)
    all_to_all x1, blocking collectives, on_device(): mine = lax.all_to_all(parts, NEAR, 0, 0)  23 us
    ppermute x5, starting transfers between devices, moved(): return lax.ppermute(block, AXES, route)  15.1 us
    ppermute x5, waiting for transfers between devices, moved(): return lax.ppermute(block, AXES, route)  12.8 us
    ppermute x3, starting transfers between devices, on_device(): lax.ppermute(part, FAR, [(n, (n - step) % N_FAR) for n in range(N_FAR)])  8.09 us
    ppermute x2, starting transfers between devices, swapped(): return lax.ppermute(block, 'c', [(0, 1), (1, 0)])  5.77 us
    all_to_all x1, starting transfers between devices, on_device(): got = lax.all_to_all(half.reshape(N_NEAR, CHUNK, D), NEAR, 0, 0)  4.31 us
    pallas_call x1, Pallas kernels, on_device(): call(attend_kernel, [shaped((4, HALF_D, D), BF16), shaped((2, D, TOKENS),...  4.25 us
    all_to_all x1, waiting for transfers between devices, on_device(): got = lax.all_to_all(half.reshape(N_NEAR, CHUNK, D), NEAR, 0, 0)  3.77 us
  transfers between devices with their start and end apart: 11, of which 5 were waited for; matrix products, arithmetic and copies ran while one was open for 1% of the time, Pallas kernels for 6%

profile of v1, /device:TPU:1, one launch (start us, length us, event | category | flops | bytes accessed | tf_op | source)
XLA Modules:
  0.0 92.6 jit_solution(12261696459990671163)
XLA Ops:
  0.6 1.2 %shard_map.101 = (bf16[2,3,6,4,512]{4,3,2,1,0:T(4,128)(2,1)S(1)}, bf16[2,3,6,4,512]{4,3,2,1,0:T(4,128)(2,1)S(1)}, bf16[2,3,6,4,512]{4,3,2,1,0:T(4,128)(2,1)S(1)}, bf16[2,3,6,4,512]{4,3,2,1,0:T(4,128)(2,1)S(1)}) custom-call(bf16[6,12,4,512]{3,2,1,0:T(4,128)(2,1)} %bitcast.13, bf16[6,12,4,512]{3,2,1,0:T(4,128)(2,1)} %bitcast.15), custom_call_target="tpu_custom_call" | custom-call | tf_op jit(solution)/shard_map/pallas_call | solution.py:318
  1.8 6.7 %collective-permute-start = (bf16[2,3,6,4,512]{4,3,2,1,0:T(4,128)(2,1)S(1)}, bf16[2,3,6,4,512]{4,3,2,1,0:T(4,128)(2,1)S(1)}, u32[]{:S(2)}, u32[]{:S(2)}) collective-permute-start(bf16[2,3,6,4,512]{4,3,2,1,0:T(4,128)(2,1)S(1)} %get-tuple-element.32), channel_id=1, source_target_pairs={{0,255},{1,248},{2,249},{3,250},{4,251},{5,252},{6,253},{7,254},{8... | collective-permute-start | bytes 442376 | tf_op jit(solution)/shard_map/ppermute | solution.py:305
  8.5 0.2 collective-permute-start.1
  8.7 5.4 %collective-permute-start.2 = (bf16[2,3,6,4,512]{4,3,2,1,0:T(4,128)(2,1)S(1)}, bf16[2,3,6,4,512]{4,3,2,1,0:T(4,128)(2,1)S(1)}, u32[]{:S(2)}, u32[]{:S(2)}) collective-permute-start(bf16[2,3,6,4,512]{4,3,2,1,0:T(4,128)(2,1)S(1)} %get-tuple-element.34), channel_id=1, source_target_pairs={{0,248},{1,249},{2,250},{3,251},{4,252},{5,253},{6,254},{7,255},{8... | collective-permute-start | bytes 442376 | tf_op jit(solution)/shard_map/ppermute | solution.py:305
  14.2 0.8 reshape.27
  15.0 0.3 copy.14
  15.2 0.1 eq.15
  15.4 1.5 %shard_map.102 = (bf16[512,1536]{1,0:T(8,128)(2,1)S(1)}, bf16[512,512]{1,0:T(8,128)(2,1)S(1)}, f32[1,512]{1,0:T(1,128)S(1)}) custom-call(bf16[512,1536]{1,0:T(8,128)(2,1)} %qkv_ref.1, bf16[512,512]{1,0:T(8,128)(2,1)} %proj_ref.1, f32[1,512]{1,0:T(1,128)} %bitcast.18), custom_call_target="tpu_custom_call" | custom-call | tf_op jit(solution)/shard_map/pallas_call | solution.py:332
  16.9 0.1 compare_select_fusion.bias_ref
  17.0 0.0 collective-permute-done.corner_ref
  17.0 0.0 collective-permute-done.1.right_ref
  17.1 0.0 collective-permute-done.2.below_ref
  17.1 4.3 %shard_map.103 = (bf16[4,256,512]{2,1,0:T(8,128)(2,1)S(1)}, bf16[2,512,288]{2,1,0:T(8,128)(2,1)S(1)}, bf16[4,288,512]{2,1,0:T(8,128)(2,1)S(1)}, bf16[288,512]{1,...) custom-call(bf16[2,3,6,4,512]{4,3,2,1,0:T(4,128)(2,1)S(1)} %collective-permute-done.corner_ref, ...), custom_call_target="tpu_custom_call" | custom-call | tf_op jit(solution)/shard_map/pallas_call | solution.py:340
  21.3 3.0 %collective-permute-start.4 = (bf16[4,256,512]{2,1,0:T(8,128)(2,1)S(1)}, bf16[4,256,512]{2,1,0:T(8,128)(2,1)S(1)}, u32[]{:S(2)}, u32[]{:S(2)}) collective-permute-start(bf16[4,256,512]{2,1,0:T(8,128)(2,1)S(1)} %get-tuple-element.47), channel_id=1, source_target_pairs={{0,8},{8,0},{1,9},{9,1},{2,10},{10,2},{3,11},{11,3},{4,12},{12,4},... | collective-permute-start | bytes 3145736 | tf_op jit(solution)/shard_map/ppermute | solution.py:309
  24.4 1.8 %shard_map.104 = (bf16[4,256,512]{2,1,0:T(8,128)(2,1)S(1)}, bf16[2,3,6,4,512]{4,3,2,1,0:T(4,128)(2,1)S(1)}, bf16[2,3,6,4,512]{4,3,2,1,0:T(4,128)(2,1)S(1)}, bf16[2,2,3,6,4,512]{5,4,3,2,1,0:T(4,128)(2,1)S(1)}) custom-call(bf16[2,512,288]{2,1,0:T(8,128)(2,1)S(1)} %get-tuple-element.39.left_ref, bf16[4,288,512]{2,1,0:T(8,128)(2,1)S(1)} %get-tuple-element.40.rows_ref, ...), custom_call_target="tpu_custom_call" | custom-call | tf_op jit(solution)/shard_map/pallas_call | solution.py:354
  26.1 0.5 collective-permute-done.4.got_ref
  26.7 1.1 %shard_map.105 = bf16[4,256,512]{2,1,0:T(8,128)(2,1)} custom-call(bf16[4,256,512]{2,1,0:T(8,128)(2,1)S(1)} %get-tuple-element.46.keep_ref, bf16[4,256,512]{2,1,0:T(8,128)(2,1)S(1)} %collective-permute-done.4.got_ref), custom_call_target="tpu_custom_call" | custom-call | tf_op jit(solution)/shard_map/pallas_call | solution.py:359
  27.7 4.3 %all-to-all-start = ((bf16[32,32,512]{2,1,0:T(8,128)(2,1)}), bf16[32,32,512]{2,1,0:T(8,128)(2,1)S(1)}, u32[]{:S(2)}, u32[]{:S(2)}) async-start(bf16[32,32,512]{2,1,0:T(8,128)(2,1)} %bitcast.4), calls=%async_computation | async-start | bytes 2097152 | tf_op jit(solution)/shard_map/all_to_all | solution.py:367
  32.0 2.1 %collective-permute-start.3 = (bf16[2,2,3,6,4,512]{5,4,3,2,1,0:T(4,128)(2,1)S(1)}, bf16[2,2,3,6,4,512]{5,4,3,2,1,0:T(4,128)(2,1)S(1)}, u32[]{:S(2)}, u32[]{:S(2)}) collective-permute-start(bf16[2,2,3,6,4,512]{5,4,3,2,1,0:T(4,128)(2,1)S(1)} %get-tuple-element.45), channel_id=1, source_target_pairs={{0,8},{1,9},{2,10},{3,11},{4,12},{5,13},{6,14},{7,15},{8,16},{9,17... | collective-permute-start | bytes 884744 | tf_op jit(solution)/shard_map/ppermute | solution.py:305
  34.2 12.7 %collective-permute-done.3.lower_ref = bf16[2,2,3,6,4,512]{5,4,3,2,1,0:T(4,128)(2,1)S(1)} collective-permute-done((bf16[2,2,3,6,4,512]{5,4,3,2,1,0:T(4,128)(2,1)S(1)}, bf16[2,2,3,6,4,512]{5,4,3,2,1,0:T(4,128)(2,1)S(1)}, u32[]{:S(2)}, u32[]{:S(2)}) %collective-permute-start.3) | collective-permute-done | bytes 294944 | tf_op jit(solution)/shard_map/ppermute | solution.py:305
  46.9 3.8 %all-to-all-done.got_ref = bf16[32,32,512]{2,1,0:T(8,128)(2,1)S(1)} async-done(((bf16[32,32,512]{2,1,0:T(8,128)(2,1)}), bf16[32,32,512]{2,1,0:T(8,128)(2,1)S(1)}, u32[]{:S(2)}, u32[]{:S(2)}) %all-to-all-start) | async-done | bytes 1048608 | tf_op jit(solution)/shard_map/all_to_all | solution.py:367
  50.7 0.2 shard_map.106
  50.8 0.6 collective-permute-start.5
  51.5 0.0 copy-start
  51.5 0.0 copy-start.1
  51.5 1.5 %collective-permute-start.8 = (bf16[32,512]{1,0:T(8,128)(2,1)S(1)}, bf16[32,512]{1,0:T(8,128)(2,1)S(1)}, u32[]{:S(2)}, u32[]{:S(2)}) collective-permute-start(bf16[32,512]{1,0:T(8,128)(2,1)S(1)} %get-tuple-element.52.own_ref), channel_id=1, source_target_pairs={{0,32},{32,64},{64,96},{96,0},{1,33},{33,65},{65,97},{97,1},{2,34}... | collective-permute-start | bytes 98312 | tf_op jit(solution)/shard_map/ppermute | solution.py:373
  52.9 5.6 %collective-permute-start.7 = (bf16[32,512]{1,0:T(8,128)(2,1)S(1)}, bf16[32,512]{1,0:T(8,128)(2,1)S(1)}, u32[]{:S(2)}, u32[]{:S(2)}) collective-permute-start(bf16[32,512]{1,0:T(8,128)(2,1)S(1)} %get-tuple-element.52.own_ref), channel_id=1, source_target_pairs={{0,64},{32,96},{64,0},{96,32},{1,65},{33,97},{65,1},{97,33},{2,66}... | collective-permute-start | bytes 98312 | tf_op jit(solution)/shard_map/ppermute | solution.py:373
  58.5 1.0 %collective-permute-start.6 = (bf16[32,512]{1,0:T(8,128)(2,1)S(1)}, bf16[32,512]{1,0:T(8,128)(2,1)S(1)}, u32[]{:S(2)}, u32[]{:S(2)}) collective-permute-start(bf16[32,512]{1,0:T(8,128)(2,1)S(1)} %get-tuple-element.52.own_ref), channel_id=1, source_target_pairs={{0,96},{32,0},{64,32},{96,64},{1,97},{33,1},{65,33},{97,65},{2,98}... | collective-permute-start | bytes 98312 | tf_op jit(solution)/shard_map/ppermute | solution.py:373
  59.5 0.0 collective-permute-done.8.three_ref
  59.5 1.3 %collective-permute-done.7.two_ref = bf16[32,512]{1,0:T(8,128)(2,1)S(1)} collective-permute-done((bf16[32,512]{1,0:T(8,128)(2,1)S(1)}, bf16[32,512]{1,0:T(8,128)(2,1)S(1)}, u32[]{:S(2)}, u32[]{:S(2)}) %collective-permute-start.7) | collective-permute-done | bytes 32800 | tf_op jit(solution)/shard_map/ppermute | solution.py:373
  60.8 1.7 %collective-permute-done.6.one_ref = bf16[32,512]{1,0:T(8,128)(2,1)S(1)} collective-permute-done((bf16[32,512]{1,0:T(8,128)(2,1)S(1)}, bf16[32,512]{1,0:T(8,128)(2,1)S(1)}, u32[]{:S(2)}, u32[]{:S(2)}) %collective-permute-start.6) | collective-permute-done | bytes 32800 | tf_op jit(solution)/shard_map/ppermute | solution.py:373
  62.5 0.0 collective-permute-done.5.side_ref
  62.5 0.1 shard_map.108
  62.6 23.0 %all_to_all.10 = bf16[32,32,512]{2,1,0:T(8,128)(2,1)S(1)} all-to-all(bf16[32,32,512]{2,1,0:T(8,128)(2,1)S(1)} %shard_map.108), channel_id=1, replica_groups=mesh['xl'=2,'zh'=4,'zl'=2,'c'=2,'y'=4,'xh'=2] {'xh','xl','y','zl'}, dimensions={0} | all-to-all | bytes 2097152 | tf_op jit(solution)/shard_map/all_to_all | solution.py:384
  85.5 2.7 %collective-permute-start.9 = (bf16[4,256,512]{2,1,0:T(8,128)(2,1)S(1)}, bf16[4,256,512]{2,1,0:T(8,128)(2,1)S(1)}, u32[]{:S(2)}, u32[]{:S(2)}) collective-permute-start(bf16[4,256,512]{2,1,0:T(8,128)(2,1)S(1)} %bitcast.11), channel_id=1, source_target_pairs={{0,8},{8,0},{1,9},{9,1},{2,10},{10,2},{3,11},{11,3},{4,12},{12,4},... | collective-permute-start | bytes 3145736 | tf_op jit(solution)/shard_map/ppermute | solution.py:309
  88.3 0.0 copy-done
  88.3 0.0 copy-done.1
  88.3 1.0 %shard_map.107 = (bf16[6,12,4,512]{3,2,1,0:T(4,128)(2,1)}, bf16[6,12,4,512]{3,2,1,0:T(4,128)(2,1)}) custom-call(bf16[6,12,4,512]{3,2,1,0:T(4,128)(2,1)S(1)} %bitcast.14, bf16[6,12,4,512]{3,2,1,0:T(4,128)(2,1)S(1)} %bitcast.16, bf16[2,3,6,4,512]{4,3,2,1,0:T(4,128)(2,1)S(1)} %get-tuple-element.44.own_ref, ...), custom_call_target="tpu_custom_call" | custom-call | tf_op jit(solution)/shard_map/pallas_call | solution.py:409
  89.3 1.6 %shard_map.109 = (f32[512,1536]{1,0:T(8,128)}, f32[512,512]{1,0:T(8,128)}, f32[1,512]{1,0:T(1,128)S(1)}) custom-call(bf16[4,256,512]{2,1,0:T(8,128)(2,1)S(1)} %bitcast.12, bf16[512,1536]{1,0:T(8,128)(2,1)S(1)} %get-tuple-element.37.qkv_ref, f32[1,512]{1,0:T(1,128)S(1)} %get-tuple-element.36.gain_ref), custom_call_target="tpu_custom_call" | custom-call | tf_op jit(solution)/shard_map/pallas_call | solution.py:387
  90.8 0.0 collective-permute-done.9.ref
  90.8 1.6 %shard_map.110 = (f32[512,1536]{1,0:T(8,128)}, f32[512,512]{1,0:T(8,128)}, f32[1,512]{1,0:T(1,128)}) custom-call(bf16[4,256,512]{2,1,0:T(8,128)(2,1)S(1)} %collective-permute-done.9.ref, bf16[512,1536]{1,0:T(8,128)(2,1)S(1)} %get-tuple-element.37.qkv_ref, f32[1,512]{1,0:T(1,128)S(1)} %get-tuple-element.36.gain_ref, ...), custom_call_target="tpu_custom_call", output_to_operand_aliasing={{0}: (3, {}), {1}: (4, {})} | custom-call | tf_op jit(solution)/shard_map/pallas_call | solution.py:395
Async XLA Ops:
  1.8 15.2 %collective-permute-start = (bf16[2,3,6,4,512]{4,3,2,1,0:T(4,128)(2,1)S(1)}, bf16[2,3,6,4,512]{4,3,2,1,0:T(4,128)(2,1)S(1)}, u32[]{:S(2)}, u32[]{:S(2)}) collective-permute-start(bf16[2,3,6,4,512]{4,3,2,1,0:T(4,128)(2,1)S(1)} %get-tuple-element.32), channel_id=1, source_target_pairs={{0,255},{1,248},{2,249},{3,250},{4,251},{5,252},{6,253},{7,254},{8... | collective-permute-start | bytes 442376 | tf_op jit(solution)/shard_map/ppermute | solution.py:305
  8.5 8.5 %collective-permute-start.1 = (bf16[2,3,6,4,512]{4,3,2,1,0:T(4,128)(2,1)S(1)}, bf16[2,3,6,4,512]{4,3,2,1,0:T(4,128)(2,1)S(1)}, u32[]{:S(2)}, u32[]{:S(2)}) collective-permute-start(bf16[2,3,6,4,512]{4,3,2,1,0:T(4,128)(2,1)S(1)} %get-tuple-element.33), channel_id=1, source_target_pairs={{0,7},{1,0},{2,1},{3,2},{4,3},{5,4},{6,5},{7,6},{8,15},{9,8},{10,9... | collective-permute-start | bytes 442376 | tf_op jit(solution)/shard_map/ppermute | solution.py:305
  8.7 8.3 %collective-permute-start.2 = (bf16[2,3,6,4,512]{4,3,2,1,0:T(4,128)(2,1)S(1)}, bf16[2,3,6,4,512]{4,3,2,1,0:T(4,128)(2,1)S(1)}, u32[]{:S(2)}, u32[]{:S(2)}) collective-permute-start(bf16[2,3,6,4,512]{4,3,2,1,0:T(4,128)(2,1)S(1)} %get-tuple-element.34), channel_id=1, source_target_pairs={{0,248},{1,249},{2,250},{3,251},{4,252},{5,253},{6,254},{7,255},{8... | collective-permute-start | bytes 442376 | tf_op jit(solution)/shard_map/ppermute | solution.py:305
  21.3 5.3 %collective-permute-start.4 = (bf16[4,256,512]{2,1,0:T(8,128)(2,1)S(1)}, bf16[4,256,512]{2,1,0:T(8,128)(2,1)S(1)}, u32[]{:S(2)}, u32[]{:S(2)}) collective-permute-start(bf16[4,256,512]{2,1,0:T(8,128)(2,1)S(1)} %get-tuple-element.47), channel_id=1, source_target_pairs={{0,8},{8,0},{1,9},{9,1},{2,10},{10,2},{3,11},{11,3},{4,12},{12,4},... | collective-permute-start | bytes 3145736 | tf_op jit(solution)/shard_map/ppermute | solution.py:309
  27.7 23.0 %all-to-all-start = ((bf16[32,32,512]{2,1,0:T(8,128)(2,1)}), bf16[32,32,512]{2,1,0:T(8,128)(2,1)S(1)}, u32[]{:S(2)}, u32[]{:S(2)}) async-start(bf16[32,32,512]{2,1,0:T(8,128)(2,1)} %bitcast.4), calls=%async_computation | async-start | bytes 2097152 | tf_op jit(solution)/shard_map/all_to_all | solution.py:367
  32.0 14.9 %collective-permute-start.3 = (bf16[2,2,3,6,4,512]{5,4,3,2,1,0:T(4,128)(2,1)S(1)}, bf16[2,2,3,6,4,512]{5,4,3,2,1,0:T(4,128)(2,1)S(1)}, u32[]{:S(2)}, u32[]{:S(2)}) collective-permute-start(bf16[2,2,3,6,4,512]{5,4,3,2,1,0:T(4,128)(2,1)S(1)} %get-tuple-element.45), channel_id=1, source_target_pairs={{0,8},{1,9},{2,10},{3,11},{4,12},{5,13},{6,14},{7,15},{8,16},{9,17... | collective-permute-start | bytes 884744 | tf_op jit(solution)/shard_map/ppermute | solution.py:305
  50.8 11.6 %collective-permute-start.5 = (bf16[2,2,3,6,4,512]{5,4,3,2,1,0:T(4,128)(2,1)S(1)}, bf16[2,2,3,6,4,512]{5,4,3,2,1,0:T(4,128)(2,1)S(1)}, u32[]{:S(2)}, u32[]{:S(2)}) collective-permute-start(bf16[2,2,3,6,4,512]{5,4,3,2,1,0:T(4,128)(2,1)S(1)} %get-tuple-element.49), channel_id=1, source_target_pairs={{0,1},{1,2},{2,3},{3,4},{4,5},{5,6},{6,7},{7,0},{8,9},{9,10},{10,1... | collective-permute-start | bytes 884744 | tf_op jit(solution)/shard_map/ppermute | solution.py:305
  51.5 36.8 %copy-start = (bf16[4,6,12,512]{3,0,2,1:T(4,128)(2,1)S(1)}, bf16[4,6,12,512]{3,0,2,1:T(4,128)(2,1)}, u32[]{:S(2)}) copy-start(bf16[4,6,12,512]{3,0,2,1:T(4,128)(2,1)} %param.6) | copy-start | bytes 884740
  51.5 36.8 %copy-start.1 = (bf16[4,6,12,512]{3,0,2,1:T(4,128)(2,1)S(1)}, bf16[4,6,12,512]{3,0,2,1:T(4,128)(2,1)}, u32[]{:S(2)}) copy-start(bf16[4,6,12,512]{3,0,2,1:T(4,128)(2,1)} %param.7) | copy-start | bytes 884740
  51.5 8.1 %collective-permute-start.8 = (bf16[32,512]{1,0:T(8,128)(2,1)S(1)}, bf16[32,512]{1,0:T(8,128)(2,1)S(1)}, u32[]{:S(2)}, u32[]{:S(2)}) collective-permute-start(bf16[32,512]{1,0:T(8,128)(2,1)S(1)} %get-tuple-element.52.own_ref), channel_id=1, source_target_pairs={{0,32},{32,64},{64,96},{96,0},{1,33},{33,65},{65,97},{97,1},{2,34}... | collective-permute-start | bytes 98312 | tf_op jit(solution)/shard_map/ppermute | solution.py:373
  52.9 7.9 %collective-permute-start.7 = (bf16[32,512]{1,0:T(8,128)(2,1)S(1)}, bf16[32,512]{1,0:T(8,128)(2,1)S(1)}, u32[]{:S(2)}, u32[]{:S(2)}) collective-permute-start(bf16[32,512]{1,0:T(8,128)(2,1)S(1)} %get-tuple-element.52.own_ref), channel_id=1, source_target_pairs={{0,64},{32,96},{64,0},{96,32},{1,65},{33,97},{65,1},{97,33},{2,66}... | collective-permute-start | bytes 98312 | tf_op jit(solution)/shard_map/ppermute | solution.py:373
  58.5 4.0 %collective-permute-start.6 = (bf16[32,512]{1,0:T(8,128)(2,1)S(1)}, bf16[32,512]{1,0:T(8,128)(2,1)S(1)}, u32[]{:S(2)}, u32[]{:S(2)}) collective-permute-start(bf16[32,512]{1,0:T(8,128)(2,1)S(1)} %get-tuple-element.52.own_ref), channel_id=1, source_target_pairs={{0,96},{32,0},{64,32},{96,64},{1,97},{33,1},{65,33},{97,65},{2,98}... | collective-permute-start | bytes 98312 | tf_op jit(solution)/shard_map/ppermute | solution.py:373
  85.5 5.3 %collective-permute-start.9 = (bf16[4,256,512]{2,1,0:T(8,128)(2,1)S(1)}, bf16[4,256,512]{2,1,0:T(8,128)(2,1)S(1)}, u32[]{:S(2)}, u32[]{:S(2)}) collective-permute-start(bf16[4,256,512]{2,1,0:T(8,128)(2,1)S(1)} %bitcast.11), channel_id=1, source_target_pairs={{0,8},{8,0},{1,9},{9,1},{2,10},{10,2},{3,11},{11,3},{4,12},{12,4},... | collective-permute-start | bytes 3145736 | tf_op jit(solution)/shard_map/ppermute | solution.py:309

commit v2 on v1

--- a/solution.py
+++ b/solution.py
@@ -21,7 +21,6 @@
 AXES = tuple(SIZES)
 LAT = AXES[:4]
 LON = AXES[4:]
-NEAR = ("xh", "xl", "y", "zl")
 N_NEAR = 32
 FAR = "zh"
 N_FAR = 4
@@ -29,6 +28,23 @@
 PIECE = (2, HALF_R, HALF_C, 4, D)
 F32 = jnp.float32
 BF16 = jnp.bfloat16
+
+
+def spot(x, y, z, core):
+    return ((x % 2) * 16 + z * 2 + core) * 8 + y * 2 + x // 2
+
+
+FOUR, EIGHT, TWO = range(4), range(8), range(2)
+LINES = [[spot(x, y, z, 0) for x in FOUR] for y in FOUR for z in EIGHT]
+LINES += [[spot(x, y, z, 1) for y in FOUR] for x in FOUR for z in EIGHT]
+SHEETS = [[spot(x, y, 2 * f + z, 0) for y in FOUR for z in TWO] for x in FOUR for f in FOUR]
+SHEETS += [[spot(x, y, 2 * f + z, 1) for x in FOUR for z in TWO] for y in FOUR for f in FOUR]
+NEAR = [[spot(x, y, 2 * f + z, 0) for x in FOUR for y in FOUR for z in TWO] for f in FOUR]
+NEAR += [[spot(x, y, 2 * f + z, 1) for y in FOUR for x in FOUR for z in TWO] for f in FOUR]
+
+
+def exchanged(parts, groups):
+    return lax.all_to_all(parts, AXES, 0, 0, axis_index_groups=groups)
 
 
 def dot(left, right):
@@ -203,6 +219,15 @@
         copies.append(copy)
     for copy in copies:
         copy.wait()
+
+
+def line_kernel(got_ref, out_ref):
+    for n in range(8):
+        rows = slice(n * CHUNK, (n + 1) * CHUNK)
+        total = got_ref[0, rows].astype(F32)
+        for line in range(1, 4):
+            total += got_ref[line, rows].astype(F32)
+        out_ref[n] = total.astype(BF16)
 
 
 def sum_kernel(got_ref, lower_ref, right_ref, out_ref, side_ref):
@@ -364,7 +389,9 @@
         anywhere,
         mib=4,
     )(keep, got)
-    got = lax.all_to_all(half.reshape(N_NEAR, CHUNK, D), NEAR, 0, 0)
+    got = exchanged(half.reshape(4, 8 * CHUNK, D), LINES)
+    part = call(line_kernel, shaped((8, CHUNK, D), BF16), mib=6)(got)
+    got = exchanged(part, SHEETS)
     lower_back = moved(lower_back, 1, 0)
     part, side_back = call(
         sum_kernel, [shaped((CHUNK, D), BF16), pair], ins=[vmem] * 3, out_specs=[vmem] * 2, mib=6
@@ -381,7 +408,7 @@
         out_specs=vmem,
         mib=4,
     )(part, *others, side_back)
-    mine = lax.all_to_all(parts, NEAR, 0, 0)
+    mine = exchanged(parts, NEAR)
     mine = mine.reshape(4, HALF_D, D)
     other = swapped(mine)
     grads = call(

time: 92.9 us -> 94.1 us (1.013)
  waiting for transfers between devices: 20 us -> 8.15 us
  blocking collectives: 23 us -> 32.2 us
  starting transfers between devices: 33.2 us -> 37 us
    all_to_all x1 -> x2, blocking collectives: 23 us -> 32.2 us  [exchanged(): return lax.all_to_all(parts, AXES, 0, 0, axis_index_groups=groups)]
    ppermute x5, waiting for transfers between devices: 12.8 us -> 3.84 us  [moved(): return lax.ppermute(block, AXES, route)]
    all_to_all x1, waiting for transfers between devices: 3.77 us -> 0.87 us  [exchanged(): return lax.all_to_all(parts, AXES, 0, 0, axis_index_groups=groups)]
    ppermute x2, starting transfers between devices: 5.77 us -> 7.97 us  [swapped(): return lax.ppermute(block, 'c', [(0, 1), (1, 0)])]
    ppermute x5, starting transfers between devices: 15.1 us -> 16.3 us  [moved(): return lax.ppermute(block, AXES, route)]
    ppermute x3, starting transfers between devices: 8.09 us -> 9.28 us  [on_device(): lax.ppermute(part, FAR, [(n, (n - step) % N_FAR) for n in range(N_FAR)])]
where the time goes in v2:
time: 94.1 us; the launch traced here: 93.7 us
  starting transfers between devices  37 us (39%)
  blocking collectives  32.2 us (34%)
  Pallas kernels  14.2 us (15%)
  waiting for transfers between devices  8.15 us (9%)
  local copies, waits for them, and re-layouts  1.2 us (1%)
    all_to_all x2, blocking collectives, exchanged(): return lax.all_to_all(parts, AXES, 0, 0, axis_index_groups=groups)  32.2 us
    ppermute x5, starting transfers between devices, moved(): return lax.ppermute(block, AXES, route)  16.3 us
    ppermute x3, starting transfers between devices, on_device(): lax.ppermute(part, FAR, [(n, (n - step) % N_FAR) for n in range(N_FAR)])  9.28 us
    ppermute x2, starting transfers between devices, swapped(): return lax.ppermute(block, 'c', [(0, 1), (1, 0)])  7.97 us
    pallas_call x1, Pallas kernels, on_device(): call(attend_kernel, [shaped((4, HALF_D, D), BF16), shaped((2, D, TOKENS),...  4.25 us
    ppermute x5, waiting for transfers between devices, moved(): return lax.ppermute(block, AXES, route)  3.84 us
    all_to_all x1, starting transfers between devices, exchanged(): return lax.all_to_all(parts, AXES, 0, 0, axis_index_groups=groups)  3.41 us
    ppermute x3, waiting for transfers between devices, on_device(): lax.ppermute(part, FAR, [(n, (n - step) % N_FAR) for n in range(N_FAR)])  2.92 us
  transfers between devices with their start and end apart: 11, of which 5 were waited for; matrix products, arithmetic and copies ran while one was open for 1% of the time, Pallas kernels for 6%

profile of v2, /device:TPU:1, one launch (start us, length us, event | category | flops | bytes accessed | tf_op | source)
XLA Modules:
  0.0 93.7 jit_solution(12882920677867653881)
XLA Ops:
  0.6 1.2 %shard_map.101 = (bf16[2,3,6,4,512]{4,3,2,1,0:T(4,128)(2,1)S(1)}, bf16[2,3,6,4,512]{4,3,2,1,0:T(4,128)(2,1)S(1)}, bf16[2,3,6,4,512]{4,3,2,1,0:T(4,128)(2,1)S(1)}, bf16[2,3,6,4,512]{4,3,2,1,0:T(4,128)(2,1)S(1)}) custom-call(bf16[6,12,4,512]{3,2,1,0:T(4,128)(2,1)} %bitcast.12, bf16[6,12,4,512]{3,2,1,0:T(4,128)(2,1)} %bitcast.14), custom_call_target="tpu_custom_call" | custom-call | tf_op jit(solution)/shard_map/pallas_call | solution.py:343
  1.8 6.7 %collective-permute-start = (bf16[2,3,6,4,512]{4,3,2,1,0:T(4,128)(2,1)S(1)}, bf16[2,3,6,4,512]{4,3,2,1,0:T(4,128)(2,1)S(1)}, u32[]{:S(2)}, u32[]{:S(2)}) collective-permute-start(bf16[2,3,6,4,512]{4,3,2,1,0:T(4,128)(2,1)S(1)} %get-tuple-element.32), channel_id=1, source_target_pairs={{0,255},{1,248},{2,249},{3,250},{4,251},{5,252},{6,253},{7,254},{8... | collective-permute-start | bytes 442376 | tf_op jit(solution)/shard_map/ppermute | solution.py:330
  8.5 0.2 collective-permute-start.1
  8.7 5.4 %collective-permute-start.2 = (bf16[2,3,6,4,512]{4,3,2,1,0:T(4,128)(2,1)S(1)}, bf16[2,3,6,4,512]{4,3,2,1,0:T(4,128)(2,1)S(1)}, u32[]{:S(2)}, u32[]{:S(2)}) collective-permute-start(bf16[2,3,6,4,512]{4,3,2,1,0:T(4,128)(2,1)S(1)} %get-tuple-element.34), channel_id=1, source_target_pairs={{0,248},{1,249},{2,250},{3,251},{4,252},{5,253},{6,254},{7,255},{8... | collective-permute-start | bytes 442376 | tf_op jit(solution)/shard_map/ppermute | solution.py:330
  14.2 0.8 reshape.24
  15.0 0.3 copy.14
  15.2 0.1 eq.15
  15.4 1.5 %shard_map.102 = (bf16[512,1536]{1,0:T(8,128)(2,1)S(1)}, bf16[512,512]{1,0:T(8,128)(2,1)S(1)}, f32[1,512]{1,0:T(1,128)S(1)}) custom-call(bf16[512,1536]{1,0:T(8,128)(2,1)} %qkv_ref.1, bf16[512,512]{1,0:T(8,128)(2,1)} %proj_ref.1, f32[1,512]{1,0:T(1,128)} %bitcast.17), custom_call_target="tpu_custom_call" | custom-call | tf_op jit(solution)/shard_map/pallas_call | solution.py:357
  16.9 0.1 compare_select_fusion.bias_ref
  17.0 0.0 collective-permute-done.corner_ref
  17.0 0.0 collective-permute-done.1.right_ref
  17.1 0.0 collective-permute-done.2.below_ref
  17.1 4.3 %shard_map.103 = (bf16[4,256,512]{2,1,0:T(8,128)(2,1)S(1)}, bf16[2,512,288]{2,1,0:T(8,128)(2,1)S(1)}, bf16[4,288,512]{2,1,0:T(8,128)(2,1)S(1)}, bf16[288,512]{1,...) custom-call(bf16[2,3,6,4,512]{4,3,2,1,0:T(4,128)(2,1)S(1)} %collective-permute-done.corner_ref, ...), custom_call_target="tpu_custom_call" | custom-call | tf_op jit(solution)/shard_map/pallas_call | solution.py:365
  21.3 3.0 %collective-permute-start.4 = (bf16[4,256,512]{2,1,0:T(8,128)(2,1)S(1)}, bf16[4,256,512]{2,1,0:T(8,128)(2,1)S(1)}, u32[]{:S(2)}, u32[]{:S(2)}) collective-permute-start(bf16[4,256,512]{2,1,0:T(8,128)(2,1)S(1)} %get-tuple-element.47), channel_id=1, source_target_pairs={{0,8},{8,0},{1,9},{9,1},{2,10},{10,2},{3,11},{11,3},{4,12},{12,4},... | collective-permute-start | bytes 3145736 | tf_op jit(solution)/shard_map/ppermute | solution.py:334
  24.4 1.8 %shard_map.104 = (bf16[4,256,512]{2,1,0:T(8,128)(2,1)S(1)}, bf16[2,3,6,4,512]{4,3,2,1,0:T(4,128)(2,1)S(1)}, bf16[2,3,6,4,512]{4,3,2,1,0:T(4,128)(2,1)S(1)}, bf16[2,2,3,6,4,512]{5,4,3,2,1,0:T(4,128)(2,1)S(1)}) custom-call(bf16[2,512,288]{2,1,0:T(8,128)(2,1)S(1)} %get-tuple-element.39.left_ref, bf16[4,288,512]{2,1,0:T(8,128)(2,1)S(1)} %get-tuple-element.40.rows_ref, ...), custom_call_target="tpu_custom_call" | custom-call | tf_op jit(solution)/shard_map/pallas_call | solution.py:379
  26.1 0.5 collective-permute-done.4.got_ref
  26.7 0.4 shard_map.105
  27.0 12.5 %all_to_all.15.got_ref = bf16[4,256,512]{2,1,0:T(8,128)(2,1)S(1)} all-to-all(bf16[4,256,512]{2,1,0:T(8,128)(2,1)S(1)} %shard_map.105), channel_id=1, replica_groups={{0,128,1,129},{16,144,17,145},{32,160,33,161},{48,176,49,177},{64,192,6..., dimensions={0} | all-to-all | bytes 2097152 | tf_op jit(solution)/shard_map/all_to_all | solution.py:47
  39.5 0.8 shard_map.106
  40.3 3.4 %all-to-all-start.1 = ((bf16[8,32,512]{2,1,0:T(8,128)(2,1)}), bf16[8,32,512]{2,1,0:T(8,128)(2,1)S(1)}, u32[]{:S(2)}, u32[]{:S(2)}) async-start(bf16[8,32,512]{2,1,0:T(8,128)(2,1)} %shard_map.106), calls=%async_computation.1 | async-start | bytes 524288 | tf_op jit(solution)/shard_map/all_to_all | solution.py:47
  43.7 2.8 %collective-permute-start.3 = (bf16[2,2,3,6,4,512]{5,4,3,2,1,0:T(4,128)(2,1)S(1)}, bf16[2,2,3,6,4,512]{5,4,3,2,1,0:T(4,128)(2,1)S(1)}, u32[]{:S(2)}, u32[]{:S(2)}) collective-permute-start(bf16[2,2,3,6,4,512]{5,4,3,2,1,0:T(4,128)(2,1)S(1)} %get-tuple-element.45), channel_id=1, source_target_pairs={{0,8},{1,9},{2,10},{3,11},{4,12},{5,13},{6,14},{7,15},{8,16},{9,17... | collective-permute-start | bytes 884744 | tf_op jit(solution)/shard_map/ppermute | solution.py:330
  46.6 3.8 %collective-permute-done.3.lower_ref = bf16[2,2,3,6,4,512]{5,4,3,2,1,0:T(4,128)(2,1)S(1)} collective-permute-done((bf16[2,2,3,6,4,512]{5,4,3,2,1,0:T(4,128)(2,1)S(1)}, bf16[2,2,3,6,4,512]{5,4,3,2,1,0:T(4,128)(2,1)S(1)}, u32[]{:S(2)}, u32[]{:S(2)}) %collective-permute-start.3) | collective-permute-done | bytes 294944 | tf_op jit(solution)/shard_map/ppermute | solution.py:330
  50.4 0.9 all-to-all-done.1.got_ref
  51.3 0.1 shard_map.107
  51.3 1.2 %collective-permute-start.5 = (bf16[2,2,3,6,4,512]{5,4,3,2,1,0:T(4,128)(2,1)S(1)}, bf16[2,2,3,6,4,512]{5,4,3,2,1,0:T(4,128)(2,1)S(1)}, u32[]{:S(2)}, u32[]{:S(2)}) collective-permute-start(bf16[2,2,3,6,4,512]{5,4,3,2,1,0:T(4,128)(2,1)S(1)} %get-tuple-element.49), channel_id=1, source_target_pairs={{0,1},{1,2},{2,3},{3,4},{4,5},{5,6},{6,7},{7,0},{8,9},{9,10},{10,1... | collective-permute-start | bytes 884744 | tf_op jit(solution)/shard_map/ppermute | solution.py:330
  52.5 0.0 copy-start
  52.5 0.0 copy-start.1
  52.5 2.7 %collective-permute-start.8 = (bf16[32,512]{1,0:T(8,128)(2,1)S(1)}, bf16[32,512]{1,0:T(8,128)(2,1)S(1)}, u32[]{:S(2)}, u32[]{:S(2)}) collective-permute-start(bf16[32,512]{1,0:T(8,128)(2,1)S(1)} %get-tuple-element.52.own_ref), channel_id=1, source_target_pairs={{0,32},{32,64},{64,96},{96,0},{1,33},{33,65},{65,97},{97,1},{2,34}... | collective-permute-start | bytes 98312 | tf_op jit(solution)/shard_map/ppermute | solution.py:400
  55.2 5.6 %collective-permute-start.7 = (bf16[32,512]{1,0:T(8,128)(2,1)S(1)}, bf16[32,512]{1,0:T(8,128)(2,1)S(1)}, u32[]{:S(2)}, u32[]{:S(2)}) collective-permute-start(bf16[32,512]{1,0:T(8,128)(2,1)S(1)} %get-tuple-element.52.own_ref), channel_id=1, source_target_pairs={{0,64},{32,96},{64,0},{96,32},{1,65},{33,97},{65,1},{97,33},{2,66}... | collective-permute-start | bytes 98312 | tf_op jit(solution)/shard_map/ppermute | solution.py:400
  60.7 1.0 %collective-permute-start.6 = (bf16[32,512]{1,0:T(8,128)(2,1)S(1)}, bf16[32,512]{1,0:T(8,128)(2,1)S(1)}, u32[]{:S(2)}, u32[]{:S(2)}) collective-permute-start(bf16[32,512]{1,0:T(8,128)(2,1)S(1)} %get-tuple-element.52.own_ref), channel_id=1, source_target_pairs={{0,96},{32,0},{64,32},{96,64},{1,97},{33,1},{65,33},{97,65},{2,98}... | collective-permute-start | bytes 98312 | tf_op jit(solution)/shard_map/ppermute | solution.py:400
  61.8 0.0 collective-permute-done.8.three_ref
  61.8 0.9 collective-permute-done.7.two_ref
  62.7 2.0 %collective-permute-done.6.one_ref = bf16[32,512]{1,0:T(8,128)(2,1)S(1)} collective-permute-done((bf16[32,512]{1,0:T(8,128)(2,1)S(1)}, bf16[32,512]{1,0:T(8,128)(2,1)S(1)}, u32[]{:S(2)}, u32[]{:S(2)}) %collective-permute-start.6) | collective-permute-done | bytes 32800 | tf_op jit(solution)/shard_map/ppermute | solution.py:400
  64.7 0.0 collective-permute-done.5.side_ref
  64.7 0.1 shard_map.109
  64.8 19.7 %all_to_all.16 = bf16[32,32,512]{2,1,0:T(8,128)(2,1)S(1)} all-to-all(bf16[32,32,512]{2,1,0:T(8,128)(2,1)S(1)} %shard_map.109), channel_id=1, replica_groups={{0,16,2,18,4,20,6,22,128,144,130,146,132,148,134,150,1,17,3,19,5,21,7,2..., dimensions={0} | all-to-all | bytes 2097152 | tf_op jit(solution)/shard_map/all_to_all | solution.py:47
  84.5 4.9 %collective-permute-start.9 = (bf16[4,256,512]{2,1,0:T(8,128)(2,1)S(1)}, bf16[4,256,512]{2,1,0:T(8,128)(2,1)S(1)}, u32[]{:S(2)}, u32[]{:S(2)}) collective-permute-start(bf16[4,256,512]{2,1,0:T(8,128)(2,1)S(1)} %bitcast.10), channel_id=1, source_target_pairs={{0,8},{8,0},{1,9},{9,1},{2,10},{10,2},{3,11},{11,3},{4,12},{12,4},... | collective-permute-start | bytes 3145736 | tf_op jit(solution)/shard_map/ppermute | solution.py:334
  89.5 0.0 copy-done
  89.5 0.0 copy-done.1
  89.5 1.0 %shard_map.108 = (bf16[6,12,4,512]{3,2,1,0:T(4,128)(2,1)}, bf16[6,12,4,512]{3,2,1,0:T(4,128)(2,1)}) custom-call(bf16[6,12,4,512]{3,2,1,0:T(4,128)(2,1)S(1)} %bitcast.13, bf16[6,12,4,512]{3,2,1,0:T(4,128)(2,1)S(1)} %bitcast.15, bf16[2,3,6,4,512]{4,3,2,1,0:T(4,128)(2,1)S(1)} %get-tuple-element.44.own_ref, ...), custom_call_target="tpu_custom_call" | custom-call | tf_op jit(solution)/shard_map/pallas_call | solution.py:436
  90.4 1.6 %shard_map.110 = (f32[512,1536]{1,0:T(8,128)}, f32[512,512]{1,0:T(8,128)}, f32[1,512]{1,0:T(1,128)S(1)}) custom-call(bf16[4,256,512]{2,1,0:T(8,128)(2,1)S(1)} %bitcast.11, bf16[512,1536]{1,0:T(8,128)(2,1)S(1)} %get-tuple-element.37.qkv_ref, f32[1,512]{1,0:T(1,128)S(1)} %get-tuple-element.36.gain_ref), custom_call_target="tpu_custom_call" | custom-call | tf_op jit(solution)/shard_map/pallas_call | solution.py:414
  92.0 0.0 collective-permute-done.9.ref
  92.0 1.6 %shard_map.111 = (f32[512,1536]{1,0:T(8,128)}, f32[512,512]{1,0:T(8,128)}, f32[1,512]{1,0:T(1,128)}) custom-call(bf16[4,256,512]{2,1,0:T(8,128)(2,1)S(1)} %collective-permute-done.9.ref, bf16[512,1536]{1,0:T(8,128)(2,1)S(1)} %get-tuple-element.37.qkv_ref, f32[1,512]{1,0:T(1,128)S(1)} %get-tuple-element.36.gain_ref, ...), custom_call_target="tpu_custom_call", output_to_operand_aliasing={{0}: (3, {}), {1}: (4, {})} | custom-call | tf_op jit(solution)/shard_map/pallas_call | solution.py:422
Async XLA Ops:
  1.8 15.2 %collective-permute-start = (bf16[2,3,6,4,512]{4,3,2,1,0:T(4,128)(2,1)S(1)}, bf16[2,3,6,4,512]{4,3,2,1,0:T(4,128)(2,1)S(1)}, u32[]{:S(2)}, u32[]{:S(2)}) collective-permute-start(bf16[2,3,6,4,512]{4,3,2,1,0:T(4,128)(2,1)S(1)} %get-tuple-element.32), channel_id=1, source_target_pairs={{0,255},{1,248},{2,249},{3,250},{4,251},{5,252},{6,253},{7,254},{8... | collective-permute-start | bytes 442376 | tf_op jit(solution)/shard_map/ppermute | solution.py:330
  8.5 8.5 %collective-permute-start.1 = (bf16[2,3,6,4,512]{4,3,2,1,0:T(4,128)(2,1)S(1)}, bf16[2,3,6,4,512]{4,3,2,1,0:T(4,128)(2,1)S(1)}, u32[]{:S(2)}, u32[]{:S(2)}) collective-permute-start(bf16[2,3,6,4,512]{4,3,2,1,0:T(4,128)(2,1)S(1)} %get-tuple-element.33), channel_id=1, source_target_pairs={{0,7},{1,0},{2,1},{3,2},{4,3},{5,4},{6,5},{7,6},{8,15},{9,8},{10,9... | collective-permute-start | bytes 442376 | tf_op jit(solution)/shard_map/ppermute | solution.py:330
  8.7 8.3 %collective-permute-start.2 = (bf16[2,3,6,4,512]{4,3,2,1,0:T(4,128)(2,1)S(1)}, bf16[2,3,6,4,512]{4,3,2,1,0:T(4,128)(2,1)S(1)}, u32[]{:S(2)}, u32[]{:S(2)}) collective-permute-start(bf16[2,3,6,4,512]{4,3,2,1,0:T(4,128)(2,1)S(1)} %get-tuple-element.34), channel_id=1, source_target_pairs={{0,248},{1,249},{2,250},{3,251},{4,252},{5,253},{6,254},{7,255},{8... | collective-permute-start | bytes 442376 | tf_op jit(solution)/shard_map/ppermute | solution.py:330
  21.3 5.3 %collective-permute-start.4 = (bf16[4,256,512]{2,1,0:T(8,128)(2,1)S(1)}, bf16[4,256,512]{2,1,0:T(8,128)(2,1)S(1)}, u32[]{:S(2)}, u32[]{:S(2)}) collective-permute-start(bf16[4,256,512]{2,1,0:T(8,128)(2,1)S(1)} %get-tuple-element.47), channel_id=1, source_target_pairs={{0,8},{8,0},{1,9},{9,1},{2,10},{10,2},{3,11},{11,3},{4,12},{12,4},... | collective-permute-start | bytes 3145736 | tf_op jit(solution)/shard_map/ppermute | solution.py:334
  40.3 11.0 %all-to-all-start.1 = ((bf16[8,32,512]{2,1,0:T(8,128)(2,1)}), bf16[8,32,512]{2,1,0:T(8,128)(2,1)S(1)}, u32[]{:S(2)}, u32[]{:S(2)}) async-start(bf16[8,32,512]{2,1,0:T(8,128)(2,1)} %shard_map.106), calls=%async_computation.1 | async-start | bytes 524288 | tf_op jit(solution)/shard_map/all_to_all | solution.py:47
  43.7 6.7 %collective-permute-start.3 = (bf16[2,2,3,6,4,512]{5,4,3,2,1,0:T(4,128)(2,1)S(1)}, bf16[2,2,3,6,4,512]{5,4,3,2,1,0:T(4,128)(2,1)S(1)}, u32[]{:S(2)}, u32[]{:S(2)}) collective-permute-start(bf16[2,2,3,6,4,512]{5,4,3,2,1,0:T(4,128)(2,1)S(1)} %get-tuple-element.45), channel_id=1, source_target_pairs={{0,8},{1,9},{2,10},{3,11},{4,12},{5,13},{6,14},{7,15},{8,16},{9,17... | collective-permute-start | bytes 884744 | tf_op jit(solution)/shard_map/ppermute | solution.py:330
  51.3 13.4 %collective-permute-start.5 = (bf16[2,2,3,6,4,512]{5,4,3,2,1,0:T(4,128)(2,1)S(1)}, bf16[2,2,3,6,4,512]{5,4,3,2,1,0:T(4,128)(2,1)S(1)}, u32[]{:S(2)}, u32[]{:S(2)}) collective-permute-start(bf16[2,2,3,6,4,512]{5,4,3,2,1,0:T(4,128)(2,1)S(1)} %get-tuple-element.49), channel_id=1, source_target_pairs={{0,1},{1,2},{2,3},{3,4},{4,5},{5,6},{6,7},{7,0},{8,9},{9,10},{10,1... | collective-permute-start | bytes 884744 | tf_op jit(solution)/shard_map/ppermute | solution.py:330
  52.5 37.0 %copy-start = (bf16[4,6,12,512]{3,0,2,1:T(4,128)(2,1)S(1)}, bf16[4,6,12,512]{3,0,2,1:T(4,128)(2,1)}, u32[]{:S(2)}) copy-start(bf16[4,6,12,512]{3,0,2,1:T(4,128)(2,1)} %param.6) | copy-start | bytes 884740
  52.5 37.0 %copy-start.1 = (bf16[4,6,12,512]{3,0,2,1:T(4,128)(2,1)S(1)}, bf16[4,6,12,512]{3,0,2,1:T(4,128)(2,1)}, u32[]{:S(2)}) copy-start(bf16[4,6,12,512]{3,0,2,1:T(4,128)(2,1)} %param.7) | copy-start | bytes 884740
  52.5 9.3 %collective-permute-start.8 = (bf16[32,512]{1,0:T(8,128)(2,1)S(1)}, bf16[32,512]{1,0:T(8,128)(2,1)S(1)}, u32[]{:S(2)}, u32[]{:S(2)}) collective-permute-start(bf16[32,512]{1,0:T(8,128)(2,1)S(1)} %get-tuple-element.52.own_ref), channel_id=1, source_target_pairs={{0,32},{32,64},{64,96},{96,0},{1,33},{33,65},{65,97},{97,1},{2,34}... | collective-permute-start | bytes 98312 | tf_op jit(solution)/shard_map/ppermute | solution.py:400
  55.2 7.5 %collective-permute-start.7 = (bf16[32,512]{1,0:T(8,128)(2,1)S(1)}, bf16[32,512]{1,0:T(8,128)(2,1)S(1)}, u32[]{:S(2)}, u32[]{:S(2)}) collective-permute-start(bf16[32,512]{1,0:T(8,128)(2,1)S(1)} %get-tuple-element.52.own_ref), channel_id=1, source_target_pairs={{0,64},{32,96},{64,0},{96,32},{1,65},{33,97},{65,1},{97,33},{2,66}... | collective-permute-start | bytes 98312 | tf_op jit(solution)/shard_map/ppermute | solution.py:400
  60.7 4.0 %collective-permute-start.6 = (bf16[32,512]{1,0:T(8,128)(2,1)S(1)}, bf16[32,512]{1,0:T(8,128)(2,1)S(1)}, u32[]{:S(2)}, u32[]{:S(2)}) collective-permute-start(bf16[32,512]{1,0:T(8,128)(2,1)S(1)} %get-tuple-element.52.own_ref), channel_id=1, source_target_pairs={{0,96},{32,0},{64,32},{96,64},{1,97},{33,1},{65,33},{97,65},{2,98}... | collective-permute-start | bytes 98312 | tf_op jit(solution)/shard_map/ppermute | solution.py:400
  84.5 7.5 %collective-permute-start.9 = (bf16[4,256,512]{2,1,0:T(8,128)(2,1)S(1)}, bf16[4,256,512]{2,1,0:T(8,128)(2,1)S(1)}, u32[]{:S(2)}, u32[]{:S(2)}) collective-permute-start(bf16[4,256,512]{2,1,0:T(8,128)(2,1)S(1)} %bitcast.10), channel_id=1, source_target_pairs={{0,8},{8,0},{1,9},{9,1},{2,10},{10,2},{3,11},{11,3},{4,12},{12,4},... | collective-permute-start | bytes 3145736 | tf_op jit(solution)/shard_map/ppermute | solution.py:334

commit v3 on v2

--- a/solution.py
+++ b/solution.py
@@ -221,7 +221,8 @@
         copy.wait()
 
 
-def line_kernel(got_ref, out_ref):
+def line_kernel(got_ref, lower_ref, out_ref):
+    del lower_ref
     for n in range(8):
         rows = slice(n * CHUNK, (n + 1) * CHUNK)
         total = got_ref[0, rows].astype(F32)
@@ -390,9 +391,11 @@
         mib=4,
     )(keep, got)
     got = exchanged(half.reshape(4, 8 * CHUNK, D), LINES)
-    part = call(line_kernel, shaped((8, CHUNK, D), BF16), mib=6)(got)
+    lower_back = moved(lower_back, 1, 0)
+    part = call(
+        line_kernel, shaped((8, CHUNK, D), BF16), ins=[vmem, anywhere], out_specs=vmem, mib=6
+    )(got, lower_back)
     got = exchanged(part, SHEETS)
-    lower_back = moved(lower_back, 1, 0)
     part, side_back = call(
         sum_kernel, [shaped((CHUNK, D), BF16), pair], ins=[vmem] * 3, out_specs=[vmem] * 2, mib=6
     )(got, lower_back, right_back)

time: 94.1 us -> 92.7 us (0.985)
  waiting for transfers between devices: 8.15 us -> 13.4 us
  blocking collectives: 32.2 us -> 28.7 us
  starting transfers between devices: 37 us -> 33.8 us
    all_to_all x1, waiting for transfers between devices: 0.87 us -> 5.95 us  [exchanged(): return lax.all_to_all(parts, AXES, 0, 0, axis_index_groups=groups)]
    all_to_all x2, blocking collectives: 32.2 us -> 28.7 us  [exchanged(): return lax.all_to_all(parts, AXES, 0, 0, axis_index_groups=groups)]
    ppermute x5, starting transfers between devices: 16.3 us -> 13.3 us  [moved(): return lax.ppermute(block, AXES, route)]
where the time goes in v3:
time: 92.7 us; the launch traced here: 92.4 us
  starting transfers between devices  33.8 us (36%)
  blocking collectives  28.7 us (31%)
  Pallas kernels  14.2 us (15%)
  waiting for transfers between devices  13.4 us (14%)
  local copies, waits for them, and re-layouts  1.2 us (1%)
    all_to_all x2, blocking collectives, exchanged(): return lax.all_to_all(parts, AXES, 0, 0, axis_index_groups=groups)  28.7 us
    ppermute x5, starting transfers between devices, moved(): return lax.ppermute(block, AXES, route)  13.3 us
    ppermute x3, starting transfers between devices, on_device(): lax.ppermute(part, FAR, [(n, (n - step) % N_FAR) for n in range(N_FAR)])  9.46 us
    ppermute x2, starting transfers between devices, swapped(): return lax.ppermute(block, 'c', [(0, 1), (1, 0)])  7.49 us
    all_to_all x1, waiting for transfers between devices, exchanged(): return lax.all_to_all(parts, AXES, 0, 0, axis_index_groups=groups)  5.95 us
    pallas_call x1, Pallas kernels, on_device(): call(attend_kernel, [shaped((4, HALF_D, D), BF16), shaped((2, D, TOKENS),...  4.25 us
    ppermute x5, waiting for transfers between devices, moved(): return lax.ppermute(block, AXES, route)  3.67 us
    all_to_all x1, starting transfers between devices, exchanged(): return lax.all_to_all(parts, AXES, 0, 0, axis_index_groups=groups)  3.53 us
  transfers between devices with their start and end apart: 11, of which 5 were waited for; matrix products, arithmetic and copies ran while one was open for 1% of the time, Pallas kernels for 6%

profile of v3, /device:TPU:1, one launch (start us, length us, event | category | flops | bytes accessed | tf_op | source)
XLA Modules:
  0.0 92.4 jit_solution(67826950723801953)
XLA Ops:
  0.6 1.2 %shard_map.101 = (bf16[2,3,6,4,512]{4,3,2,1,0:T(4,128)(2,1)S(1)}, bf16[2,3,6,4,512]{4,3,2,1,0:T(4,128)(2,1)S(1)}, bf16[2,3,6,4,512]{4,3,2,1,0:T(4,128)(2,1)S(1)}, bf16[2,3,6,4,512]{4,3,2,1,0:T(4,128)(2,1)S(1)}) custom-call(bf16[6,12,4,512]{3,2,1,0:T(4,128)(2,1)} %bitcast.12, bf16[6,12,4,512]{3,2,1,0:T(4,128)(2,1)} %bitcast.14), custom_call_target="tpu_custom_call" | custom-call | tf_op jit(solution)/shard_map/pallas_call | solution.py:344
  1.8 6.7 %collective-permute-start = (bf16[2,3,6,4,512]{4,3,2,1,0:T(4,128)(2,1)S(1)}, bf16[2,3,6,4,512]{4,3,2,1,0:T(4,128)(2,1)S(1)}, u32[]{:S(2)}, u32[]{:S(2)}) collective-permute-start(bf16[2,3,6,4,512]{4,3,2,1,0:T(4,128)(2,1)S(1)} %get-tuple-element.32), channel_id=1, source_target_pairs={{0,255},{1,248},{2,249},{3,250},{4,251},{5,252},{6,253},{7,254},{8... | collective-permute-start | bytes 442376 | tf_op jit(solution)/shard_map/ppermute | solution.py:331
  8.5 0.2 collective-permute-start.1
  8.7 5.4 %collective-permute-start.2 = (bf16[2,3,6,4,512]{4,3,2,1,0:T(4,128)(2,1)S(1)}, bf16[2,3,6,4,512]{4,3,2,1,0:T(4,128)(2,1)S(1)}, u32[]{:S(2)}, u32[]{:S(2)}) collective-permute-start(bf16[2,3,6,4,512]{4,3,2,1,0:T(4,128)(2,1)S(1)} %get-tuple-element.34), channel_id=1, source_target_pairs={{0,248},{1,249},{2,250},{3,251},{4,252},{5,253},{6,254},{7,255},{8... | collective-permute-start | bytes 442376 | tf_op jit(solution)/shard_map/ppermute | solution.py:331
  14.2 0.8 reshape.24
  15.0 0.3 copy.14
  15.2 0.1 eq.15
  15.4 1.5 %shard_map.102 = (bf16[512,1536]{1,0:T(8,128)(2,1)S(1)}, bf16[512,512]{1,0:T(8,128)(2,1)S(1)}, f32[1,512]{1,0:T(1,128)S(1)}) custom-call(bf16[512,1536]{1,0:T(8,128)(2,1)} %qkv_ref.1, bf16[512,512]{1,0:T(8,128)(2,1)} %proj_ref.1, f32[1,512]{1,0:T(1,128)} %bitcast.17), custom_call_target="tpu_custom_call" | custom-call | tf_op jit(solution)/shard_map/pallas_call | solution.py:358
  16.9 0.1 compare_select_fusion.bias_ref
  17.0 0.0 collective-permute-done.corner_ref
  17.0 0.0 collective-permute-done.1.right_ref
  17.1 0.0 collective-permute-done.2.below_ref
  17.1 4.3 %shard_map.103 = (bf16[4,256,512]{2,1,0:T(8,128)(2,1)S(1)}, bf16[2,512,288]{2,1,0:T(8,128)(2,1)S(1)}, bf16[4,288,512]{2,1,0:T(8,128)(2,1)S(1)}, bf16[288,512]{1,...) custom-call(bf16[2,3,6,4,512]{4,3,2,1,0:T(4,128)(2,1)S(1)} %collective-permute-done.corner_ref, ...), custom_call_target="tpu_custom_call" | custom-call | tf_op jit(solution)/shard_map/pallas_call | solution.py:366
  21.3 3.0 %collective-permute-start.4 = (bf16[4,256,512]{2,1,0:T(8,128)(2,1)S(1)}, bf16[4,256,512]{2,1,0:T(8,128)(2,1)S(1)}, u32[]{:S(2)}, u32[]{:S(2)}) collective-permute-start(bf16[4,256,512]{2,1,0:T(8,128)(2,1)S(1)} %get-tuple-element.47), channel_id=1, source_target_pairs={{0,8},{8,0},{1,9},{9,1},{2,10},{10,2},{3,11},{11,3},{4,12},{12,4},... | collective-permute-start | bytes 3145736 | tf_op jit(solution)/shard_map/ppermute | solution.py:335
  24.4 1.8 %shard_map.104 = (bf16[4,256,512]{2,1,0:T(8,128)(2,1)S(1)}, bf16[2,3,6,4,512]{4,3,2,1,0:T(4,128)(2,1)S(1)}, bf16[2,3,6,4,512]{4,3,2,1,0:T(4,128)(2,1)S(1)}, bf16[2,2,3,6,4,512]{5,4,3,2,1,0:T(4,128)(2,1)S(1)}) custom-call(bf16[2,512,288]{2,1,0:T(8,128)(2,1)S(1)} %get-tuple-element.39.left_ref, bf16[4,288,512]{2,1,0:T(8,128)(2,1)S(1)} %get-tuple-element.40.rows_ref, ...), custom_call_target="tpu_custom_call" | custom-call | tf_op jit(solution)/shard_map/pallas_call | solution.py:380
  26.1 0.5 collective-permute-done.4.got_ref
  26.7 1.1 %shard_map.105 = bf16[4,256,512]{2,1,0:T(8,128)(2,1)} custom-call(bf16[4,256,512]{2,1,0:T(8,128)(2,1)S(1)} %get-tuple-element.46.keep_ref, bf16[4,256,512]{2,1,0:T(8,128)(2,1)S(1)} %collective-permute-done.4.got_ref), custom_call_target="tpu_custom_call" | custom-call | tf_op jit(solution)/shard_map/pallas_call | solution.py:385
  27.7 3.5 %all-to-all-start = ((bf16[4,256,512]{2,1,0:T(8,128)(2,1)}), bf16[4,256,512]{2,1,0:T(8,128)(2,1)S(1)}, u32[]{:S(2)}, u32[]{:S(2)}) async-start(bf16[4,256,512]{2,1,0:T(8,128)(2,1)} %shard_map.105), calls=%async_computation | async-start | bytes 2097152 | tf_op jit(solution)/shard_map/all_to_all | solution.py:47
  31.3 0.1 collective-permute-start.3
  31.3 3.7 %collective-permute-done.3.lower_ref = bf16[2,2,3,6,4,512]{5,4,3,2,1,0:T(4,128)(2,1)S(1)} collective-permute-done((bf16[2,2,3,6,4,512]{5,4,3,2,1,0:T(4,128)(2,1)S(1)}, bf16[2,2,3,6,4,512]{5,4,3,2,1,0:T(4,128)(2,1)S(1)}, u32[]{:S(2)}, u32[]{:S(2)}) %collective-permute-start.3) | collective-permute-done | bytes 294944 | tf_op jit(solution)/shard_map/ppermute | solution.py:331
  35.0 6.0 %all-to-all-done.got_ref = bf16[4,256,512]{2,1,0:T(8,128)(2,1)S(1)} async-done(((bf16[4,256,512]{2,1,0:T(8,128)(2,1)}), bf16[4,256,512]{2,1,0:T(8,128)(2,1)S(1)}, u32[]{:S(2)}, u32[]{:S(2)}) %all-to-all-start) | async-done | bytes 1048608 | tf_op jit(solution)/shard_map/all_to_all | solution.py:47
  41.0 0.1 shard_map.106
  41.1 8.5 %all_to_all.15.got_ref = bf16[8,32,512]{2,1,0:T(8,128)(2,1)S(1)} all-to-all(bf16[8,32,512]{2,1,0:T(8,128)(2,1)S(1)} %shard_map.106), channel_id=1, replica_groups={{0,16,2,18,4,20,6,22},{32,48,34,50,36,52,38,54},{64,80,66,82,68,84,70,8..., dimensions={0} | all-to-all | bytes 524288 | tf_op jit(solution)/shard_map/all_to_all | solution.py:47
  49.6 0.1 shard_map.107
  49.7 0.9 collective-permute-start.5
  50.6 0.0 copy-start
  50.6 0.0 copy-start.1
  50.6 2.9 %collective-permute-start.8 = (bf16[32,512]{1,0:T(8,128)(2,1)S(1)}, bf16[32,512]{1,0:T(8,128)(2,1)S(1)}, u32[]{:S(2)}, u32[]{:S(2)}) collective-permute-start(bf16[32,512]{1,0:T(8,128)(2,1)S(1)} %get-tuple-element.52.own_ref), channel_id=1, source_target_pairs={{0,32},{32,64},{64,96},{96,0},{1,33},{33,65},{65,97},{97,1},{2,34}... | collective-permute-start | bytes 98312 | tf_op jit(solution)/shard_map/ppermute | solution.py:403
  53.5 5.6 %collective-permute-start.7 = (bf16[32,512]{1,0:T(8,128)(2,1)S(1)}, bf16[32,512]{1,0:T(8,128)(2,1)S(1)}, u32[]{:S(2)}, u32[]{:S(2)}) collective-permute-start(bf16[32,512]{1,0:T(8,128)(2,1)S(1)} %get-tuple-element.52.own_ref), channel_id=1, source_target_pairs={{0,64},{32,96},{64,0},{96,32},{1,65},{33,97},{65,1},{97,33},{2,66}... | collective-permute-start | bytes 98312 | tf_op jit(solution)/shard_map/ppermute | solution.py:403
  59.0 1.0 %collective-permute-start.6 = (bf16[32,512]{1,0:T(8,128)(2,1)S(1)}, bf16[32,512]{1,0:T(8,128)(2,1)S(1)}, u32[]{:S(2)}, u32[]{:S(2)}) collective-permute-start(bf16[32,512]{1,0:T(8,128)(2,1)S(1)} %get-tuple-element.52.own_ref), channel_id=1, source_target_pairs={{0,96},{32,0},{64,32},{96,64},{1,97},{33,1},{65,33},{97,65},{2,98}... | collective-permute-start | bytes 98312 | tf_op jit(solution)/shard_map/ppermute | solution.py:403
  60.1 0.0 collective-permute-done.8.three_ref
  60.1 1.0 %collective-permute-done.7.two_ref = bf16[32,512]{1,0:T(8,128)(2,1)S(1)} collective-permute-done((bf16[32,512]{1,0:T(8,128)(2,1)S(1)}, bf16[32,512]{1,0:T(8,128)(2,1)S(1)}, u32[]{:S(2)}, u32[]{:S(2)}) %collective-permute-start.7) | collective-permute-done | bytes 32800 | tf_op jit(solution)/shard_map/ppermute | solution.py:403
  61.1 2.3 %collective-permute-done.6.one_ref = bf16[32,512]{1,0:T(8,128)(2,1)S(1)} collective-permute-done((bf16[32,512]{1,0:T(8,128)(2,1)S(1)}, bf16[32,512]{1,0:T(8,128)(2,1)S(1)}, u32[]{:S(2)}, u32[]{:S(2)}) %collective-permute-start.6) | collective-permute-done | bytes 32800 | tf_op jit(solution)/shard_map/ppermute | solution.py:403
  63.4 0.0 collective-permute-done.5.side_ref
  63.4 0.1 shard_map.109
  63.5 20.2 %all_to_all.16 = bf16[32,32,512]{2,1,0:T(8,128)(2,1)S(1)} all-to-all(bf16[32,32,512]{2,1,0:T(8,128)(2,1)S(1)} %shard_map.109), channel_id=1, replica_groups={{0,16,2,18,4,20,6,22,128,144,130,146,132,148,134,150,1,17,3,19,5,21,7,2..., dimensions={0} | all-to-all | bytes 2097152 | tf_op jit(solution)/shard_map/all_to_all | solution.py:47
  83.7 4.4 %collective-permute-start.9 = (bf16[4,256,512]{2,1,0:T(8,128)(2,1)S(1)}, bf16[4,256,512]{2,1,0:T(8,128)(2,1)S(1)}, u32[]{:S(2)}, u32[]{:S(2)}) collective-permute-start(bf16[4,256,512]{2,1,0:T(8,128)(2,1)S(1)} %bitcast.10), channel_id=1, source_target_pairs={{0,8},{8,0},{1,9},{9,1},{2,10},{10,2},{3,11},{11,3},{4,12},{12,4},... | collective-permute-start | bytes 3145736 | tf_op jit(solution)/shard_map/ppermute | solution.py:335
  88.1 0.0 copy-done
  88.1 0.0 copy-done.1
  88.1 1.0 %shard_map.108 = (bf16[6,12,4,512]{3,2,1,0:T(4,128)(2,1)}, bf16[6,12,4,512]{3,2,1,0:T(4,128)(2,1)}) custom-call(bf16[6,12,4,512]{3,2,1,0:T(4,128)(2,1)S(1)} %bitcast.13, bf16[6,12,4,512]{3,2,1,0:T(4,128)(2,1)S(1)} %bitcast.15, bf16[2,3,6,4,512]{4,3,2,1,0:T(4,128)(2,1)S(1)} %get-tuple-element.44.own_ref, ...), custom_call_target="tpu_custom_call" | custom-call | tf_op jit(solution)/shard_map/pallas_call | solution.py:439
  89.1 1.6 %shard_map.110 = (f32[512,1536]{1,0:T(8,128)}, f32[512,512]{1,0:T(8,128)}, f32[1,512]{1,0:T(1,128)S(1)}) custom-call(bf16[4,256,512]{2,1,0:T(8,128)(2,1)S(1)} %bitcast.11, bf16[512,1536]{1,0:T(8,128)(2,1)S(1)} %get-tuple-element.37.qkv_ref, f32[1,512]{1,0:T(1,128)S(1)} %get-tuple-element.36.gain_ref), custom_call_target="tpu_custom_call" | custom-call | tf_op jit(solution)/shard_map/pallas_call | solution.py:417
  90.6 0.0 collective-permute-done.9.ref
  90.7 1.6 %shard_map.111 = (f32[512,1536]{1,0:T(8,128)}, f32[512,512]{1,0:T(8,128)}, f32[1,512]{1,0:T(1,128)}) custom-call(bf16[4,256,512]{2,1,0:T(8,128)(2,1)S(1)} %collective-permute-done.9.ref, bf16[512,1536]{1,0:T(8,128)(2,1)S(1)} %get-tuple-element.37.qkv_ref, f32[1,512]{1,0:T(1,128)S(1)} %get-tuple-element.36.gain_ref, ...), custom_call_target="tpu_custom_call", output_to_operand_aliasing={{0}: (3, {}), {1}: (4, {})} | custom-call | tf_op jit(solution)/shard_map/pallas_call | solution.py:425
Async XLA Ops:
  1.8 15.2 %collective-permute-start = (bf16[2,3,6,4,512]{4,3,2,1,0:T(4,128)(2,1)S(1)}, bf16[2,3,6,4,512]{4,3,2,1,0:T(4,128)(2,1)S(1)}, u32[]{:S(2)}, u32[]{:S(2)}) collective-permute-start(bf16[2,3,6,4,512]{4,3,2,1,0:T(4,128)(2,1)S(1)} %get-tuple-element.32), channel_id=1, source_target_pairs={{0,255},{1,248},{2,249},{3,250},{4,251},{5,252},{6,253},{7,254},{8... | collective-permute-start | bytes 442376 | tf_op jit(solution)/shard_map/ppermute | solution.py:331
  8.5 8.5 %collective-permute-start.1 = (bf16[2,3,6,4,512]{4,3,2,1,0:T(4,128)(2,1)S(1)}, bf16[2,3,6,4,512]{4,3,2,1,0:T(4,128)(2,1)S(1)}, u32[]{:S(2)}, u32[]{:S(2)}) collective-permute-start(bf16[2,3,6,4,512]{4,3,2,1,0:T(4,128)(2,1)S(1)} %get-tuple-element.33), channel_id=1, source_target_pairs={{0,7},{1,0},{2,1},{3,2},{4,3},{5,4},{6,5},{7,6},{8,15},{9,8},{10,9... | collective-permute-start | bytes 442376 | tf_op jit(solution)/shard_map/ppermute | solution.py:331
  8.7 8.3 %collective-permute-start.2 = (bf16[2,3,6,4,512]{4,3,2,1,0:T(4,128)(2,1)S(1)}, bf16[2,3,6,4,512]{4,3,2,1,0:T(4,128)(2,1)S(1)}, u32[]{:S(2)}, u32[]{:S(2)}) collective-permute-start(bf16[2,3,6,4,512]{4,3,2,1,0:T(4,128)(2,1)S(1)} %get-tuple-element.34), channel_id=1, source_target_pairs={{0,248},{1,249},{2,250},{3,251},{4,252},{5,253},{6,254},{7,255},{8... | collective-permute-start | bytes 442376 | tf_op jit(solution)/shard_map/ppermute | solution.py:331
  21.3 5.3 %collective-permute-start.4 = (bf16[4,256,512]{2,1,0:T(8,128)(2,1)S(1)}, bf16[4,256,512]{2,1,0:T(8,128)(2,1)S(1)}, u32[]{:S(2)}, u32[]{:S(2)}) collective-permute-start(bf16[4,256,512]{2,1,0:T(8,128)(2,1)S(1)} %get-tuple-element.47), channel_id=1, source_target_pairs={{0,8},{8,0},{1,9},{9,1},{2,10},{10,2},{3,11},{11,3},{4,12},{12,4},... | collective-permute-start | bytes 3145736 | tf_op jit(solution)/shard_map/ppermute | solution.py:335
  27.7 13.2 %all-to-all-start = ((bf16[4,256,512]{2,1,0:T(8,128)(2,1)}), bf16[4,256,512]{2,1,0:T(8,128)(2,1)S(1)}, u32[]{:S(2)}, u32[]{:S(2)}) async-start(bf16[4,256,512]{2,1,0:T(8,128)(2,1)} %shard_map.105), calls=%async_computation | async-start | bytes 2097152 | tf_op jit(solution)/shard_map/all_to_all | solution.py:47
  31.3 3.8 %collective-permute-start.3 = (bf16[2,2,3,6,4,512]{5,4,3,2,1,0:T(4,128)(2,1)S(1)}, bf16[2,2,3,6,4,512]{5,4,3,2,1,0:T(4,128)(2,1)S(1)}, u32[]{:S(2)}, u32[]{:S(2)}) collective-permute-start(bf16[2,2,3,6,4,512]{5,4,3,2,1,0:T(4,128)(2,1)S(1)} %get-tuple-element.45), channel_id=1, source_target_pairs={{0,8},{1,9},{2,10},{3,11},{4,12},{5,13},{6,14},{7,15},{8,16},{9,17... | collective-permute-start | bytes 884744 | tf_op jit(solution)/shard_map/ppermute | solution.py:331
  49.7 13.7 %collective-permute-start.5 = (bf16[2,2,3,6,4,512]{5,4,3,2,1,0:T(4,128)(2,1)S(1)}, bf16[2,2,3,6,4,512]{5,4,3,2,1,0:T(4,128)(2,1)S(1)}, u32[]{:S(2)}, u32[]{:S(2)}) collective-permute-start(bf16[2,2,3,6,4,512]{5,4,3,2,1,0:T(4,128)(2,1)S(1)} %get-tuple-element.49), channel_id=1, source_target_pairs={{0,1},{1,2},{2,3},{3,4},{4,5},{5,6},{6,7},{7,0},{8,9},{9,10},{10,1... | collective-permute-start | bytes 884744 | tf_op jit(solution)/shard_map/ppermute | solution.py:331
  50.6 37.5 %copy-start = (bf16[4,6,12,512]{3,0,2,1:T(4,128)(2,1)S(1)}, bf16[4,6,12,512]{3,0,2,1:T(4,128)(2,1)}, u32[]{:S(2)}) copy-start(bf16[4,6,12,512]{3,0,2,1:T(4,128)(2,1)} %param.6) | copy-start | bytes 884740
  50.6 37.5 %copy-start.1 = (bf16[4,6,12,512]{3,0,2,1:T(4,128)(2,1)S(1)}, bf16[4,6,12,512]{3,0,2,1:T(4,128)(2,1)}, u32[]{:S(2)}) copy-start(bf16[4,6,12,512]{3,0,2,1:T(4,128)(2,1)} %param.7) | copy-start | bytes 884740
  50.6 9.5 %collective-permute-start.8 = (bf16[32,512]{1,0:T(8,128)(2,1)S(1)}, bf16[32,512]{1,0:T(8,128)(2,1)S(1)}, u32[]{:S(2)}, u32[]{:S(2)}) collective-permute-start(bf16[32,512]{1,0:T(8,128)(2,1)S(1)} %get-tuple-element.52.own_ref), channel_id=1, source_target_pairs={{0,32},{32,64},{64,96},{96,0},{1,33},{33,65},{65,97},{97,1},{2,34}... | collective-permute-start | bytes 98312 | tf_op jit(solution)/shard_map/ppermute | solution.py:403
  53.5 7.6 %collective-permute-start.7 = (bf16[32,512]{1,0:T(8,128)(2,1)S(1)}, bf16[32,512]{1,0:T(8,128)(2,1)S(1)}, u32[]{:S(2)}, u32[]{:S(2)}) collective-permute-start(bf16[32,512]{1,0:T(8,128)(2,1)S(1)} %get-tuple-element.52.own_ref), channel_id=1, source_target_pairs={{0,64},{32,96},{64,0},{96,32},{1,65},{33,97},{65,1},{97,33},{2,66}... | collective-permute-start | bytes 98312 | tf_op jit(solution)/shard_map/ppermute | solution.py:403
  59.0 4.3 %collective-permute-start.6 = (bf16[32,512]{1,0:T(8,128)(2,1)S(1)}, bf16[32,512]{1,0:T(8,128)(2,1)S(1)}, u32[]{:S(2)}, u32[]{:S(2)}) collective-permute-start(bf16[32,512]{1,0:T(8,128)(2,1)S(1)} %get-tuple-element.52.own_ref), channel_id=1, source_target_pairs={{0,96},{32,0},{64,32},{96,64},{1,97},{33,1},{65,33},{97,65},{2,98}... | collective-permute-start | bytes 98312 | tf_op jit(solution)/shard_map/ppermute | solution.py:403
  83.7 7.0 %collective-permute-start.9 = (bf16[4,256,512]{2,1,0:T(8,128)(2,1)S(1)}, bf16[4,256,512]{2,1,0:T(8,128)(2,1)S(1)}, u32[]{:S(2)}, u32[]{:S(2)}) collective-permute-start(bf16[4,256,512]{2,1,0:T(8,128)(2,1)S(1)} %bitcast.10), channel_id=1, source_target_pairs={{0,8},{8,0},{1,9},{9,1},{2,10},{10,2},{3,11},{11,3},{4,12},{12,4},... | collective-permute-start | bytes 3145736 | tf_op jit(solution)/shard_map/ppermute | solution.py:335

commit v4 on v3

--- a/solution.py
+++ b/solution.py
@@ -40,7 +40,7 @@
 SHEETS = [[spot(x, y, 2 * f + z, 0) for y in FOUR for z in TWO] for x in FOUR for f in FOUR]
 SHEETS += [[spot(x, y, 2 * f + z, 1) for x in FOUR for z in TWO] for y in FOUR for f in FOUR]
 NEAR = [[spot(x, y, 2 * f + z, 0) for x in FOUR for y in FOUR for z in TWO] for f in FOUR]
-NEAR += [[spot(x, y, 2 * f + z, 1) for y in FOUR for x in FOUR for z in TWO] for f in FOUR]
+NEAR += [[spot(x, y, 2 * f + z, 1) for x in FOUR for y in FOUR for z in TWO] for f in FOUR]
 
 
 def exchanged(parts, groups):
@@ -211,12 +211,15 @@
 
 
 def add_kernel(keep_ref, got_ref, out_ref, held, sems):
+    core = lax.axis_index("c")
     copies = []
-    for block in range(4):
-        held[block] = (keep_ref[block].astype(F32) + got_ref[block].astype(F32)).astype(BF16)
-        copy = pltpu.make_async_copy(held.at[block], out_ref.at[block], sems.at[block])
-        copy.start()
-        copies.append(copy)
+    for x in range(4):
+        held[x] = (keep_ref[x].astype(F32) + got_ref[x].astype(F32)).astype(BF16)
+        for y in range(4):
+            place = (4 * x + y) * (1 - core) + (4 * y + x) * core
+            group = held.at[x, pl.ds(y * 2 * CHUNK, 2 * CHUNK)]
+            copies.append(pltpu.make_async_copy(group, out_ref.at[place], sems.at[4 * x + y]))
+            copies[-1].start()
     for copy in copies:
         copy.wait()
 
@@ -384,8 +387,8 @@
     )(*state, gain, qkv_weight, proj_weight)
     half = call(
         add_kernel,
-        shaped((4, HALF_D, D), BF16),
-        [pltpu.VMEM((4, HALF_D, D), BF16), pltpu.SemaphoreType.DMA((4,))],
+        shaped((16, 2 * CHUNK, D), BF16),
+        [pltpu.VMEM((4, HALF_D, D), BF16), pltpu.SemaphoreType.DMA((16,))],
         [vmem] * 2,
         anywhere,
         mib=4,

time: 92.7 us -> 92.8 us (level)
  no operation moved by 1% of the time
where the time goes in v4:
time: 92.8 us; the launch traced here: 92.4 us
  starting transfers between devices  33 us (36%)
  blocking collectives  29.5 us (32%)
  Pallas kernels  14.3 us (15%)
  waiting for transfers between devices  13.4 us (14%)
  local copies, waits for them, and re-layouts  1.2 us (1%)
    all_to_all x2, blocking collectives, exchanged(): return lax.all_to_all(parts, AXES, 0, 0, axis_index_groups=groups)  29.5 us
    ppermute x5, starting transfers between devices, moved(): return lax.ppermute(block, AXES, route)  13.3 us
    ppermute x3, starting transfers between devices, on_device(): lax.ppermute(part, FAR, [(n, (n - step) % N_FAR) for n in range(N_FAR)])  9.46 us
    ppermute x2, starting transfers between devices, swapped(): return lax.ppermute(block, 'c', [(0, 1), (1, 0)])  6.66 us
    all_to_all x1, waiting for transfers between devices, exchanged(): return lax.all_to_all(parts, AXES, 0, 0, axis_index_groups=groups)  5.95 us
    pallas_call x1, Pallas kernels, on_device(): call(attend_kernel, [shaped((4, HALF_D, D), BF16), shaped((2, D, TOKENS),...  4.25 us
    ppermute x5, waiting for transfers between devices, moved(): return lax.ppermute(block, AXES, route)  3.67 us
    all_to_all x1, starting transfers between devices, exchanged(): return lax.all_to_all(parts, AXES, 0, 0, axis_index_groups=groups)  3.53 us
  transfers between devices with their start and end apart: 11, of which 5 were waited for; matrix products, arithmetic and copies ran while one was open for 1% of the time, Pallas kernels for 6%

profile of v4, /device:TPU:1, one launch (start us, length us, event | category | flops | bytes accessed | tf_op | source)
XLA Modules:
  0.0 92.4 jit_solution(5372305913094319178)
XLA Ops:
  0.6 1.2 %shard_map.101 = (bf16[2,3,6,4,512]{4,3,2,1,0:T(4,128)(2,1)S(1)}, bf16[2,3,6,4,512]{4,3,2,1,0:T(4,128)(2,1)S(1)}, bf16[2,3,6,4,512]{4,3,2,1,0:T(4,128)(2,1)S(1)}, bf16[2,3,6,4,512]{4,3,2,1,0:T(4,128)(2,1)S(1)}) custom-call(bf16[6,12,4,512]{3,2,1,0:T(4,128)(2,1)} %bitcast.13, bf16[6,12,4,512]{3,2,1,0:T(4,128)(2,1)} %bitcast.15), custom_call_target="tpu_custom_call" | custom-call | tf_op jit(solution)/shard_map/pallas_call | solution.py:347
  1.8 6.7 %collective-permute-start = (bf16[2,3,6,4,512]{4,3,2,1,0:T(4,128)(2,1)S(1)}, bf16[2,3,6,4,512]{4,3,2,1,0:T(4,128)(2,1)S(1)}, u32[]{:S(2)}, u32[]{:S(2)}) collective-permute-start(bf16[2,3,6,4,512]{4,3,2,1,0:T(4,128)(2,1)S(1)} %get-tuple-element.32), channel_id=1, source_target_pairs={{0,255},{1,248},{2,249},{3,250},{4,251},{5,252},{6,253},{7,254},{8... | collective-permute-start | bytes 442376 | tf_op jit(solution)/shard_map/ppermute | solution.py:334
  8.5 0.2 collective-permute-start.1
  8.7 5.4 %collective-permute-start.2 = (bf16[2,3,6,4,512]{4,3,2,1,0:T(4,128)(2,1)S(1)}, bf16[2,3,6,4,512]{4,3,2,1,0:T(4,128)(2,1)S(1)}, u32[]{:S(2)}, u32[]{:S(2)}) collective-permute-start(bf16[2,3,6,4,512]{4,3,2,1,0:T(4,128)(2,1)S(1)} %get-tuple-element.34), channel_id=1, source_target_pairs={{0,248},{1,249},{2,250},{3,251},{4,252},{5,253},{6,254},{7,255},{8... | collective-permute-start | bytes 442376 | tf_op jit(solution)/shard_map/ppermute | solution.py:334
  14.2 0.8 reshape.27
  15.0 0.3 copy.14
  15.2 0.1 eq.15
  15.4 1.5 %shard_map.102 = (bf16[512,1536]{1,0:T(8,128)(2,1)S(1)}, bf16[512,512]{1,0:T(8,128)(2,1)S(1)}, f32[1,512]{1,0:T(1,128)S(1)}) custom-call(bf16[512,1536]{1,0:T(8,128)(2,1)} %qkv_ref.1, bf16[512,512]{1,0:T(8,128)(2,1)} %proj_ref.1, f32[1,512]{1,0:T(1,128)} %bitcast.18), custom_call_target="tpu_custom_call" | custom-call | tf_op jit(solution)/shard_map/pallas_call | solution.py:361
  16.9 0.1 compare_select_fusion.bias_ref
  17.0 0.0 collective-permute-done.corner_ref
  17.0 0.0 collective-permute-done.1.right_ref
  17.1 0.0 collective-permute-done.2.below_ref
  17.1 4.3 %shard_map.103 = (bf16[4,256,512]{2,1,0:T(8,128)(2,1)S(1)}, bf16[2,512,288]{2,1,0:T(8,128)(2,1)S(1)}, bf16[4,288,512]{2,1,0:T(8,128)(2,1)S(1)}, bf16[288,512]{1,...) custom-call(bf16[2,3,6,4,512]{4,3,2,1,0:T(4,128)(2,1)S(1)} %collective-permute-done.corner_ref, ...), custom_call_target="tpu_custom_call" | custom-call | tf_op jit(solution)/shard_map/pallas_call | solution.py:369
  21.3 3.0 %collective-permute-start.4 = (bf16[4,256,512]{2,1,0:T(8,128)(2,1)S(1)}, bf16[4,256,512]{2,1,0:T(8,128)(2,1)S(1)}, u32[]{:S(2)}, u32[]{:S(2)}) collective-permute-start(bf16[4,256,512]{2,1,0:T(8,128)(2,1)S(1)} %get-tuple-element.47), channel_id=1, source_target_pairs={{0,8},{8,0},{1,9},{9,1},{2,10},{10,2},{3,11},{11,3},{4,12},{12,4},... | collective-permute-start | bytes 3145736 | tf_op jit(solution)/shard_map/ppermute | solution.py:338
  24.4 1.8 %shard_map.104 = (bf16[4,256,512]{2,1,0:T(8,128)(2,1)S(1)}, bf16[2,3,6,4,512]{4,3,2,1,0:T(4,128)(2,1)S(1)}, bf16[2,3,6,4,512]{4,3,2,1,0:T(4,128)(2,1)S(1)}, bf16[2,2,3,6,4,512]{5,4,3,2,1,0:T(4,128)(2,1)S(1)}) custom-call(bf16[2,512,288]{2,1,0:T(8,128)(2,1)S(1)} %get-tuple-element.39.left_ref, bf16[4,288,512]{2,1,0:T(8,128)(2,1)S(1)} %get-tuple-element.40.rows_ref, ...), custom_call_target="tpu_custom_call" | custom-call | tf_op jit(solution)/shard_map/pallas_call | solution.py:383
  26.1 0.5 collective-permute-done.4.got_ref
  26.7 1.1 %shard_map.105 = bf16[16,64,512]{2,1,0:T(8,128)(2,1)} custom-call(bf16[4,256,512]{2,1,0:T(8,128)(2,1)S(1)} %get-tuple-element.46.keep_ref, bf16[4,256,512]{2,1,0:T(8,128)(2,1)S(1)} %collective-permute-done.4.got_ref), custom_call_target="tpu_custom_call" | custom-call | tf_op jit(solution)/shard_map/pallas_call | solution.py:388
  27.8 3.5 %all-to-all-start = ((bf16[4,256,512]{2,1,0:T(8,128)(2,1)}), bf16[4,256,512]{2,1,0:T(8,128)(2,1)S(1)}, u32[]{:S(2)}, u32[]{:S(2)}) async-start(bf16[4,256,512]{2,1,0:T(8,128)(2,1)} %bitcast.4), calls=%async_computation | async-start | bytes 2097152 | tf_op jit(solution)/shard_map/all_to_all | solution.py:47
  31.3 0.1 collective-permute-start.3
  31.4 3.7 %collective-permute-done.3.lower_ref = bf16[2,2,3,6,4,512]{5,4,3,2,1,0:T(4,128)(2,1)S(1)} collective-permute-done((bf16[2,2,3,6,4,512]{5,4,3,2,1,0:T(4,128)(2,1)S(1)}, bf16[2,2,3,6,4,512]{5,4,3,2,1,0:T(4,128)(2,1)S(1)}, u32[]{:S(2)}, u32[]{:S(2)}) %collective-permute-start.3) | collective-permute-done | bytes 294944 | tf_op jit(solution)/shard_map/ppermute | solution.py:334
  35.1 6.0 %all-to-all-done.got_ref = bf16[4,256,512]{2,1,0:T(8,128)(2,1)S(1)} async-done(((bf16[4,256,512]{2,1,0:T(8,128)(2,1)}), bf16[4,256,512]{2,1,0:T(8,128)(2,1)S(1)}, u32[]{:S(2)}, u32[]{:S(2)}) %all-to-all-start) | async-done | bytes 1048608 | tf_op jit(solution)/shard_map/all_to_all | solution.py:47
  41.1 0.1 shard_map.106
  41.2 8.5 %all_to_all.15.got_ref = bf16[8,32,512]{2,1,0:T(8,128)(2,1)S(1)} all-to-all(bf16[8,32,512]{2,1,0:T(8,128)(2,1)S(1)} %shard_map.106), channel_id=1, replica_groups={{0,16,2,18,4,20,6,22},{32,48,34,50,36,52,38,54},{64,80,66,82,68,84,70,8..., dimensions={0} | all-to-all | bytes 524288 | tf_op jit(solution)/shard_map/all_to_all | solution.py:47
  49.7 0.1 shard_map.107
  49.8 0.9 collective-permute-start.5
  50.7 0.0 copy-start
  50.7 0.0 copy-start.1
  50.7 2.9 %collective-permute-start.8 = (bf16[32,512]{1,0:T(8,128)(2,1)S(1)}, bf16[32,512]{1,0:T(8,128)(2,1)S(1)}, u32[]{:S(2)}, u32[]{:S(2)}) collective-permute-start(bf16[32,512]{1,0:T(8,128)(2,1)S(1)} %get-tuple-element.52.own_ref), channel_id=1, source_target_pairs={{0,32},{32,64},{64,96},{96,0},{1,33},{33,65},{65,97},{97,1},{2,34}... | collective-permute-start | bytes 98312 | tf_op jit(solution)/shard_map/ppermute | solution.py:406
  53.6 5.6 %collective-permute-start.7 = (bf16[32,512]{1,0:T(8,128)(2,1)S(1)}, bf16[32,512]{1,0:T(8,128)(2,1)S(1)}, u32[]{:S(2)}, u32[]{:S(2)}) collective-permute-start(bf16[32,512]{1,0:T(8,128)(2,1)S(1)} %get-tuple-element.52.own_ref), channel_id=1, source_target_pairs={{0,64},{32,96},{64,0},{96,32},{1,65},{33,97},{65,1},{97,33},{2,66}... | collective-permute-start | bytes 98312 | tf_op jit(solution)/shard_map/ppermute | solution.py:406
  59.1 1.0 %collective-permute-start.6 = (bf16[32,512]{1,0:T(8,128)(2,1)S(1)}, bf16[32,512]{1,0:T(8,128)(2,1)S(1)}, u32[]{:S(2)}, u32[]{:S(2)}) collective-permute-start(bf16[32,512]{1,0:T(8,128)(2,1)S(1)} %get-tuple-element.52.own_ref), channel_id=1, source_target_pairs={{0,96},{32,0},{64,32},{96,64},{1,97},{33,1},{65,33},{97,65},{2,98}... | collective-permute-start | bytes 98312 | tf_op jit(solution)/shard_map/ppermute | solution.py:406
  60.2 0.0 collective-permute-done.8.three_ref
  60.2 1.0 %collective-permute-done.7.two_ref = bf16[32,512]{1,0:T(8,128)(2,1)S(1)} collective-permute-done((bf16[32,512]{1,0:T(8,128)(2,1)S(1)}, bf16[32,512]{1,0:T(8,128)(2,1)S(1)}, u32[]{:S(2)}, u32[]{:S(2)}) %collective-permute-start.7) | collective-permute-done | bytes 32800 | tf_op jit(solution)/shard_map/ppermute | solution.py:406
  61.2 2.3 %collective-permute-done.6.one_ref = bf16[32,512]{1,0:T(8,128)(2,1)S(1)} collective-permute-done((bf16[32,512]{1,0:T(8,128)(2,1)S(1)}, bf16[32,512]{1,0:T(8,128)(2,1)S(1)}, u32[]{:S(2)}, u32[]{:S(2)}) %collective-permute-start.6) | collective-permute-done | bytes 32800 | tf_op jit(solution)/shard_map/ppermute | solution.py:406
  63.4 0.0 collective-permute-done.5.side_ref
  63.5 0.1 shard_map.109
  63.6 20.9 %all_to_all.16 = bf16[32,32,512]{2,1,0:T(8,128)(2,1)S(1)} all-to-all(bf16[32,32,512]{2,1,0:T(8,128)(2,1)S(1)} %shard_map.109), channel_id=1, replica_groups={{0,16,2,18,4,20,6,22,128,144,130,146,132,148,134,150,1,17,3,19,5,21,7,2..., dimensions={0} | all-to-all | bytes 2097152 | tf_op jit(solution)/shard_map/all_to_all | solution.py:47
  84.5 3.6 %collective-permute-start.9 = (bf16[4,256,512]{2,1,0:T(8,128)(2,1)S(1)}, bf16[4,256,512]{2,1,0:T(8,128)(2,1)S(1)}, u32[]{:S(2)}, u32[]{:S(2)}) collective-permute-start(bf16[4,256,512]{2,1,0:T(8,128)(2,1)S(1)} %bitcast.11), channel_id=1, source_target_pairs={{0,8},{8,0},{1,9},{9,1},{2,10},{10,2},{3,11},{11,3},{4,12},{12,4},... | collective-permute-start | bytes 3145736 | tf_op jit(solution)/shard_map/ppermute | solution.py:338
  88.1 0.0 copy-done
  88.1 0.0 copy-done.1
  88.1 1.0 %shard_map.108 = (bf16[6,12,4,512]{3,2,1,0:T(4,128)(2,1)}, bf16[6,12,4,512]{3,2,1,0:T(4,128)(2,1)}) custom-call(bf16[6,12,4,512]{3,2,1,0:T(4,128)(2,1)S(1)} %bitcast.14, bf16[6,12,4,512]{3,2,1,0:T(4,128)(2,1)S(1)} %bitcast.16, bf16[2,3,6,4,512]{4,3,2,1,0:T(4,128)(2,1)S(1)} %get-tuple-element.44.own_ref, ...), custom_call_target="tpu_custom_call" | custom-call | tf_op jit(solution)/shard_map/pallas_call | solution.py:442
  89.1 1.6 %shard_map.110 = (f32[512,1536]{1,0:T(8,128)}, f32[512,512]{1,0:T(8,128)}, f32[1,512]{1,0:T(1,128)S(1)}) custom-call(bf16[4,256,512]{2,1,0:T(8,128)(2,1)S(1)} %bitcast.12, bf16[512,1536]{1,0:T(8,128)(2,1)S(1)} %get-tuple-element.37.qkv_ref, f32[1,512]{1,0:T(1,128)S(1)} %get-tuple-element.36.gain_ref), custom_call_target="tpu_custom_call" | custom-call | tf_op jit(solution)/shard_map/pallas_call | solution.py:420
  90.7 0.0 collective-permute-done.9.ref
  90.7 1.6 %shard_map.111 = (f32[512,1536]{1,0:T(8,128)}, f32[512,512]{1,0:T(8,128)}, f32[1,512]{1,0:T(1,128)}) custom-call(bf16[4,256,512]{2,1,0:T(8,128)(2,1)S(1)} %collective-permute-done.9.ref, bf16[512,1536]{1,0:T(8,128)(2,1)S(1)} %get-tuple-element.37.qkv_ref, f32[1,512]{1,0:T(1,128)S(1)} %get-tuple-element.36.gain_ref, ...), custom_call_target="tpu_custom_call", output_to_operand_aliasing={{0}: (3, {}), {1}: (4, {})} | custom-call | tf_op jit(solution)/shard_map/pallas_call | solution.py:428
Async XLA Ops:
  1.8 15.2 %collective-permute-start = (bf16[2,3,6,4,512]{4,3,2,1,0:T(4,128)(2,1)S(1)}, bf16[2,3,6,4,512]{4,3,2,1,0:T(4,128)(2,1)S(1)}, u32[]{:S(2)}, u32[]{:S(2)}) collective-permute-start(bf16[2,3,6,4,512]{4,3,2,1,0:T(4,128)(2,1)S(1)} %get-tuple-element.32), channel_id=1, source_target_pairs={{0,255},{1,248},{2,249},{3,250},{4,251},{5,252},{6,253},{7,254},{8... | collective-permute-start | bytes 442376 | tf_op jit(solution)/shard_map/ppermute | solution.py:334
  8.5 8.5 %collective-permute-start.1 = (bf16[2,3,6,4,512]{4,3,2,1,0:T(4,128)(2,1)S(1)}, bf16[2,3,6,4,512]{4,3,2,1,0:T(4,128)(2,1)S(1)}, u32[]{:S(2)}, u32[]{:S(2)}) collective-permute-start(bf16[2,3,6,4,512]{4,3,2,1,0:T(4,128)(2,1)S(1)} %get-tuple-element.33), channel_id=1, source_target_pairs={{0,7},{1,0},{2,1},{3,2},{4,3},{5,4},{6,5},{7,6},{8,15},{9,8},{10,9... | collective-permute-start | bytes 442376 | tf_op jit(solution)/shard_map/ppermute | solution.py:334
  8.7 8.3 %collective-permute-start.2 = (bf16[2,3,6,4,512]{4,3,2,1,0:T(4,128)(2,1)S(1)}, bf16[2,3,6,4,512]{4,3,2,1,0:T(4,128)(2,1)S(1)}, u32[]{:S(2)}, u32[]{:S(2)}) collective-permute-start(bf16[2,3,6,4,512]{4,3,2,1,0:T(4,128)(2,1)S(1)} %get-tuple-element.34), channel_id=1, source_target_pairs={{0,248},{1,249},{2,250},{3,251},{4,252},{5,253},{6,254},{7,255},{8... | collective-permute-start | bytes 442376 | tf_op jit(solution)/shard_map/ppermute | solution.py:334
  21.3 5.3 %collective-permute-start.4 = (bf16[4,256,512]{2,1,0:T(8,128)(2,1)S(1)}, bf16[4,256,512]{2,1,0:T(8,128)(2,1)S(1)}, u32[]{:S(2)}, u32[]{:S(2)}) collective-permute-start(bf16[4,256,512]{2,1,0:T(8,128)(2,1)S(1)} %get-tuple-element.47), channel_id=1, source_target_pairs={{0,8},{8,0},{1,9},{9,1},{2,10},{10,2},{3,11},{11,3},{4,12},{12,4},... | collective-permute-start | bytes 3145736 | tf_op jit(solution)/shard_map/ppermute | solution.py:338
  27.8 13.2 %all-to-all-start = ((bf16[4,256,512]{2,1,0:T(8,128)(2,1)}), bf16[4,256,512]{2,1,0:T(8,128)(2,1)S(1)}, u32[]{:S(2)}, u32[]{:S(2)}) async-start(bf16[4,256,512]{2,1,0:T(8,128)(2,1)} %bitcast.4), calls=%async_computation | async-start | bytes 2097152 | tf_op jit(solution)/shard_map/all_to_all | solution.py:47
  31.3 3.8 %collective-permute-start.3 = (bf16[2,2,3,6,4,512]{5,4,3,2,1,0:T(4,128)(2,1)S(1)}, bf16[2,2,3,6,4,512]{5,4,3,2,1,0:T(4,128)(2,1)S(1)}, u32[]{:S(2)}, u32[]{:S(2)}) collective-permute-start(bf16[2,2,3,6,4,512]{5,4,3,2,1,0:T(4,128)(2,1)S(1)} %get-tuple-element.45), channel_id=1, source_target_pairs={{0,8},{1,9},{2,10},{3,11},{4,12},{5,13},{6,14},{7,15},{8,16},{9,17... | collective-permute-start | bytes 884744 | tf_op jit(solution)/shard_map/ppermute | solution.py:334
  49.8 13.7 %collective-permute-start.5 = (bf16[2,2,3,6,4,512]{5,4,3,2,1,0:T(4,128)(2,1)S(1)}, bf16[2,2,3,6,4,512]{5,4,3,2,1,0:T(4,128)(2,1)S(1)}, u32[]{:S(2)}, u32[]{:S(2)}) collective-permute-start(bf16[2,2,3,6,4,512]{5,4,3,2,1,0:T(4,128)(2,1)S(1)} %get-tuple-element.49), channel_id=1, source_target_pairs={{0,1},{1,2},{2,3},{3,4},{4,5},{5,6},{6,7},{7,0},{8,9},{9,10},{10,1... | collective-permute-start | bytes 884744 | tf_op jit(solution)/shard_map/ppermute | solution.py:334
  50.7 37.4 %copy-start = (bf16[4,6,12,512]{3,0,2,1:T(4,128)(2,1)S(1)}, bf16[4,6,12,512]{3,0,2,1:T(4,128)(2,1)}, u32[]{:S(2)}) copy-start(bf16[4,6,12,512]{3,0,2,1:T(4,128)(2,1)} %param.6) | copy-start | bytes 884740
  50.7 37.4 %copy-start.1 = (bf16[4,6,12,512]{3,0,2,1:T(4,128)(2,1)S(1)}, bf16[4,6,12,512]{3,0,2,1:T(4,128)(2,1)}, u32[]{:S(2)}) copy-start(bf16[4,6,12,512]{3,0,2,1:T(4,128)(2,1)} %param.7) | copy-start | bytes 884740
  50.7 9.5 %collective-permute-start.8 = (bf16[32,512]{1,0:T(8,128)(2,1)S(1)}, bf16[32,512]{1,0:T(8,128)(2,1)S(1)}, u32[]{:S(2)}, u32[]{:S(2)}) collective-permute-start(bf16[32,512]{1,0:T(8,128)(2,1)S(1)} %get-tuple-element.52.own_ref), channel_id=1, source_target_pairs={{0,32},{32,64},{64,96},{96,0},{1,33},{33,65},{65,97},{97,1},{2,34}... | collective-permute-start | bytes 98312 | tf_op jit(solution)/shard_map/ppermute | solution.py:406
  53.6 7.6 %collective-permute-start.7 = (bf16[32,512]{1,0:T(8,128)(2,1)S(1)}, bf16[32,512]{1,0:T(8,128)(2,1)S(1)}, u32[]{:S(2)}, u32[]{:S(2)}) collective-permute-start(bf16[32,512]{1,0:T(8,128)(2,1)S(1)} %get-tuple-element.52.own_ref), channel_id=1, source_target_pairs={{0,64},{32,96},{64,0},{96,32},{1,65},{33,97},{65,1},{97,33},{2,66}... | collective-permute-start | bytes 98312 | tf_op jit(solution)/shard_map/ppermute | solution.py:406
  59.1 4.3 %collective-permute-start.6 = (bf16[32,512]{1,0:T(8,128)(2,1)S(1)}, bf16[32,512]{1,0:T(8,128)(2,1)S(1)}, u32[]{:S(2)}, u32[]{:S(2)}) collective-permute-start(bf16[32,512]{1,0:T(8,128)(2,1)S(1)} %get-tuple-element.52.own_ref), channel_id=1, source_target_pairs={{0,96},{32,0},{64,32},{96,64},{1,97},{33,1},{65,33},{97,65},{2,98}... | collective-permute-start | bytes 98312 | tf_op jit(solution)/shard_map/ppermute | solution.py:406
  84.5 6.2 %collective-permute-start.9 = (bf16[4,256,512]{2,1,0:T(8,128)(2,1)S(1)}, bf16[4,256,512]{2,1,0:T(8,128)(2,1)S(1)}, u32[]{:S(2)}, u32[]{:S(2)}) collective-permute-start(bf16[4,256,512]{2,1,0:T(8,128)(2,1)S(1)} %bitcast.11), channel_id=1, source_target_pairs={{0,8},{8,0},{1,9},{9,1},{2,10},{10,2},{3,11},{11,3},{4,12},{12,4},... | collective-permute-start | bytes 3145736 | tf_op jit(solution)/shard_map/ppermute | solution.py:338

commit v5 on v1

--- a/solution.py
+++ b/solution.py
@@ -214,11 +214,13 @@
     out_ref[...] = total.astype(BF16)
 
 
-def spread_kernel(own_ref, one_ref, two_ref, three_ref, side_ref, out_ref):
+def pair_kernel(own_ref, other_ref, out_ref):
+    out_ref[...] = (own_ref[...].astype(F32) + other_ref[...].astype(F32)).astype(BF16)
+
+
+def spread_kernel(own_ref, other_ref, side_ref, out_ref):
     del side_ref
-    even = own_ref[...].astype(F32) + two_ref[...].astype(F32)
-    odd = one_ref[...].astype(F32) + three_ref[...].astype(F32)
-    total = (even + odd).astype(BF16)
+    total = (own_ref[...].astype(F32) + other_ref[...].astype(F32)).astype(BF16)
     for n in range(out_ref.shape[0]):
         out_ref[n] = total
 
@@ -369,18 +371,17 @@
     part, side_back = call(
         sum_kernel, [shaped((CHUNK, D), BF16), pair], ins=[vmem] * 3, out_specs=[vmem] * 2, mib=6
     )(got, lower_back, right_back)
-    others = [
-        lax.ppermute(part, FAR, [(n, (n - step) % N_FAR) for n in range(N_FAR)])
-        for step in range(1, N_FAR)
-    ]
+    other = lax.ppermute(part, FAR, [(n, n ^ 1) for n in range(N_FAR)])
+    part = call(pair_kernel, shaped((CHUNK, D), BF16), mib=1)(part, other)
+    other = lax.ppermute(part, FAR, [(n, n ^ 2) for n in range(N_FAR)])
     side_back = moved(side_back, 0, 1)
     parts = call(
         spread_kernel,
         shaped((N_NEAR, CHUNK, D), BF16),
-        ins=[vmem] * 4 + [anywhere],
+        ins=[vmem] * 2 + [anywhere],
         out_specs=vmem,
         mib=4,
-    )(part, *others, side_back)
+    )(part, other, side_back)
     mine = lax.all_to_all(parts, NEAR, 0, 0)
     mine = mine.reshape(4, HALF_D, D)
     other = swapped(mine)

time: 92.9 us -> 91.9 us (0.989)
  waiting for transfers between devices: 20 us -> 21.8 us
  blocking collectives: 23 us -> 21.6 us
  starting transfers between devices: 33.2 us -> 31.9 us
    ppermute x3 -> x2, starting transfers between devices: 8.09 us -> 6.22 us  [the longest x1 4.73 us: on_device(): other = lax.ppermute(part, FAR, [(n, n ^ 2) for n in range(N_FAR)])]
    ppermute x3 -> x2, waiting for transfers between devices: 2.92 us -> 4.76 us  [the longest x1 2.55 us: on_device(): other = lax.ppermute(part, FAR, [(n, n ^ 2) for n in range(N_FAR)])]
    all_to_all x1, blocking collectives: 23 us -> 21.6 us  [on_device(): mine = lax.all_to_all(parts, NEAR, 0, 0)]
  transfers between devices with their start and end apart: 11 -> 10, of which waited for: 5 -> 5; matrix products, arithmetic and copies ran while one was open for 1% -> 1% of each run, Pallas kernels for 6% -> 6%
where the time goes in v5:
time: 91.9 us; the launch traced here: 91.6 us
  starting transfers between devices  31.9 us (35%)
  waiting for transfers between devices  21.8 us (24%)
  blocking collectives  21.6 us (24%)
  Pallas kernels  14.2 us (15%)
  local copies, waits for them, and re-layouts  1.2 us (1%)
    all_to_all x1, blocking collectives, on_device(): mine = lax.all_to_all(parts, NEAR, 0, 0)  21.6 us
    ppermute x5, starting transfers between devices, moved(): return lax.ppermute(block, AXES, route)  15.1 us
    ppermute x5, waiting for transfers between devices, moved(): return lax.ppermute(block, AXES, route)  12.8 us
    ppermute x2, starting transfers between devices, swapped(): return lax.ppermute(block, 'c', [(0, 1), (1, 0)])  6.3 us
    ppermute x1, starting transfers between devices, on_device(): other = lax.ppermute(part, FAR, [(n, n ^ 2) for n in range(N_FAR)])  4.73 us
    all_to_all x1, starting transfers between devices, on_device(): got = lax.all_to_all(half.reshape(N_NEAR, CHUNK, D), NEAR, 0, 0)  4.3 us
    pallas_call x1, Pallas kernels, on_device(): call(attend_kernel, [shaped((4, HALF_D, D), BF16), shaped((2, D, TOKENS),...  4.27 us
    all_to_all x1, waiting for transfers between devices, on_device(): got = lax.all_to_all(half.reshape(N_NEAR, CHUNK, D), NEAR, 0, 0)  3.77 us
  transfers between devices with their start and end apart: 10, of which 5 were waited for; matrix products, arithmetic and copies ran while one was open for 1% of the time, Pallas kernels for 6%

profile of v5, /device:TPU:1, one launch (start us, length us, event | category | flops | bytes accessed | tf_op | source)
XLA Modules:
  0.0 91.6 jit_solution(9088065096447514128)
XLA Ops:
  0.6 1.2 %shard_map.101 = (bf16[2,3,6,4,512]{4,3,2,1,0:T(4,128)(2,1)S(1)}, bf16[2,3,6,4,512]{4,3,2,1,0:T(4,128)(2,1)S(1)}, bf16[2,3,6,4,512]{4,3,2,1,0:T(4,128)(2,1)S(1)}, bf16[2,3,6,4,512]{4,3,2,1,0:T(4,128)(2,1)S(1)}) custom-call(bf16[6,12,4,512]{3,2,1,0:T(4,128)(2,1)} %bitcast.13, bf16[6,12,4,512]{3,2,1,0:T(4,128)(2,1)} %bitcast.15), custom_call_target="tpu_custom_call" | custom-call | tf_op jit(solution)/shard_map/pallas_call | solution.py:320
  1.8 6.7 %collective-permute-start = (bf16[2,3,6,4,512]{4,3,2,1,0:T(4,128)(2,1)S(1)}, bf16[2,3,6,4,512]{4,3,2,1,0:T(4,128)(2,1)S(1)}, u32[]{:S(2)}, u32[]{:S(2)}) collective-permute-start(bf16[2,3,6,4,512]{4,3,2,1,0:T(4,128)(2,1)S(1)} %get-tuple-element.32), channel_id=1, source_target_pairs={{0,255},{1,248},{2,249},{3,250},{4,251},{5,252},{6,253},{7,254},{8... | collective-permute-start | bytes 442376 | tf_op jit(solution)/shard_map/ppermute | solution.py:307
  8.5 0.2 collective-permute-start.1
  8.7 5.4 %collective-permute-start.2 = (bf16[2,3,6,4,512]{4,3,2,1,0:T(4,128)(2,1)S(1)}, bf16[2,3,6,4,512]{4,3,2,1,0:T(4,128)(2,1)S(1)}, u32[]{:S(2)}, u32[]{:S(2)}) collective-permute-start(bf16[2,3,6,4,512]{4,3,2,1,0:T(4,128)(2,1)S(1)} %get-tuple-element.34), channel_id=1, source_target_pairs={{0,248},{1,249},{2,250},{3,251},{4,252},{5,253},{6,254},{7,255},{8... | collective-permute-start | bytes 442376 | tf_op jit(solution)/shard_map/ppermute | solution.py:307
  14.2 0.8 reshape.27
  15.0 0.3 copy.14
  15.2 0.1 eq.15
  15.4 1.5 %shard_map.102 = (bf16[512,1536]{1,0:T(8,128)(2,1)S(1)}, bf16[512,512]{1,0:T(8,128)(2,1)S(1)}, f32[1,512]{1,0:T(1,128)S(1)}) custom-call(bf16[512,1536]{1,0:T(8,128)(2,1)} %qkv_ref.1, bf16[512,512]{1,0:T(8,128)(2,1)} %proj_ref.1, f32[1,512]{1,0:T(1,128)} %bitcast.18), custom_call_target="tpu_custom_call" | custom-call | tf_op jit(solution)/shard_map/pallas_call | solution.py:334
  16.9 0.1 compare_select_fusion.bias_ref
  17.0 0.0 collective-permute-done.corner_ref
  17.0 0.0 collective-permute-done.1.right_ref
  17.1 0.0 collective-permute-done.2.below_ref
  17.1 4.3 %shard_map.103 = (bf16[4,256,512]{2,1,0:T(8,128)(2,1)S(1)}, bf16[2,512,288]{2,1,0:T(8,128)(2,1)S(1)}, bf16[4,288,512]{2,1,0:T(8,128)(2,1)S(1)}, bf16[288,512]{1,...) custom-call(bf16[2,3,6,4,512]{4,3,2,1,0:T(4,128)(2,1)S(1)} %collective-permute-done.corner_ref, ...), custom_call_target="tpu_custom_call" | custom-call | tf_op jit(solution)/shard_map/pallas_call | solution.py:342
  21.3 3.0 %collective-permute-start.4 = (bf16[4,256,512]{2,1,0:T(8,128)(2,1)S(1)}, bf16[4,256,512]{2,1,0:T(8,128)(2,1)S(1)}, u32[]{:S(2)}, u32[]{:S(2)}) collective-permute-start(bf16[4,256,512]{2,1,0:T(8,128)(2,1)S(1)} %get-tuple-element.47), channel_id=1, source_target_pairs={{0,8},{8,0},{1,9},{9,1},{2,10},{10,2},{3,11},{11,3},{4,12},{12,4},... | collective-permute-start | bytes 3145736 | tf_op jit(solution)/shard_map/ppermute | solution.py:311
  24.4 1.8 %shard_map.104 = (bf16[4,256,512]{2,1,0:T(8,128)(2,1)S(1)}, bf16[2,3,6,4,512]{4,3,2,1,0:T(4,128)(2,1)S(1)}, bf16[2,3,6,4,512]{4,3,2,1,0:T(4,128)(2,1)S(1)}, bf16[2,2,3,6,4,512]{5,4,3,2,1,0:T(4,128)(2,1)S(1)}) custom-call(bf16[2,512,288]{2,1,0:T(8,128)(2,1)S(1)} %get-tuple-element.39.left_ref, bf16[4,288,512]{2,1,0:T(8,128)(2,1)S(1)} %get-tuple-element.40.rows_ref, ...), custom_call_target="tpu_custom_call" | custom-call | tf_op jit(solution)/shard_map/pallas_call | solution.py:356
  26.1 0.5 collective-permute-done.4.got_ref
  26.7 1.1 %shard_map.105 = bf16[4,256,512]{2,1,0:T(8,128)(2,1)} custom-call(bf16[4,256,512]{2,1,0:T(8,128)(2,1)S(1)} %get-tuple-element.46.keep_ref, bf16[4,256,512]{2,1,0:T(8,128)(2,1)S(1)} %collective-permute-done.4.got_ref), custom_call_target="tpu_custom_call" | custom-call | tf_op jit(solution)/shard_map/pallas_call | solution.py:361
  27.7 4.3 %all-to-all-start = ((bf16[32,32,512]{2,1,0:T(8,128)(2,1)}), bf16[32,32,512]{2,1,0:T(8,128)(2,1)S(1)}, u32[]{:S(2)}, u32[]{:S(2)}) async-start(bf16[32,32,512]{2,1,0:T(8,128)(2,1)} %bitcast.4), calls=%async_computation | async-start | bytes 2097152 | tf_op jit(solution)/shard_map/all_to_all | solution.py:369
  32.0 2.1 %collective-permute-start.3 = (bf16[2,2,3,6,4,512]{5,4,3,2,1,0:T(4,128)(2,1)S(1)}, bf16[2,2,3,6,4,512]{5,4,3,2,1,0:T(4,128)(2,1)S(1)}, u32[]{:S(2)}, u32[]{:S(2)}) collective-permute-start(bf16[2,2,3,6,4,512]{5,4,3,2,1,0:T(4,128)(2,1)S(1)} %get-tuple-element.45), channel_id=1, source_target_pairs={{0,8},{1,9},{2,10},{3,11},{4,12},{5,13},{6,14},{7,15},{8,16},{9,17... | collective-permute-start | bytes 884744 | tf_op jit(solution)/shard_map/ppermute | solution.py:307
  34.2 12.7 %collective-permute-done.3.lower_ref = bf16[2,2,3,6,4,512]{5,4,3,2,1,0:T(4,128)(2,1)S(1)} collective-permute-done((bf16[2,2,3,6,4,512]{5,4,3,2,1,0:T(4,128)(2,1)S(1)}, bf16[2,2,3,6,4,512]{5,4,3,2,1,0:T(4,128)(2,1)S(1)}, u32[]{:S(2)}, u32[]{:S(2)}) %collective-permute-start.3) | collective-permute-done | bytes 294944 | tf_op jit(solution)/shard_map/ppermute | solution.py:307
  46.9 3.8 %all-to-all-done.got_ref = bf16[32,32,512]{2,1,0:T(8,128)(2,1)S(1)} async-done(((bf16[32,32,512]{2,1,0:T(8,128)(2,1)}), bf16[32,32,512]{2,1,0:T(8,128)(2,1)S(1)}, u32[]{:S(2)}, u32[]{:S(2)}) %all-to-all-start) | async-done | bytes 1048608 | tf_op jit(solution)/shard_map/all_to_all | solution.py:369
  50.7 0.2 shard_map.106
  50.8 0.6 collective-permute-start.5
  51.5 1.5 %collective-permute-start.6 = (bf16[32,512]{1,0:T(8,128)(2,1)S(1)}, bf16[32,512]{1,0:T(8,128)(2,1)S(1)}, u32[]{:S(2)}, u32[]{:S(2)}) collective-permute-start(bf16[32,512]{1,0:T(8,128)(2,1)S(1)} %get-tuple-element.52.own_ref), channel_id=1, source_target_pairs={{0,32},{32,0},{64,96},{96,64},{1,33},{33,1},{65,97},{97,65},{2,34}... | collective-permute-start | bytes 98312 | tf_op jit(solution)/shard_map/ppermute | solution.py:374
  53.0 2.2 %collective-permute-done.6.other_ref = bf16[32,512]{1,0:T(8,128)(2,1)S(1)} collective-permute-done((bf16[32,512]{1,0:T(8,128)(2,1)S(1)}, bf16[32,512]{1,0:T(8,128)(2,1)S(1)}, u32[]{:S(2)}, u32[]{:S(2)}) %collective-permute-start.6) | collective-permute-done | bytes 32800 | tf_op jit(solution)/shard_map/ppermute | solution.py:374
  55.2 0.0 copy-start
  55.2 0.0 copy-start.1
  55.2 4.7 %collective-permute-start.7 = (bf16[32,512]{1,0:T(8,128)(2,1)S(1)}, bf16[32,512]{1,0:T(8,128)(2,1)S(1)}, u32[]{:S(2)}, u32[]{:S(2)}) collective-permute-start(bf16[32,512]{1,0:T(8,128)(2,1)S(1)} %shard_map.108.own_ref), channel_id=1, source_target_pairs={{0,64},{32,96},{64,0},{96,32},{1,65},{33,97},{65,1},{97,33},{2,66}... | collective-permute-start | bytes 98312 | tf_op jit(solution)/shard_map/ppermute | solution.py:376
  59.9 2.5 %collective-permute-done.7.other_ref = bf16[32,512]{1,0:T(8,128)(2,1)S(1)} collective-permute-done((bf16[32,512]{1,0:T(8,128)(2,1)S(1)}, bf16[32,512]{1,0:T(8,128)(2,1)S(1)}, u32[]{:S(2)}, u32[]{:S(2)}) %collective-permute-start.7) | collective-permute-done | bytes 32800 | tf_op jit(solution)/shard_map/ppermute | solution.py:376
  62.5 0.0 collective-permute-done.5.side_ref
  62.5 0.1 shard_map.109
  62.6 21.6 %all_to_all.10 = bf16[32,32,512]{2,1,0:T(8,128)(2,1)S(1)} all-to-all(bf16[32,32,512]{2,1,0:T(8,128)(2,1)S(1)} %shard_map.109), channel_id=1, replica_groups=mesh['xl'=2,'zh'=4,'zl'=2,'c'=2,'y'=4,'xh'=2] {'xh','xl','y','zl'}, dimensions={0} | all-to-all | bytes 2097152 | tf_op jit(solution)/shard_map/all_to_all | solution.py:385
  84.2 3.3 %collective-permute-start.8 = (bf16[4,256,512]{2,1,0:T(8,128)(2,1)S(1)}, bf16[4,256,512]{2,1,0:T(8,128)(2,1)S(1)}, u32[]{:S(2)}, u32[]{:S(2)}) collective-permute-start(bf16[4,256,512]{2,1,0:T(8,128)(2,1)S(1)} %bitcast.11), channel_id=1, source_target_pairs={{0,8},{8,0},{1,9},{9,1},{2,10},{10,2},{3,11},{11,3},{4,12},{12,4},... | collective-permute-start | bytes 3145736 | tf_op jit(solution)/shard_map/ppermute | solution.py:311
  87.4 0.0 copy-done
  87.4 0.0 copy-done.1
  87.4 1.0 %shard_map.107 = (bf16[6,12,4,512]{3,2,1,0:T(4,128)(2,1)}, bf16[6,12,4,512]{3,2,1,0:T(4,128)(2,1)}) custom-call(bf16[6,12,4,512]{3,2,1,0:T(4,128)(2,1)S(1)} %bitcast.14, bf16[6,12,4,512]{3,2,1,0:T(4,128)(2,1)S(1)} %bitcast.16, bf16[2,3,6,4,512]{4,3,2,1,0:T(4,128)(2,1)S(1)} %get-tuple-element.44.own_ref, ...), custom_call_target="tpu_custom_call" | custom-call | tf_op jit(solution)/shard_map/pallas_call | solution.py:410
  88.4 1.6 %shard_map.110 = (f32[512,1536]{1,0:T(8,128)}, f32[512,512]{1,0:T(8,128)}, f32[1,512]{1,0:T(1,128)S(1)}) custom-call(bf16[4,256,512]{2,1,0:T(8,128)(2,1)S(1)} %bitcast.12, bf16[512,1536]{1,0:T(8,128)(2,1)S(1)} %get-tuple-element.37.qkv_ref, f32[1,512]{1,0:T(1,128)S(1)} %get-tuple-element.36.gain_ref), custom_call_target="tpu_custom_call" | custom-call | tf_op jit(solution)/shard_map/pallas_call | solution.py:388
  90.0 0.0 collective-permute-done.8.ref
  90.0 1.6 %shard_map.111 = (f32[512,1536]{1,0:T(8,128)}, f32[512,512]{1,0:T(8,128)}, f32[1,512]{1,0:T(1,128)}) custom-call(bf16[4,256,512]{2,1,0:T(8,128)(2,1)S(1)} %collective-permute-done.8.ref, bf16[512,1536]{1,0:T(8,128)(2,1)S(1)} %get-tuple-element.37.qkv_ref, f32[1,512]{1,0:T(1,128)S(1)} %get-tuple-element.36.gain_ref, ...), custom_call_target="tpu_custom_call", output_to_operand_aliasing={{0}: (3, {}), {1}: (4, {})} | custom-call | tf_op jit(solution)/shard_map/pallas_call | solution.py:396
  (1 shorter events, 0.0 us)
Async XLA Ops:
  1.8 15.2 %collective-permute-start = (bf16[2,3,6,4,512]{4,3,2,1,0:T(4,128)(2,1)S(1)}, bf16[2,3,6,4,512]{4,3,2,1,0:T(4,128)(2,1)S(1)}, u32[]{:S(2)}, u32[]{:S(2)}) collective-permute-start(bf16[2,3,6,4,512]{4,3,2,1,0:T(4,128)(2,1)S(1)} %get-tuple-element.32), channel_id=1, source_target_pairs={{0,255},{1,248},{2,249},{3,250},{4,251},{5,252},{6,253},{7,254},{8... | collective-permute-start | bytes 442376 | tf_op jit(solution)/shard_map/ppermute | solution.py:307
  8.5 8.5 %collective-permute-start.1 = (bf16[2,3,6,4,512]{4,3,2,1,0:T(4,128)(2,1)S(1)}, bf16[2,3,6,4,512]{4,3,2,1,0:T(4,128)(2,1)S(1)}, u32[]{:S(2)}, u32[]{:S(2)}) collective-permute-start(bf16[2,3,6,4,512]{4,3,2,1,0:T(4,128)(2,1)S(1)} %get-tuple-element.33), channel_id=1, source_target_pairs={{0,7},{1,0},{2,1},{3,2},{4,3},{5,4},{6,5},{7,6},{8,15},{9,8},{10,9... | collective-permute-start | bytes 442376 | tf_op jit(solution)/shard_map/ppermute | solution.py:307
  8.7 8.3 %collective-permute-start.2 = (bf16[2,3,6,4,512]{4,3,2,1,0:T(4,128)(2,1)S(1)}, bf16[2,3,6,4,512]{4,3,2,1,0:T(4,128)(2,1)S(1)}, u32[]{:S(2)}, u32[]{:S(2)}) collective-permute-start(bf16[2,3,6,4,512]{4,3,2,1,0:T(4,128)(2,1)S(1)} %get-tuple-element.34), channel_id=1, source_target_pairs={{0,248},{1,249},{2,250},{3,251},{4,252},{5,253},{6,254},{7,255},{8... | collective-permute-start | bytes 442376 | tf_op jit(solution)/shard_map/ppermute | solution.py:307
  21.3 5.3 %collective-permute-start.4 = (bf16[4,256,512]{2,1,0:T(8,128)(2,1)S(1)}, bf16[4,256,512]{2,1,0:T(8,128)(2,1)S(1)}, u32[]{:S(2)}, u32[]{:S(2)}) collective-permute-start(bf16[4,256,512]{2,1,0:T(8,128)(2,1)S(1)} %get-tuple-element.47), channel_id=1, source_target_pairs={{0,8},{8,0},{1,9},{9,1},{2,10},{10,2},{3,11},{11,3},{4,12},{12,4},... | collective-permute-start | bytes 3145736 | tf_op jit(solution)/shard_map/ppermute | solution.py:311
  27.7 23.0 %all-to-all-start = ((bf16[32,32,512]{2,1,0:T(8,128)(2,1)}), bf16[32,32,512]{2,1,0:T(8,128)(2,1)S(1)}, u32[]{:S(2)}, u32[]{:S(2)}) async-start(bf16[32,32,512]{2,1,0:T(8,128)(2,1)} %bitcast.4), calls=%async_computation | async-start | bytes 2097152 | tf_op jit(solution)/shard_map/all_to_all | solution.py:369
  32.0 14.9 %collective-permute-start.3 = (bf16[2,2,3,6,4,512]{5,4,3,2,1,0:T(4,128)(2,1)S(1)}, bf16[2,2,3,6,4,512]{5,4,3,2,1,0:T(4,128)(2,1)S(1)}, u32[]{:S(2)}, u32[]{:S(2)}) collective-permute-start(bf16[2,2,3,6,4,512]{5,4,3,2,1,0:T(4,128)(2,1)S(1)} %get-tuple-element.45), channel_id=1, source_target_pairs={{0,8},{1,9},{2,10},{3,11},{4,12},{5,13},{6,14},{7,15},{8,16},{9,17... | collective-permute-start | bytes 884744 | tf_op jit(solution)/shard_map/ppermute | solution.py:307
  50.8 11.6 %collective-permute-start.5 = (bf16[2,2,3,6,4,512]{5,4,3,2,1,0:T(4,128)(2,1)S(1)}, bf16[2,2,3,6,4,512]{5,4,3,2,1,0:T(4,128)(2,1)S(1)}, u32[]{:S(2)}, u32[]{:S(2)}) collective-permute-start(bf16[2,2,3,6,4,512]{5,4,3,2,1,0:T(4,128)(2,1)S(1)} %get-tuple-element.49), channel_id=1, source_target_pairs={{0,1},{1,2},{2,3},{3,4},{4,5},{5,6},{6,7},{7,0},{8,9},{9,10},{10,1... | collective-permute-start | bytes 884744 | tf_op jit(solution)/shard_map/ppermute | solution.py:307
  51.5 3.7 %collective-permute-start.6 = (bf16[32,512]{1,0:T(8,128)(2,1)S(1)}, bf16[32,512]{1,0:T(8,128)(2,1)S(1)}, u32[]{:S(2)}, u32[]{:S(2)}) collective-permute-start(bf16[32,512]{1,0:T(8,128)(2,1)S(1)} %get-tuple-element.52.own_ref), channel_id=1, source_target_pairs={{0,32},{32,0},{64,96},{96,64},{1,33},{33,1},{65,97},{97,65},{2,34}... | collective-permute-start | bytes 98312 | tf_op jit(solution)/shard_map/ppermute | solution.py:374
  55.2 32.3 %copy-start = (bf16[4,6,12,512]{3,0,2,1:T(4,128)(2,1)S(1)}, bf16[4,6,12,512]{3,0,2,1:T(4,128)(2,1)}, u32[]{:S(2)}) copy-start(bf16[4,6,12,512]{3,0,2,1:T(4,128)(2,1)} %param.6) | copy-start | bytes 884740
  55.2 32.2 %copy-start.1 = (bf16[4,6,12,512]{3,0,2,1:T(4,128)(2,1)S(1)}, bf16[4,6,12,512]{3,0,2,1:T(4,128)(2,1)}, u32[]{:S(2)}) copy-start(bf16[4,6,12,512]{3,0,2,1:T(4,128)(2,1)} %param.7) | copy-start | bytes 884740
  55.2 7.3 %collective-permute-start.7 = (bf16[32,512]{1,0:T(8,128)(2,1)S(1)}, bf16[32,512]{1,0:T(8,128)(2,1)S(1)}, u32[]{:S(2)}, u32[]{:S(2)}) collective-permute-start(bf16[32,512]{1,0:T(8,128)(2,1)S(1)} %shard_map.108.own_ref), channel_id=1, source_target_pairs={{0,64},{32,96},{64,0},{96,32},{1,65},{33,97},{65,1},{97,33},{2,66}... | collective-permute-start | bytes 98312 | tf_op jit(solution)/shard_map/ppermute | solution.py:376
  84.2 5.8 %collective-permute-start.8 = (bf16[4,256,512]{2,1,0:T(8,128)(2,1)S(1)}, bf16[4,256,512]{2,1,0:T(8,128)(2,1)S(1)}, u32[]{:S(2)}, u32[]{:S(2)}) collective-permute-start(bf16[4,256,512]{2,1,0:T(8,128)(2,1)S(1)} %bitcast.11), channel_id=1, source_target_pairs={{0,8},{8,0},{1,9},{9,1},{2,10},{10,2},{3,11},{11,3},{4,12},{12,4},... | collective-permute-start | bytes 3145736 | tf_op jit(solution)/shard_map/ppermute | solution.py:311

commit v6 on v5

--- a/solution.py
+++ b/solution.py
@@ -194,15 +194,8 @@
         copy.wait()
 
 
-def add_kernel(keep_ref, got_ref, out_ref, held, sems):
-    copies = []
-    for block in range(4):
-        held[block] = (keep_ref[block].astype(F32) + got_ref[block].astype(F32)).astype(BF16)
-        copy = pltpu.make_async_copy(held.at[block], out_ref.at[block], sems.at[block])
-        copy.start()
-        copies.append(copy)
-    for copy in copies:
-        copy.wait()
+def add_kernel(keep_ref, got_ref, out_ref):
+    out_ref[...] = (keep_ref[...].astype(F32) + got_ref[...].astype(F32)).astype(BF16)
 
 
 def sum_kernel(got_ref, lower_ref, right_ref, out_ref, side_ref):
@@ -358,14 +351,7 @@
         [shaped((4, HALF_D, D), BF16), shaped(PIECE, BF16), shaped(PIECE, BF16), pair],
         mib=16,
     )(*state, gain, qkv_weight, proj_weight)
-    half = call(
-        add_kernel,
-        shaped((4, HALF_D, D), BF16),
-        [pltpu.VMEM((4, HALF_D, D), BF16), pltpu.SemaphoreType.DMA((4,))],
-        [vmem] * 2,
-        anywhere,
-        mib=4,
-    )(keep, got)
+    half = call(add_kernel, pltpu.VMEM((4, HALF_D, D), BF16), mib=4)(keep, got)
     got = lax.all_to_all(half.reshape(N_NEAR, CHUNK, D), NEAR, 0, 0)
     lower_back = moved(lower_back, 1, 0)
     part, side_back = call(

time: 91.9 us -> 92 us (level)
  no operation moved by 1% of the time
where the time goes in v6:
time: 92 us; the launch traced here: 91.7 us
  starting transfers between devices  31.9 us (35%)
  waiting for transfers between devices  21.8 us (24%)
  blocking collectives  21.6 us (23%)
  Pallas kernels  14.4 us (16%)
  local copies, waits for them, and re-layouts  1.2 us (1%)
    all_to_all x1, blocking collectives, on_device(): mine = lax.all_to_all(parts, NEAR, 0, 0)  21.6 us
    ppermute x5, starting transfers between devices, moved(): return lax.ppermute(block, AXES, route)  15.1 us
    ppermute x5, waiting for transfers between devices, moved(): return lax.ppermute(block, AXES, route)  12.8 us
    ppermute x2, starting transfers between devices, swapped(): return lax.ppermute(block, 'c', [(0, 1), (1, 0)])  6.3 us
    ppermute x1, starting transfers between devices, on_device(): other = lax.ppermute(part, FAR, [(n, n ^ 2) for n in range(N_FAR)])  4.73 us
    all_to_all x1, starting transfers between devices, on_device(): got = lax.all_to_all(half.reshape(N_NEAR, CHUNK, D), NEAR, 0, 0)  4.29 us
    pallas_call x1, Pallas kernels, on_device(): call(attend_kernel, [shaped((4, HALF_D, D), BF16), shaped((2, D, TOKENS),...  4.27 us
    all_to_all x1, waiting for transfers between devices, on_device(): got = lax.all_to_all(half.reshape(N_NEAR, CHUNK, D), NEAR, 0, 0)  3.77 us
  transfers between devices with their start and end apart: 10, of which 5 were waited for; matrix products, arithmetic and copies ran while one was open for 1% of the time, Pallas kernels for 6%

profile of v6, /device:TPU:1, one launch (start us, length us, event | category | flops | bytes accessed | tf_op | source)
XLA Modules:
  0.0 91.7 jit_solution(8048006310286023220)
XLA Ops:
  0.6 1.2 %shard_map.101 = (bf16[2,3,6,4,512]{4,3,2,1,0:T(4,128)(2,1)S(1)}, bf16[2,3,6,4,512]{4,3,2,1,0:T(4,128)(2,1)S(1)}, bf16[2,3,6,4,512]{4,3,2,1,0:T(4,128)(2,1)S(1)}, bf16[2,3,6,4,512]{4,3,2,1,0:T(4,128)(2,1)S(1)}) custom-call(bf16[6,12,4,512]{3,2,1,0:T(4,128)(2,1)} %bitcast.13, bf16[6,12,4,512]{3,2,1,0:T(4,128)(2,1)} %bitcast.15), custom_call_target="tpu_custom_call" | custom-call | tf_op jit(solution)/shard_map/pallas_call | solution.py:313
  1.8 6.7 %collective-permute-start = (bf16[2,3,6,4,512]{4,3,2,1,0:T(4,128)(2,1)S(1)}, bf16[2,3,6,4,512]{4,3,2,1,0:T(4,128)(2,1)S(1)}, u32[]{:S(2)}, u32[]{:S(2)}) collective-permute-start(bf16[2,3,6,4,512]{4,3,2,1,0:T(4,128)(2,1)S(1)} %get-tuple-element.32), channel_id=1, source_target_pairs={{0,255},{1,248},{2,249},{3,250},{4,251},{5,252},{6,253},{7,254},{8... | collective-permute-start | bytes 442376 | tf_op jit(solution)/shard_map/ppermute | solution.py:300
  8.5 0.2 collective-permute-start.1
  8.7 5.4 %collective-permute-start.2 = (bf16[2,3,6,4,512]{4,3,2,1,0:T(4,128)(2,1)S(1)}, bf16[2,3,6,4,512]{4,3,2,1,0:T(4,128)(2,1)S(1)}, u32[]{:S(2)}, u32[]{:S(2)}) collective-permute-start(bf16[2,3,6,4,512]{4,3,2,1,0:T(4,128)(2,1)S(1)} %get-tuple-element.34), channel_id=1, source_target_pairs={{0,248},{1,249},{2,250},{3,251},{4,252},{5,253},{6,254},{7,255},{8... | collective-permute-start | bytes 442376 | tf_op jit(solution)/shard_map/ppermute | solution.py:300
  14.2 0.8 reshape.27
  15.0 0.3 copy.14
  15.2 0.1 eq.15
  15.4 1.5 %shard_map.102 = (bf16[512,1536]{1,0:T(8,128)(2,1)S(1)}, bf16[512,512]{1,0:T(8,128)(2,1)S(1)}, f32[1,512]{1,0:T(1,128)S(1)}) custom-call(bf16[512,1536]{1,0:T(8,128)(2,1)} %qkv_ref.1, bf16[512,512]{1,0:T(8,128)(2,1)} %proj_ref.1, f32[1,512]{1,0:T(1,128)} %bitcast.18), custom_call_target="tpu_custom_call" | custom-call | tf_op jit(solution)/shard_map/pallas_call | solution.py:327
  16.9 0.1 compare_select_fusion.bias_ref
  17.0 0.0 collective-permute-done.corner_ref
  17.0 0.0 collective-permute-done.1.right_ref
  17.1 0.0 collective-permute-done.2.below_ref
  17.1 4.3 %shard_map.103 = (bf16[4,256,512]{2,1,0:T(8,128)(2,1)S(1)}, bf16[2,512,288]{2,1,0:T(8,128)(2,1)S(1)}, bf16[4,288,512]{2,1,0:T(8,128)(2,1)S(1)}, bf16[288,512]{1,...) custom-call(bf16[2,3,6,4,512]{4,3,2,1,0:T(4,128)(2,1)S(1)} %collective-permute-done.corner_ref, ...), custom_call_target="tpu_custom_call" | custom-call | tf_op jit(solution)/shard_map/pallas_call | solution.py:335
  21.3 3.0 %collective-permute-start.4 = (bf16[4,256,512]{2,1,0:T(8,128)(2,1)S(1)}, bf16[4,256,512]{2,1,0:T(8,128)(2,1)S(1)}, u32[]{:S(2)}, u32[]{:S(2)}) collective-permute-start(bf16[4,256,512]{2,1,0:T(8,128)(2,1)S(1)} %get-tuple-element.47), channel_id=1, source_target_pairs={{0,8},{8,0},{1,9},{9,1},{2,10},{10,2},{3,11},{11,3},{4,12},{12,4},... | collective-permute-start | bytes 3145736 | tf_op jit(solution)/shard_map/ppermute | solution.py:304
  24.4 1.8 %shard_map.104 = (bf16[4,256,512]{2,1,0:T(8,128)(2,1)S(1)}, bf16[2,3,6,4,512]{4,3,2,1,0:T(4,128)(2,1)S(1)}, bf16[2,3,6,4,512]{4,3,2,1,0:T(4,128)(2,1)S(1)}, bf16[2,2,3,6,4,512]{5,4,3,2,1,0:T(4,128)(2,1)S(1)}) custom-call(bf16[2,512,288]{2,1,0:T(8,128)(2,1)S(1)} %get-tuple-element.39.left_ref, bf16[4,288,512]{2,1,0:T(8,128)(2,1)S(1)} %get-tuple-element.40.rows_ref, ...), custom_call_target="tpu_custom_call" | custom-call | tf_op jit(solution)/shard_map/pallas_call | solution.py:349
  26.1 0.5 collective-permute-done.4.got_ref
  26.7 1.2 %shard_map.105 = bf16[4,256,512]{2,1,0:T(8,128)(2,1)} custom-call(bf16[4,256,512]{2,1,0:T(8,128)(2,1)S(1)} %get-tuple-element.46.keep_ref, bf16[4,256,512]{2,1,0:T(8,128)(2,1)S(1)} %collective-permute-done.4.got_ref), custom_call_target="tpu_custom_call" | custom-call | tf_op jit(solution)/shard_map/pallas_call | solution.py:354
  27.9 4.3 %all-to-all-start = ((bf16[32,32,512]{2,1,0:T(8,128)(2,1)}), bf16[32,32,512]{2,1,0:T(8,128)(2,1)S(1)}, u32[]{:S(2)}, u32[]{:S(2)}) async-start(bf16[32,32,512]{2,1,0:T(8,128)(2,1)} %bitcast.4), calls=%async_computation | async-start | bytes 2097152 | tf_op jit(solution)/shard_map/all_to_all | solution.py:355
  32.2 2.1 %collective-permute-start.3 = (bf16[2,2,3,6,4,512]{5,4,3,2,1,0:T(4,128)(2,1)S(1)}, bf16[2,2,3,6,4,512]{5,4,3,2,1,0:T(4,128)(2,1)S(1)}, u32[]{:S(2)}, u32[]{:S(2)}) collective-permute-start(bf16[2,2,3,6,4,512]{5,4,3,2,1,0:T(4,128)(2,1)S(1)} %get-tuple-element.45), channel_id=1, source_target_pairs={{0,8},{1,9},{2,10},{3,11},{4,12},{5,13},{6,14},{7,15},{8,16},{9,17... | collective-permute-start | bytes 884744 | tf_op jit(solution)/shard_map/ppermute | solution.py:300
  34.3 12.7 %collective-permute-done.3.lower_ref = bf16[2,2,3,6,4,512]{5,4,3,2,1,0:T(4,128)(2,1)S(1)} collective-permute-done((bf16[2,2,3,6,4,512]{5,4,3,2,1,0:T(4,128)(2,1)S(1)}, bf16[2,2,3,6,4,512]{5,4,3,2,1,0:T(4,128)(2,1)S(1)}, u32[]{:S(2)}, u32[]{:S(2)}) %collective-permute-start.3) | collective-permute-done | bytes 294944 | tf_op jit(solution)/shard_map/ppermute | solution.py:300
  47.0 3.8 %all-to-all-done.got_ref = bf16[32,32,512]{2,1,0:T(8,128)(2,1)S(1)} async-done(((bf16[32,32,512]{2,1,0:T(8,128)(2,1)}), bf16[32,32,512]{2,1,0:T(8,128)(2,1)S(1)}, u32[]{:S(2)}, u32[]{:S(2)}) %all-to-all-start) | async-done | bytes 1048608 | tf_op jit(solution)/shard_map/all_to_all | solution.py:355
  50.8 0.2 shard_map.106
  51.0 0.6 collective-permute-start.5
  51.6 1.5 %collective-permute-start.6 = (bf16[32,512]{1,0:T(8,128)(2,1)S(1)}, bf16[32,512]{1,0:T(8,128)(2,1)S(1)}, u32[]{:S(2)}, u32[]{:S(2)}) collective-permute-start(bf16[32,512]{1,0:T(8,128)(2,1)S(1)} %get-tuple-element.52.own_ref), channel_id=1, source_target_pairs={{0,32},{32,0},{64,96},{96,64},{1,33},{33,1},{65,97},{97,65},{2,34}... | collective-permute-start | bytes 98312 | tf_op jit(solution)/shard_map/ppermute | solution.py:360
  53.1 2.2 %collective-permute-done.6.other_ref = bf16[32,512]{1,0:T(8,128)(2,1)S(1)} collective-permute-done((bf16[32,512]{1,0:T(8,128)(2,1)S(1)}, bf16[32,512]{1,0:T(8,128)(2,1)S(1)}, u32[]{:S(2)}, u32[]{:S(2)}) %collective-permute-start.6) | collective-permute-done | bytes 32800 | tf_op jit(solution)/shard_map/ppermute | solution.py:360
  55.3 0.0 copy-start
  55.3 0.0 copy-start.1
  55.3 4.7 %collective-permute-start.7 = (bf16[32,512]{1,0:T(8,128)(2,1)S(1)}, bf16[32,512]{1,0:T(8,128)(2,1)S(1)}, u32[]{:S(2)}, u32[]{:S(2)}) collective-permute-start(bf16[32,512]{1,0:T(8,128)(2,1)S(1)} %shard_map.108.own_ref), channel_id=1, source_target_pairs={{0,64},{32,96},{64,0},{96,32},{1,65},{33,97},{65,1},{97,33},{2,66}... | collective-permute-start | bytes 98312 | tf_op jit(solution)/shard_map/ppermute | solution.py:362
  60.1 2.5 %collective-permute-done.7.other_ref = bf16[32,512]{1,0:T(8,128)(2,1)S(1)} collective-permute-done((bf16[32,512]{1,0:T(8,128)(2,1)S(1)}, bf16[32,512]{1,0:T(8,128)(2,1)S(1)}, u32[]{:S(2)}, u32[]{:S(2)}) %collective-permute-start.7) | collective-permute-done | bytes 32800 | tf_op jit(solution)/shard_map/ppermute | solution.py:362
  62.6 0.0 collective-permute-done.5.side_ref
  62.6 0.1 shard_map.109
  62.7 21.6 %all_to_all.10 = bf16[32,32,512]{2,1,0:T(8,128)(2,1)S(1)} all-to-all(bf16[32,32,512]{2,1,0:T(8,128)(2,1)S(1)} %shard_map.109), channel_id=1, replica_groups=mesh['xl'=2,'zh'=4,'zl'=2,'c'=2,'y'=4,'xh'=2] {'xh','xl','y','zl'}, dimensions={0} | all-to-all | bytes 2097152 | tf_op jit(solution)/shard_map/all_to_all | solution.py:371
  84.3 3.3 %collective-permute-start.8 = (bf16[4,256,512]{2,1,0:T(8,128)(2,1)S(1)}, bf16[4,256,512]{2,1,0:T(8,128)(2,1)S(1)}, u32[]{:S(2)}, u32[]{:S(2)}) collective-permute-start(bf16[4,256,512]{2,1,0:T(8,128)(2,1)S(1)} %bitcast.11), channel_id=1, source_target_pairs={{0,8},{8,0},{1,9},{9,1},{2,10},{10,2},{3,11},{11,3},{4,12},{12,4},... | collective-permute-start | bytes 3145736 | tf_op jit(solution)/shard_map/ppermute | solution.py:304
  87.6 0.0 copy-done
  87.6 0.0 copy-done.1
  87.6 1.0 %shard_map.107 = (bf16[6,12,4,512]{3,2,1,0:T(4,128)(2,1)}, bf16[6,12,4,512]{3,2,1,0:T(4,128)(2,1)}) custom-call(bf16[6,12,4,512]{3,2,1,0:T(4,128)(2,1)S(1)} %bitcast.14, bf16[6,12,4,512]{3,2,1,0:T(4,128)(2,1)S(1)} %bitcast.16, bf16[2,3,6,4,512]{4,3,2,1,0:T(4,128)(2,1)S(1)} %get-tuple-element.44.own_ref, ...), custom_call_target="tpu_custom_call" | custom-call | tf_op jit(solution)/shard_map/pallas_call | solution.py:396
  88.5 1.6 %shard_map.110 = (f32[512,1536]{1,0:T(8,128)}, f32[512,512]{1,0:T(8,128)}, f32[1,512]{1,0:T(1,128)S(1)}) custom-call(bf16[4,256,512]{2,1,0:T(8,128)(2,1)S(1)} %bitcast.12, bf16[512,1536]{1,0:T(8,128)(2,1)S(1)} %get-tuple-element.37.qkv_ref, f32[1,512]{1,0:T(1,128)S(1)} %get-tuple-element.36.gain_ref), custom_call_target="tpu_custom_call" | custom-call | tf_op jit(solution)/shard_map/pallas_call | solution.py:374
  90.1 0.0 collective-permute-done.8.ref
  90.1 1.6 %shard_map.111 = (f32[512,1536]{1,0:T(8,128)}, f32[512,512]{1,0:T(8,128)}, f32[1,512]{1,0:T(1,128)}) custom-call(bf16[4,256,512]{2,1,0:T(8,128)(2,1)S(1)} %collective-permute-done.8.ref, bf16[512,1536]{1,0:T(8,128)(2,1)S(1)} %get-tuple-element.37.qkv_ref, f32[1,512]{1,0:T(1,128)S(1)} %get-tuple-element.36.gain_ref, ...), custom_call_target="tpu_custom_call", output_to_operand_aliasing={{0}: (3, {}), {1}: (4, {})} | custom-call | tf_op jit(solution)/shard_map/pallas_call | solution.py:382
  (1 shorter events, 0.0 us)
Async XLA Ops:
  1.8 15.2 %collective-permute-start = (bf16[2,3,6,4,512]{4,3,2,1,0:T(4,128)(2,1)S(1)}, bf16[2,3,6,4,512]{4,3,2,1,0:T(4,128)(2,1)S(1)}, u32[]{:S(2)}, u32[]{:S(2)}) collective-permute-start(bf16[2,3,6,4,512]{4,3,2,1,0:T(4,128)(2,1)S(1)} %get-tuple-element.32), channel_id=1, source_target_pairs={{0,255},{1,248},{2,249},{3,250},{4,251},{5,252},{6,253},{7,254},{8... | collective-permute-start | bytes 442376 | tf_op jit(solution)/shard_map/ppermute | solution.py:300
  8.5 8.5 %collective-permute-start.1 = (bf16[2,3,6,4,512]{4,3,2,1,0:T(4,128)(2,1)S(1)}, bf16[2,3,6,4,512]{4,3,2,1,0:T(4,128)(2,1)S(1)}, u32[]{:S(2)}, u32[]{:S(2)}) collective-permute-start(bf16[2,3,6,4,512]{4,3,2,1,0:T(4,128)(2,1)S(1)} %get-tuple-element.33), channel_id=1, source_target_pairs={{0,7},{1,0},{2,1},{3,2},{4,3},{5,4},{6,5},{7,6},{8,15},{9,8},{10,9... | collective-permute-start | bytes 442376 | tf_op jit(solution)/shard_map/ppermute | solution.py:300
  8.7 8.3 %collective-permute-start.2 = (bf16[2,3,6,4,512]{4,3,2,1,0:T(4,128)(2,1)S(1)}, bf16[2,3,6,4,512]{4,3,2,1,0:T(4,128)(2,1)S(1)}, u32[]{:S(2)}, u32[]{:S(2)}) collective-permute-start(bf16[2,3,6,4,512]{4,3,2,1,0:T(4,128)(2,1)S(1)} %get-tuple-element.34), channel_id=1, source_target_pairs={{0,248},{1,249},{2,250},{3,251},{4,252},{5,253},{6,254},{7,255},{8... | collective-permute-start | bytes 442376 | tf_op jit(solution)/shard_map/ppermute | solution.py:300
  21.3 5.3 %collective-permute-start.4 = (bf16[4,256,512]{2,1,0:T(8,128)(2,1)S(1)}, bf16[4,256,512]{2,1,0:T(8,128)(2,1)S(1)}, u32[]{:S(2)}, u32[]{:S(2)}) collective-permute-start(bf16[4,256,512]{2,1,0:T(8,128)(2,1)S(1)} %get-tuple-element.47), channel_id=1, source_target_pairs={{0,8},{8,0},{1,9},{9,1},{2,10},{10,2},{3,11},{11,3},{4,12},{12,4},... | collective-permute-start | bytes 3145736 | tf_op jit(solution)/shard_map/ppermute | solution.py:304
  27.9 22.9 %all-to-all-start = ((bf16[32,32,512]{2,1,0:T(8,128)(2,1)}), bf16[32,32,512]{2,1,0:T(8,128)(2,1)S(1)}, u32[]{:S(2)}, u32[]{:S(2)}) async-start(bf16[32,32,512]{2,1,0:T(8,128)(2,1)} %bitcast.4), calls=%async_computation | async-start | bytes 2097152 | tf_op jit(solution)/shard_map/all_to_all | solution.py:355
  32.2 14.9 %collective-permute-start.3 = (bf16[2,2,3,6,4,512]{5,4,3,2,1,0:T(4,128)(2,1)S(1)}, bf16[2,2,3,6,4,512]{5,4,3,2,1,0:T(4,128)(2,1)S(1)}, u32[]{:S(2)}, u32[]{:S(2)}) collective-permute-start(bf16[2,2,3,6,4,512]{5,4,3,2,1,0:T(4,128)(2,1)S(1)} %get-tuple-element.45), channel_id=1, source_target_pairs={{0,8},{1,9},{2,10},{3,11},{4,12},{5,13},{6,14},{7,15},{8,16},{9,17... | collective-permute-start | bytes 884744 | tf_op jit(solution)/shard_map/ppermute | solution.py:300
  51.0 11.6 %collective-permute-start.5 = (bf16[2,2,3,6,4,512]{5,4,3,2,1,0:T(4,128)(2,1)S(1)}, bf16[2,2,3,6,4,512]{5,4,3,2,1,0:T(4,128)(2,1)S(1)}, u32[]{:S(2)}, u32[]{:S(2)}) collective-permute-start(bf16[2,2,3,6,4,512]{5,4,3,2,1,0:T(4,128)(2,1)S(1)} %get-tuple-element.49), channel_id=1, source_target_pairs={{0,1},{1,2},{2,3},{3,4},{4,5},{5,6},{6,7},{7,0},{8,9},{9,10},{10,1... | collective-permute-start | bytes 884744 | tf_op jit(solution)/shard_map/ppermute | solution.py:300
  51.6 3.7 %collective-permute-start.6 = (bf16[32,512]{1,0:T(8,128)(2,1)S(1)}, bf16[32,512]{1,0:T(8,128)(2,1)S(1)}, u32[]{:S(2)}, u32[]{:S(2)}) collective-permute-start(bf16[32,512]{1,0:T(8,128)(2,1)S(1)} %get-tuple-element.52.own_ref), channel_id=1, source_target_pairs={{0,32},{32,0},{64,96},{96,64},{1,33},{33,1},{65,97},{97,65},{2,34}... | collective-permute-start | bytes 98312 | tf_op jit(solution)/shard_map/ppermute | solution.py:360
  55.3 32.3 %copy-start = (bf16[4,6,12,512]{3,0,2,1:T(4,128)(2,1)S(1)}, bf16[4,6,12,512]{3,0,2,1:T(4,128)(2,1)}, u32[]{:S(2)}) copy-start(bf16[4,6,12,512]{3,0,2,1:T(4,128)(2,1)} %param.6) | copy-start | bytes 884740
  55.3 32.2 %copy-start.1 = (bf16[4,6,12,512]{3,0,2,1:T(4,128)(2,1)S(1)}, bf16[4,6,12,512]{3,0,2,1:T(4,128)(2,1)}, u32[]{:S(2)}) copy-start(bf16[4,6,12,512]{3,0,2,1:T(4,128)(2,1)} %param.7) | copy-start | bytes 884740
  55.3 7.3 %collective-permute-start.7 = (bf16[32,512]{1,0:T(8,128)(2,1)S(1)}, bf16[32,512]{1,0:T(8,128)(2,1)S(1)}, u32[]{:S(2)}, u32[]{:S(2)}) collective-permute-start(bf16[32,512]{1,0:T(8,128)(2,1)S(1)} %shard_map.108.own_ref), channel_id=1, source_target_pairs={{0,64},{32,96},{64,0},{96,32},{1,65},{33,97},{65,1},{97,33},{2,66}... | collective-permute-start | bytes 98312 | tf_op jit(solution)/shard_map/ppermute | solution.py:362
  84.3 5.8 %collective-permute-start.8 = (bf16[4,256,512]{2,1,0:T(8,128)(2,1)S(1)}, bf16[4,256,512]{2,1,0:T(8,128)(2,1)S(1)}, u32[]{:S(2)}, u32[]{:S(2)}) collective-permute-start(bf16[4,256,512]{2,1,0:T(8,128)(2,1)S(1)} %bitcast.11), channel_id=1, source_target_pairs={{0,8},{8,0},{1,9},{9,1},{2,10},{10,2},{3,11},{11,3},{4,12},{12,4},... | collective-permute-start | bytes 3145736 | tf_op jit(solution)/shard_map/ppermute | solution.py:304
